TPU v7x, 512 devices: a whole 4x8x8 slice. The times are simulated.
512 devices in a mesh: dp: 16 (over y, core), seq: 32 (over z, x).
Axes of the slice: x: 4, y: 8, z: 8, core: 2. Of those that a mesh axis runs over, the one named last changes fastest.
Arguments:
- queries: bfloat16 [16, 4096, 1024], P('dp', 'seq'), may hold values from -80 to 80
- keys_in: bfloat16 [16, 4096, 1024], P('dp', 'seq'), may hold values from -4 to 4
- values_in: bfloat16 [16, 4096, 1024], P('dp', 'seq'), may hold values from -6 to 6
- cotangent: bfloat16 [16, 4096, 1024], P('dp', 'seq'), may hold values from -6 to 6
- level_slope: float32 [8], replicated, may hold values from -0.4 to 0.2
Outputs:
- grad_queries: bfloat16 [16, 4096, 1024], P('dp', 'seq')
- grad_keys: bfloat16 [16, 4096, 1024], P('dp', 'seq')
- grad_values: bfloat16 [16, 4096, 1024], P('dp', 'seq')
- grad_slope: float32 [8], replicated
All inputs are finite; a program needn't handle non-finite values.
Results may differ from a plain program's by a relative error of at most 0.007.
Values may be sent and summed in bfloat16 or wider, within the bound.
No kernel may reach another device: no remote copies, remote signals or barrier semaphores. Data moves between devices by JAX's collectives and lax.ppermute only.
A program may use at most 64 MiB of HBM per device.

v0:
```python
import math

import jax
import jax.numpy as jnp
from jax import lax
from jax.sharding import PartitionSpec as P

LEAF = 16


LOG_TWO = math.log(2.0)


def from_partner(block, axis, apart):
    count = lax.axis_size(axis)
    route = []
    for low in range(count):
        high = low | 1 << apart
        if high != low and high < count:
            route += [(low, high), (high, low)]
    return lax.ppermute(block, axis, route)


def pool_pairs(rows):
    count = rows.shape[0] // 2
    wide = rows.astype(jnp.float32).reshape(count, 2, rows.shape[1])
    return (0.5 * (wide[:, 0] + wide[:, 1])).astype(jnp.bfloat16)


def spread_pairs(grads):
    return jnp.repeat(0.5 * grads, 2, axis=0)


def pair_swap(blocks):
    groups = blocks.shape[0]
    rest = blocks.shape[1:]
    return blocks.reshape((groups // 2, 2) + rest)[:, ::-1].reshape((groups,) + rest)


def per_device(queries, keys_in, values_in, cotangent, level_slope):
    tokens = queries.shape[1]
    width = queries.shape[2]
    heads = level_slope.shape[0]
    head_dim = width // heads
    scale = 1.0 / math.sqrt(head_dim)
    leaf_len = LEAF
    local_count = (tokens // leaf_len).bit_length() - 1
    seq_count = lax.axis_size("seq")
    bit_count = seq_count.bit_length() - 1
    position = lax.axis_index("seq")
    query_loc = queries[0]
    key_loc = keys_in[0]
    val_loc = values_in[0]
    cot_loc = cotangent[0]
    coarse_keys = [key_loc]
    coarse_vals = [val_loc]
    for level_idx in range(1, local_count + 1):
        coarse_keys.append(pool_pairs(coarse_keys[-1]))
        coarse_vals.append(pool_pairs(coarse_vals[-1]))
    remote_keys = []
    remote_vals = []
    own_keys = coarse_keys[local_count]
    own_vals = coarse_vals[local_count]
    for bit_pos in range(bit_count):
        sib_keys, sib_vals = from_partner((own_keys, own_vals), "seq", bit_pos)
        remote_keys.append(sib_keys)
        remote_vals.append(sib_vals)
        if bit_pos + 1 < bit_count:
            lower = position // 2**bit_pos % 2 == 0
            joined_k = jnp.where(
                lower,
                jnp.concatenate([own_keys, sib_keys], 0),
                jnp.concatenate([sib_keys, own_keys], 0),
            )
            joined_v = jnp.where(
                lower,
                jnp.concatenate([own_vals, sib_vals], 0),
                jnp.concatenate([sib_vals, own_vals], 0),
            )
            own_keys = pool_pairs(joined_k)
            own_vals = pool_pairs(joined_v)
    setups = []
    for level_idx in range(local_count):
        if level_idx == 0:
            groups = tokens // (2 * leaf_len)
            key_blk = key_loc.reshape(groups, 2 * leaf_len, heads, head_dim)
            val_blk = val_loc.reshape(groups, 2 * leaf_len, heads, head_dim)
        else:
            groups = tokens // (leaf_len * 2**level_idx)
            key_blk = pair_swap(coarse_keys[level_idx].reshape(groups, leaf_len, heads, head_dim))
            val_blk = pair_swap(coarse_vals[level_idx].reshape(groups, leaf_len, heads, head_dim))
        setups.append((groups, key_blk, val_blk, level_idx))
    for bit_pos in range(bit_count):
        setups.append(
            (
                1,
                remote_keys[bit_pos].reshape(1, leaf_len, heads, head_dim),
                remote_vals[bit_pos].reshape(1, leaf_len, heads, head_dim),
                local_count + bit_pos,
            )
        )
    query_h = query_loc.reshape(tokens, heads, head_dim)
    cot_h = cot_loc.reshape(tokens, heads, head_dim)
    score_list = []
    for groups, key_blk, val_blk, level_idx in setups:
        query_g = query_h.reshape(groups, tokens // groups, heads, head_dim)
        raw = jnp.einsum("gqhd,gkhd->gqhk", query_g, key_blk, preferred_element_type=jnp.float32)
        score_list.append(
            raw.reshape(tokens, heads, key_blk.shape[1]) * scale
            + (level_idx * (LOG_TWO + level_slope))[:, None]
        )
    scores = jnp.concatenate(score_list, axis=-1)
    top = jnp.max(scores, axis=-1, keepdims=True)
    expo = jnp.exp(scores - top)
    probs = expo / jnp.sum(expo, axis=-1, keepdims=True)
    probs_b = probs.astype(jnp.bfloat16)
    sizes = [setup[1].shape[1] for setup in setups]
    offsets = [sum(sizes[:index]) for index in range(len(sizes))]
    attended = jnp.zeros((tokens, heads, head_dim), jnp.float32)
    dprob_list = []
    for (groups, key_blk, val_blk, level_idx), start in zip(setups, offsets):
        width_k = key_blk.shape[1]
        part = probs_b[:, :, start : start + width_k].reshape(
            groups, tokens // groups, heads, width_k
        )
        attended = attended + jnp.einsum(
            "gqhk,gkhd->gqhd", part, val_blk, preferred_element_type=jnp.float32
        ).reshape(tokens, heads, head_dim)
        cot_g = cot_h.reshape(groups, tokens // groups, heads, head_dim)
        dprob_list.append(
            jnp.einsum(
                "gqhd,gkhd->gqhk", cot_g, val_blk, preferred_element_type=jnp.float32
            ).reshape(tokens, heads, width_k)
        )
    delta = jnp.sum(cot_h.astype(jnp.float32) * attended, axis=-1, keepdims=True)
    dscores = probs * (jnp.concatenate(dprob_list, axis=-1) - delta)
    dscores_b = dscores.astype(jnp.bfloat16)
    slope_part = jnp.zeros((heads,), jnp.float32)
    grad_query = jnp.zeros((tokens, heads, head_dim), jnp.float32)
    key_grads = []
    val_grads = []
    far_keys = []
    far_vals = []
    for (groups, key_blk, val_blk, level_idx), start in zip(setups, offsets):
        width_k = key_blk.shape[1]
        slope_part = slope_part + level_idx * jnp.sum(
            dscores[:, :, start : start + width_k], axis=(0, 2)
        )
        ds_g = dscores_b[:, :, start : start + width_k].reshape(
            groups, tokens // groups, heads, width_k
        )
        pb_g = probs_b[:, :, start : start + width_k].reshape(
            groups, tokens // groups, heads, width_k
        )
        query_g = query_h.reshape(groups, tokens // groups, heads, head_dim)
        cot_g = cot_h.reshape(groups, tokens // groups, heads, head_dim)
        grad_query = (
            grad_query
            + jnp.einsum(
                "gqhk,gkhd->gqhd", ds_g, key_blk, preferred_element_type=jnp.float32
            ).reshape(tokens, heads, head_dim)
            * scale
        )
        dkey = (
            jnp.einsum("gqhk,gqhd->gkhd", ds_g, query_g, preferred_element_type=jnp.float32) * scale
        )
        dval = jnp.einsum("gqhk,gqhd->gkhd", pb_g, cot_g, preferred_element_type=jnp.float32)
        if level_idx >= local_count:
            far_keys.append(dkey.reshape(leaf_len, width))
            far_vals.append(dval.reshape(leaf_len, width))
        else:
            if level_idx > 0:
                dkey = pair_swap(dkey)
                dval = pair_swap(dval)
            key_grads.append(dkey.reshape(-1, width))
            val_grads.append(dval.reshape(-1, width))
    own_gk = jnp.zeros((leaf_len, width), jnp.float32)
    own_gv = jnp.zeros((leaf_len, width), jnp.float32)
    for bit_pos in range(bit_count - 1, -1, -1):
        lower = position // 2**bit_pos % 2 == 0
        cat_k = spread_pairs(own_gk)
        cat_v = spread_pairs(own_gv)
        mine_k = jnp.where(lower, cat_k[:leaf_len], cat_k[leaf_len:])
        mine_v = jnp.where(lower, cat_v[:leaf_len], cat_v[leaf_len:])
        other_k = jnp.where(lower, cat_k[leaf_len:], cat_k[:leaf_len])
        other_v = jnp.where(lower, cat_v[leaf_len:], cat_v[:leaf_len])
        back_k, back_v = from_partner(
            (far_keys[bit_pos] + other_k, far_vals[bit_pos] + other_v), "seq", bit_pos
        )
        own_gk = mine_k + back_k
        own_gv = mine_v + back_v
    key_grads.append(own_gk)
    val_grads.append(own_gv)
    for level_idx in range(local_count, 0, -1):
        key_grads[level_idx - 1] = key_grads[level_idx - 1] + spread_pairs(key_grads[level_idx])
        val_grads[level_idx - 1] = val_grads[level_idx - 1] + spread_pairs(val_grads[level_idx])
    grad_slope = lax.psum(slope_part, ("dp", "seq"))
    grad_q = grad_query.reshape(1, tokens, width).astype(jnp.bfloat16)
    grad_k = key_grads[0].reshape(1, tokens, width).astype(jnp.bfloat16)
    grad_v = val_grads[0].reshape(1, tokens, width).astype(jnp.bfloat16)
    return (grad_q, grad_k, grad_v, grad_slope)


def solution(mesh):
    return jax.shard_map(
        per_device,
        mesh=mesh,
        in_specs=(
            P("dp", "seq", None),
            P("dp", "seq", None),
            P("dp", "seq", None),
            P("dp", "seq", None),
            P(),
        ),
        out_specs=(P("dp", "seq", None), P("dp", "seq", None), P("dp", "seq", None), P()),
        check_vma=False,
    )
```

profile of v0, /device:TPU:6, one launch (start us, length us, event | category | flops | bytes accessed | tf_op | source)
XLA Modules:
  0.0 266.0 jit_solution(14093829960222500224)
XLA Ops:
  0.6 1.3 reshape.985
  3.7 2.7 %collective-permute-start = (bf16[16,1024]{1,0:T(8,128)(2,1)S(1)}, bf16[16,1024]{1,0:T(8,128)(2,1)S(1)}, u32[]{:S(2)}, u32[]{:S(2)}) collective-permute-start(bf16[16,1024]{1,0:T(8,128)(2,1)S(1)} %bitcast.658), channel_id=1, source_target_pairs={{0,1},{1,0},{2,3},{3,2},{4,5},{5,4},{6,7},{7,6},{8,9},{9,8},{10,11... | collective-permute-start | bytes 98312 | tf_op jit(solution)/shard_map/ppermute | solution.py:21
  8.2 3.1 %collective-permute-start.5 = (bf16[16,1024]{1,0:T(8,128)(2,1)S(1)}, bf16[16,1024]{1,0:T(8,128)(2,1)S(1)}, u32[]{:S(2)}, u32[]{:S(2)}) collective-permute-start(bf16[16,1024]{1,0:T(8,128)(2,1)S(1)} %bitcast.660), channel_id=1, source_target_pairs={{0,1},{1,0},{2,3},{3,2},{4,5},{5,4},{6,7},{7,6},{8,9},{9,8},{10,11... | collective-permute-start | bytes 98312 | tf_op jit(solution)/shard_map/ppermute | solution.py:21
  19.6 7.2 %collective-permute-start.1 = (bf16[16,1024]{1,0:T(8,128)(2,1)S(1)}, bf16[16,1024]{1,0:T(8,128)(2,1)S(1)}, u32[]{:S(2)}, u32[]{:S(2)}) collective-permute-start(bf16[16,1024]{1,0:T(8,128)(2,1)S(1)} %bitcast.672), channel_id=1, source_target_pairs={{0,2},{2,0},{1,3},{3,1},{4,6},{6,4},{5,7},{7,5},{8,10},{10,8},{9,1... | collective-permute-start | bytes 98312 | tf_op jit(solution)/shard_map/ppermute | solution.py:21
  27.0 1.9 collective-permute-start.6
  29.6 2.5 collective-permute-start.2
  32.1 2.2 collective-permute-done.6
  34.6 1.9 collective-permute-start.7
  37.2 4.6 %collective-permute-start.3 = (bf16[16,1024]{1,0:T(8,128)(2,1)S(1)}, bf16[16,1024]{1,0:T(8,128)(2,1)S(1)}, u32[]{:S(2)}, u32[]{:S(2)}) collective-permute-start(bf16[16,1024]{1,0:T(8,128)(2,1)S(1)} %bitcast.668), channel_id=1, source_target_pairs={{0,8},{8,0},{1,9},{9,1},{2,10},{10,2},{3,11},{11,3},{4,12},{12,4},... | collective-permute-start | bytes 98312 | tf_op jit(solution)/shard_map/ppermute | solution.py:21
  42.0 2.8 %collective-permute-start.8 = (bf16[16,1024]{1,0:T(8,128)(2,1)S(1)}, bf16[16,1024]{1,0:T(8,128)(2,1)S(1)}, u32[]{:S(2)}, u32[]{:S(2)}) collective-permute-start(bf16[16,1024]{1,0:T(8,128)(2,1)S(1)} %bitcast.670), channel_id=1, source_target_pairs={{0,8},{8,0},{1,9},{9,1},{2,10},{10,2},{3,11},{11,3},{4,12},{12,4},... | collective-permute-start | bytes 98312 | tf_op jit(solution)/shard_map/ppermute | solution.py:21
  45.5 8.0 %collective-permute-start.4 = (bf16[16,1024]{1,0:T(8,128)(2,1)S(1)}, bf16[16,1024]{1,0:T(8,128)(2,1)S(1)}, u32[]{:S(2)}, u32[]{:S(2)}) collective-permute-start(bf16[16,1024]{1,0:T(8,128)(2,1)S(1)} %bitcast.675), channel_id=1, source_target_pairs={{0,16},{16,0},{1,17},{17,1},{2,18},{18,2},{3,19},{19,3},{4,20},{20... | collective-permute-start | bytes 98312 | tf_op jit(solution)/shard_map/ppermute | solution.py:21
  54.3 3.6 %collective-permute-start.9 = (bf16[16,1024]{1,0:T(8,128)(2,1)}, bf16[16,1024]{1,0:T(8,128)(2,1)}, u32[]{:S(2)}, u32[]{:S(2)}) collective-permute-start(bf16[16,1024]{1,0:T(8,128)(2,1)} %bitcast.569), channel_id=1, source_target_pairs={{0,16},{16,0},{1,17},{17,1},{2,18},{18,2},{3,19},{19,3},{4,20},{20... | collective-permute-start | bytes 98312 | tf_op jit(solution)/shard_map/ppermute | solution.py:21
  68.6 1.9 convolution_bitcast_fusion.2
  70.5 1.8 convolution_bitcast_fusion.3
  72.3 1.6 convolution_bitcast_fusion.14
  77.8 1.6 fusion.18
  79.4 1.6 fusion.12
  91.9 6.3 %collective-permute-start.15 = (f32[16,1024]{1,0:T(8,128)}, f32[16,1024]{1,0:T(8,128)}, u32[]{:S(2)}, u32[]{:S(2)}) collective-permute-start(f32[16,1024]{1,0:T(8,128)} %bitcast.567), channel_id=1, source_target_pairs={{0,16},{16,0},{1,17},{17,1},{2,18},{18,2},{3,19},{19,3},{4,20},{20... | collective-permute-start | bytes 196616 | tf_op jit(solution)/shard_map/ppermute | solution.py:21
  101.0 96.5 %psum.7 = f32[8]{0:T(128)} all-reduce(f32[8]{0:T(128)S(1)} %multiply_add_fusion), channel_id=1, replica_groups=mesh['dp'=16,'seq'=32] {'dp','seq'}, use_global_device_ids=true, to_apply=%region_18.19 | all-reduce | flops 8 | bytes 64 | tf_op jit(solution)/shard_map/psum | solution.py:197
  201.6 4.7 %collective-permute-start.10 = (f32[16,1024]{1,0:T(8,128)}, f32[16,1024]{1,0:T(8,128)}, u32[]{:S(2)}, u32[]{:S(2)}) collective-permute-start(f32[16,1024]{1,0:T(8,128)} %bitcast.568), channel_id=1, source_target_pairs={{0,16},{16,0},{1,17},{17,1},{2,18},{18,2},{3,19},{19,3},{4,20},{20... | collective-permute-start | bytes 196616 | tf_op jit(solution)/shard_map/ppermute | solution.py:21
  215.7 2.0 copy.725
  217.7 2.1 add_convert_fusion.2
  223.9 3.0 %collective-permute-start.16 = (f32[16,1024]{1,0:T(8,128)S(1)}, f32[16,1024]{1,0:T(8,128)S(1)}, u32[]{:S(2)}, u32[]{:S(2)}) collective-permute-start(f32[16,1024]{1,0:T(8,128)S(1)} %bitcast_add_fusion.7), channel_id=1, source_target_pairs={{0,8},{8,0},{1,9},{9,1},{2,10},{10,2},{3,11},{11,3},{4,12},{12,4},... | collective-permute-start | bytes 196616 | tf_op jit(solution)/shard_map/ppermute | solution.py:21
  228.8 3.8 %collective-permute-start.11 = (f32[16,1024]{1,0:T(8,128)S(1)}, f32[16,1024]{1,0:T(8,128)S(1)}, u32[]{:S(2)}, u32[]{:S(2)}) collective-permute-start(f32[16,1024]{1,0:T(8,128)S(1)} %bitcast_add_fusion.11), channel_id=1, source_target_pairs={{0,8},{8,0},{1,9},{9,1},{2,10},{10,2},{3,11},{11,3},{4,12},{12,4},... | collective-permute-start | bytes 196616 | tf_op jit(solution)/shard_map/ppermute | solution.py:21
  233.6 2.7 %collective-permute-start.17 = (f32[16,1024]{1,0:T(8,128)S(1)}, f32[16,1024]{1,0:T(8,128)S(1)}, u32[]{:S(2)}, u32[]{:S(2)}) collective-permute-start(f32[16,1024]{1,0:T(8,128)S(1)} %bitcast_add_fusion.6), channel_id=1, source_target_pairs={{0,4},{4,0},{1,5},{5,1},{2,6},{6,2},{3,7},{7,3},{8,12},{12,8},{9,1... | collective-permute-start | bytes 196616 | tf_op jit(solution)/shard_map/ppermute | solution.py:21
  237.7 3.1 %collective-permute-start.12 = (f32[16,1024]{1,0:T(8,128)S(1)}, f32[16,1024]{1,0:T(8,128)S(1)}, u32[]{:S(2)}, u32[]{:S(2)}) collective-permute-start(f32[16,1024]{1,0:T(8,128)S(1)} %bitcast_add_fusion.10), channel_id=1, source_target_pairs={{0,4},{4,0},{1,5},{5,1},{2,6},{6,2},{3,7},{7,3},{8,12},{12,8},{9,1... | collective-permute-start | bytes 196616 | tf_op jit(solution)/shard_map/ppermute | solution.py:21
  241.7 4.6 %collective-permute-start.18 = (f32[16,1024]{1,0:T(8,128)S(1)}, f32[16,1024]{1,0:T(8,128)S(1)}, u32[]{:S(2)}, u32[]{:S(2)}) collective-permute-start(f32[16,1024]{1,0:T(8,128)S(1)} %bitcast_add_fusion.5), channel_id=1, source_target_pairs={{0,2},{2,0},{1,3},{3,1},{4,6},{6,4},{5,7},{7,5},{8,10},{10,8},{9,1... | collective-permute-start | bytes 196616 | tf_op jit(solution)/shard_map/ppermute | solution.py:21
  247.4 2.8 %collective-permute-start.13 = (f32[16,1024]{1,0:T(8,128)S(1)}, f32[16,1024]{1,0:T(8,128)S(1)}, u32[]{:S(2)}, u32[]{:S(2)}) collective-permute-start(f32[16,1024]{1,0:T(8,128)S(1)} %bitcast_add_fusion.9), channel_id=1, source_target_pairs={{0,2},{2,0},{1,3},{3,1},{4,6},{6,4},{5,7},{7,5},{8,10},{10,8},{9,1... | collective-permute-start | bytes 196616 | tf_op jit(solution)/shard_map/ppermute | solution.py:21
  250.3 1.9 collective-permute-start.19
  252.3 3.1 %collective-permute-done.13 = f32[16,1024]{1,0:T(8,128)S(1)} collective-permute-done((f32[16,1024]{1,0:T(8,128)S(1)}, f32[16,1024]{1,0:T(8,128)S(1)}, u32[]{:S(2)}, u32[]{:S(2)}) %collective-permute-start.13) | collective-permute-done | bytes 65568 | tf_op jit(solution)/shard_map/ppermute | solution.py:21
  256.5 2.0 collective-permute-start.14
  261.2 1.5 collective-permute-done.14
  (394 shorter events, 73.0 us)
Async XLA Ops:
  3.7 15.7 %collective-permute-start = (bf16[16,1024]{1,0:T(8,128)(2,1)S(1)}, bf16[16,1024]{1,0:T(8,128)(2,1)S(1)}, u32[]{:S(2)}, u32[]{:S(2)}) collective-permute-start(bf16[16,1024]{1,0:T(8,128)(2,1)S(1)} %bitcast.658), channel_id=1, source_target_pairs={{0,1},{1,0},{2,3},{3,2},{4,5},{5,4},{6,7},{7,6},{8,9},{9,8},{10,11... | collective-permute-start | bytes 98312 | tf_op jit(solution)/shard_map/ppermute | solution.py:21
  7.9 3.4 %copy-start.45 = (bf16[1,128,1024]{2,1,0:T(8,128)(2,1)S(1)}, bf16[1,128,1024]{2,1,0:T(8,128)(2,1)}, u32[]{:S(2)}) copy-start(bf16[1,128,1024]{2,1,0:T(8,128)(2,1)} %param.5) | copy-start | bytes 786436
  8.2 11.2 %collective-permute-start.5 = (bf16[16,1024]{1,0:T(8,128)(2,1)S(1)}, bf16[16,1024]{1,0:T(8,128)(2,1)S(1)}, u32[]{:S(2)}, u32[]{:S(2)}) collective-permute-start(bf16[16,1024]{1,0:T(8,128)(2,1)S(1)} %bitcast.660), channel_id=1, source_target_pairs={{0,1},{1,0},{2,3},{3,2},{4,5},{5,4},{6,7},{7,6},{8,9},{9,8},{10,11... | collective-permute-start | bytes 98312 | tf_op jit(solution)/shard_map/ppermute | solution.py:21
  19.3 9.6 %copy-start.24 = (bf16[16,1024]{1,0:T(8,128)(2,1)}, bf16[16,1024]{1,0:T(8,128)(2,1)S(1)}, u32[]{:S(2)}) copy-start(bf16[16,1024]{1,0:T(8,128)(2,1)S(1)} %collective-permute-done) | copy-start | bytes 98308
  19.4 9.9 %copy-start.22 = (bf16[16,1024]{1,0:T(8,128)(2,1)}, bf16[16,1024]{1,0:T(8,128)(2,1)S(1)}, u32[]{:S(2)}) copy-start(bf16[16,1024]{1,0:T(8,128)(2,1)S(1)} %collective-permute-done.5) | copy-start | bytes 98308
  19.6 9.8 %collective-permute-start.1 = (bf16[16,1024]{1,0:T(8,128)(2,1)S(1)}, bf16[16,1024]{1,0:T(8,128)(2,1)S(1)}, u32[]{:S(2)}, u32[]{:S(2)}) collective-permute-start(bf16[16,1024]{1,0:T(8,128)(2,1)S(1)} %bitcast.672), channel_id=1, source_target_pairs={{0,2},{2,0},{1,3},{3,1},{4,6},{6,4},{5,7},{7,5},{8,10},{10,8},{9,1... | collective-permute-start | bytes 98312 | tf_op jit(solution)/shard_map/ppermute | solution.py:21
  27.0 7.3 %collective-permute-start.6 = (bf16[16,1024]{1,0:T(8,128)(2,1)S(1)}, bf16[16,1024]{1,0:T(8,128)(2,1)S(1)}, u32[]{:S(2)}, u32[]{:S(2)}) collective-permute-start(bf16[16,1024]{1,0:T(8,128)(2,1)S(1)} %bitcast.662), channel_id=1, source_target_pairs={{0,2},{2,0},{1,3},{3,1},{4,6},{6,4},{5,7},{7,5},{8,10},{10,8},{9,1... | collective-permute-start | bytes 98312 | tf_op jit(solution)/shard_map/ppermute | solution.py:21
  29.4 7.1 %copy-start.26 = (bf16[16,1024]{1,0:T(8,128)(2,1)}, bf16[16,1024]{1,0:T(8,128)(2,1)S(1)}, u32[]{:S(2)}) copy-start(bf16[16,1024]{1,0:T(8,128)(2,1)S(1)} %collective-permute-done.1) | copy-start | bytes 98308
  29.6 7.3 %collective-permute-start.2 = (bf16[16,1024]{1,0:T(8,128)(2,1)S(1)}, bf16[16,1024]{1,0:T(8,128)(2,1)S(1)}, u32[]{:S(2)}, u32[]{:S(2)}) collective-permute-start(bf16[16,1024]{1,0:T(8,128)(2,1)S(1)} %bitcast.664), channel_id=1, source_target_pairs={{0,4},{4,0},{1,5},{5,1},{2,6},{6,2},{3,7},{7,3},{8,12},{12,8},{9,1... | collective-permute-start | bytes 98312 | tf_op jit(solution)/shard_map/ppermute | solution.py:21
  34.6 7.2 %collective-permute-start.7 = (bf16[16,1024]{1,0:T(8,128)(2,1)S(1)}, bf16[16,1024]{1,0:T(8,128)(2,1)S(1)}, u32[]{:S(2)}, u32[]{:S(2)}) collective-permute-start(bf16[16,1024]{1,0:T(8,128)(2,1)S(1)} %bitcast.666), channel_id=1, source_target_pairs={{0,4},{4,0},{1,5},{5,1},{2,6},{6,2},{3,7},{7,3},{8,12},{12,8},{9,1... | collective-permute-start | bytes 98312 | tf_op jit(solution)/shard_map/ppermute | solution.py:21
  36.9 7.8 %copy-start.28 = (bf16[16,1024]{1,0:T(8,128)(2,1)}, bf16[16,1024]{1,0:T(8,128)(2,1)S(1)}, u32[]{:S(2)}) copy-start(bf16[16,1024]{1,0:T(8,128)(2,1)S(1)} %collective-permute-done.2) | copy-start | bytes 98308
  37.2 8.1 %collective-permute-start.3 = (bf16[16,1024]{1,0:T(8,128)(2,1)S(1)}, bf16[16,1024]{1,0:T(8,128)(2,1)S(1)}, u32[]{:S(2)}, u32[]{:S(2)}) collective-permute-start(bf16[16,1024]{1,0:T(8,128)(2,1)S(1)} %bitcast.668), channel_id=1, source_target_pairs={{0,8},{8,0},{1,9},{9,1},{2,10},{10,2},{3,11},{11,3},{4,12},{12,4},... | collective-permute-start | bytes 98312 | tf_op jit(solution)/shard_map/ppermute | solution.py:21
  41.8 3.3 %copy-start.34 = (bf16[16,1024]{1,0:T(8,128)(2,1)}, bf16[16,1024]{1,0:T(8,128)(2,1)S(1)}, u32[]{:S(2)}) copy-start(bf16[16,1024]{1,0:T(8,128)(2,1)S(1)} %collective-permute-done.7) | copy-start | bytes 98308
  42.0 11.5 %collective-permute-start.8 = (bf16[16,1024]{1,0:T(8,128)(2,1)S(1)}, bf16[16,1024]{1,0:T(8,128)(2,1)S(1)}, u32[]{:S(2)}, u32[]{:S(2)}) collective-permute-start(bf16[16,1024]{1,0:T(8,128)(2,1)S(1)} %bitcast.670), channel_id=1, source_target_pairs={{0,8},{8,0},{1,9},{9,1},{2,10},{10,2},{3,11},{11,3},{4,12},{12,4},... | collective-permute-start | bytes 98312 | tf_op jit(solution)/shard_map/ppermute | solution.py:21
  45.2 12.7 %copy-start.30 = (bf16[16,1024]{1,0:T(8,128)(2,1)}, bf16[16,1024]{1,0:T(8,128)(2,1)S(1)}, u32[]{:S(2)}) copy-start(bf16[16,1024]{1,0:T(8,128)(2,1)S(1)} %collective-permute-done.3) | copy-start | bytes 98308
  45.5 12.9 %collective-permute-start.4 = (bf16[16,1024]{1,0:T(8,128)(2,1)S(1)}, bf16[16,1024]{1,0:T(8,128)(2,1)S(1)}, u32[]{:S(2)}, u32[]{:S(2)}) collective-permute-start(bf16[16,1024]{1,0:T(8,128)(2,1)S(1)} %bitcast.675), channel_id=1, source_target_pairs={{0,16},{16,0},{1,17},{17,1},{2,18},{18,2},{3,19},{19,3},{4,20},{20... | collective-permute-start | bytes 98312 | tf_op jit(solution)/shard_map/ppermute | solution.py:21
  53.5 4.7 %copy-start.36 = (bf16[16,1024]{1,0:T(8,128)(2,1)}, bf16[16,1024]{1,0:T(8,128)(2,1)S(1)}, u32[]{:S(2)}) copy-start(bf16[16,1024]{1,0:T(8,128)(2,1)S(1)} %collective-permute-done.8) | copy-start | bytes 98308
  54.3 22.3 %collective-permute-start.9 = (bf16[16,1024]{1,0:T(8,128)(2,1)}, bf16[16,1024]{1,0:T(8,128)(2,1)}, u32[]{:S(2)}, u32[]{:S(2)}) collective-permute-start(bf16[16,1024]{1,0:T(8,128)(2,1)} %bitcast.569), channel_id=1, source_target_pairs={{0,16},{16,0},{1,17},{17,1},{2,18},{18,2},{3,19},{19,3},{4,20},{20... | collective-permute-start | bytes 98312 | tf_op jit(solution)/shard_map/ppermute | solution.py:21
  59.3 3.5 %copy-start.4 = (bf16[128,8,144]{0,2,1:T(8,128)(2,1)}, bf16[128,8,144]{0,2,1:T(8,128)(2,1)S(1)}, u32[]{:S(2)}) copy-start(bf16[128,8,144]{0,2,1:T(8,128)(2,1)S(1)} %fusion.62) | copy-start | bytes 884740
  75.6 3.8 %copy-start.3 = (f32[128,8,128]{0,2,1:T(8,128)S(1)}, f32[128,8,128]{0,2,1:T(8,128)}, u32[]{:S(2)}) copy-start(f32[128,8,128]{0,2,1:T(8,128)} %convolution_bitcast_fusion.3) | copy-start | bytes 1572868
  91.2 7.0 %copy-start.21 = (f32[2,16,8,128]{3,1,2,0:T(8,128)S(1)}, f32[2,16,8,128]{3,1,2,0:T(8,128)}, u32[]{:S(2)}) copy-start(f32[2,16,8,128]{3,1,2,0:T(8,128)} %convolution_bitcast_fusion.11) | copy-start | bytes 393220
  91.9 130.3 %collective-permute-start.15 = (f32[16,1024]{1,0:T(8,128)}, f32[16,1024]{1,0:T(8,128)}, u32[]{:S(2)}, u32[]{:S(2)}) collective-permute-start(f32[16,1024]{1,0:T(8,128)} %bitcast.567), channel_id=1, source_target_pairs={{0,16},{16,0},{1,17},{17,1},{2,18},{18,2},{3,19},{19,3},{4,20},{20... | collective-permute-start | bytes 196616 | tf_op jit(solution)/shard_map/ppermute | solution.py:21
  100.3 97.2 %copy-start.55 = (f32[1,16,8,128]{3,1,2,0:T(8,128)S(1)}, f32[1,16,8,128]{3,1,2,0:T(8,128)}, u32[]{:S(2)}) copy-start(f32[1,16,8,128]{3,1,2,0:T(8,128)} %fusion.14) | copy-start | bytes 196612
  201.6 25.4 %collective-permute-start.10 = (f32[16,1024]{1,0:T(8,128)}, f32[16,1024]{1,0:T(8,128)}, u32[]{:S(2)}, u32[]{:S(2)}) collective-permute-start(f32[16,1024]{1,0:T(8,128)} %bitcast.568), channel_id=1, source_target_pairs={{0,16},{16,0},{1,17},{17,1},{2,18},{18,2},{3,19},{19,3},{4,20},{20... | collective-permute-start | bytes 196616 | tf_op jit(solution)/shard_map/ppermute | solution.py:21
  223.9 8.7 %collective-permute-start.16 = (f32[16,1024]{1,0:T(8,128)S(1)}, f32[16,1024]{1,0:T(8,128)S(1)}, u32[]{:S(2)}, u32[]{:S(2)}) collective-permute-start(f32[16,1024]{1,0:T(8,128)S(1)} %bitcast_add_fusion.7), channel_id=1, source_target_pairs={{0,8},{8,0},{1,9},{9,1},{2,10},{10,2},{3,11},{11,3},{4,12},{12,4},... | collective-permute-start | bytes 196616 | tf_op jit(solution)/shard_map/ppermute | solution.py:21
  228.8 7.8 %collective-permute-start.11 = (f32[16,1024]{1,0:T(8,128)S(1)}, f32[16,1024]{1,0:T(8,128)S(1)}, u32[]{:S(2)}, u32[]{:S(2)}) collective-permute-start(f32[16,1024]{1,0:T(8,128)S(1)} %bitcast_add_fusion.11), channel_id=1, source_target_pairs={{0,8},{8,0},{1,9},{9,1},{2,10},{10,2},{3,11},{11,3},{4,12},{12,4},... | collective-permute-start | bytes 196616 | tf_op jit(solution)/shard_map/ppermute | solution.py:21
  233.6 7.2 %collective-permute-start.17 = (f32[16,1024]{1,0:T(8,128)S(1)}, f32[16,1024]{1,0:T(8,128)S(1)}, u32[]{:S(2)}, u32[]{:S(2)}) collective-permute-start(f32[16,1024]{1,0:T(8,128)S(1)} %bitcast_add_fusion.6), channel_id=1, source_target_pairs={{0,4},{4,0},{1,5},{5,1},{2,6},{6,2},{3,7},{7,3},{8,12},{12,8},{9,1... | collective-permute-start | bytes 196616 | tf_op jit(solution)/shard_map/ppermute | solution.py:21
  237.7 8.6 %collective-permute-start.12 = (f32[16,1024]{1,0:T(8,128)S(1)}, f32[16,1024]{1,0:T(8,128)S(1)}, u32[]{:S(2)}, u32[]{:S(2)}) collective-permute-start(f32[16,1024]{1,0:T(8,128)S(1)} %bitcast_add_fusion.10), channel_id=1, source_target_pairs={{0,4},{4,0},{1,5},{5,1},{2,6},{6,2},{3,7},{7,3},{8,12},{12,8},{9,1... | collective-permute-start | bytes 196616 | tf_op jit(solution)/shard_map/ppermute | solution.py:21
  241.7 8.5 %collective-permute-start.18 = (f32[16,1024]{1,0:T(8,128)S(1)}, f32[16,1024]{1,0:T(8,128)S(1)}, u32[]{:S(2)}, u32[]{:S(2)}) collective-permute-start(f32[16,1024]{1,0:T(8,128)S(1)} %bitcast_add_fusion.5), channel_id=1, source_target_pairs={{0,2},{2,0},{1,3},{3,1},{4,6},{6,4},{5,7},{7,5},{8,10},{10,8},{9,1... | collective-permute-start | bytes 196616 | tf_op jit(solution)/shard_map/ppermute | solution.py:21
  247.4 8.0 %collective-permute-start.13 = (f32[16,1024]{1,0:T(8,128)S(1)}, f32[16,1024]{1,0:T(8,128)S(1)}, u32[]{:S(2)}, u32[]{:S(2)}) collective-permute-start(f32[16,1024]{1,0:T(8,128)S(1)} %bitcast_add_fusion.9), channel_id=1, source_target_pairs={{0,2},{2,0},{1,3},{3,1},{4,6},{6,4},{5,7},{7,5},{8,10},{10,8},{9,1... | collective-permute-start | bytes 196616 | tf_op jit(solution)/shard_map/ppermute | solution.py:21
  250.3 8.2 %collective-permute-start.19 = (f32[16,1024]{1,0:T(8,128)S(1)}, f32[16,1024]{1,0:T(8,128)S(1)}, u32[]{:S(2)}, u32[]{:S(2)}) collective-permute-start(f32[16,1024]{1,0:T(8,128)S(1)} %bitcast_add_fusion.4), channel_id=1, source_target_pairs={{0,1},{1,0},{2,3},{3,2},{4,5},{5,4},{6,7},{7,6},{8,9},{9,8},{10,11... | collective-permute-start | bytes 196616 | tf_op jit(solution)/shard_map/ppermute | solution.py:21
  256.5 6.2 %collective-permute-start.14 = (f32[16,1024]{1,0:T(8,128)S(1)}, f32[16,1024]{1,0:T(8,128)S(1)}, u32[]{:S(2)}, u32[]{:S(2)}) collective-permute-start(f32[16,1024]{1,0:T(8,128)S(1)} %bitcast_add_fusion.8), channel_id=1, source_target_pairs={{0,1},{1,0},{2,3},{3,2},{4,5},{5,4},{6,7},{7,6},{8,9},{9,8},{10,11... | collective-permute-start | bytes 196616 | tf_op jit(solution)/shard_map/ppermute | solution.py:21
  (48 other events, 53.6 us)
where the time goes:
time: 269 us; the launch traced here: 266 us
  blocking collectives  96.5 us (36%)
  starting transfers between devices  73.1 us (27%)
  local copies, waits for them, and re-layouts  46.3 us (17%)
  matrix products  31 us (12%)
  other arithmetic  9.27 us (3%)
  waiting for transfers between devices  7.12 us (3%)
  between operations  2.77 us (1%)
    psum x1, blocking collectives, per_device(): grad_slope = lax.psum(slope_part, ('dp', 'seq'))  96.5 us
    ppermute x20, starting transfers between devices, from_partner(): return lax.ppermute(block, axis, route)  73.1 us
    unnamed x144, local copies, waits for them, and re-layouts  20.3 us
    dot_general x8, matrix products, per_device(): jnp.einsum('gqhk,gkhd->gqhd', part, val_blk, preferred_element_type=jnp.f...  8.31 us
    ppermute x20, waiting for transfers between devices, from_partner(): return lax.ppermute(block, axis, route)  7.12 us
    dot_general x8, matrix products, per_device(): jnp.einsum('gqhk,gqhd->gkhd', pb_g, cot_g, preferred_element_type=jnp.flo...  7.08 us
    dot_general x8, matrix products, per_device(): jnp.einsum('gqhk,gqhd->gkhd', ds_g, query_g, preferred_element_type=jnp.f...  6.81 us
  transfers between devices with their start and end apart: 20, of which 4 were waited for; matrix products, arithmetic and copies ran while one was open for 18% of the time, Pallas kernels for 0%

commit v1 on v0

v1 whole, which is shorter than its diff:
```python
import math

import jax
import jax.numpy as jnp
from jax import lax
from jax.experimental import pallas as pl
from jax.experimental.pallas import tpu as pltpu
from jax.sharding import PartitionSpec as P

LOG_TWO = math.log(2.0)
HEADS = 8
HEAD_DIM = 128
WIDTH = HEADS * HEAD_DIM
TOKENS = 128
PEERS = 32
LEVELS = 8
KEYS = 144
ROWS = 304
FAR = 48
SCALE = 1.0 / math.sqrt(HEAD_DIM)
F32 = jnp.float32
BF16 = jnp.bfloat16


def iota2(rows, cols):
    row = lax.broadcasted_iota(jnp.int32, (rows, cols), 0)
    col = lax.broadcasted_iota(jnp.int32, (rows, cols), 1)
    return row, col


def mat(mask, weight):
    return jnp.where(mask, weight, 0.0).astype(BF16)


def mm(left, right, dims=((1,), (0,))):
    return lax.dot_general(left, right, (dims, ((), ())), preferred_element_type=F32)


def pooling(rows, cols):
    row, col = iota2(rows, cols)
    return mat((col >> 1) == row, 0.5)


def pool_kernel(k_ref, v_ref, l1_ref, l2_ref, l3_ref, l4_ref, slot_ref):
    me = lax.axis_index("seq")
    half = pooling(64, 128)
    l1_ref[0:64, :] = mm(half, k_ref[...]).astype(BF16)
    l1_ref[64:128, :] = mm(half, v_ref[...]).astype(BF16)
    l2 = mm(pooling(64, 128), l1_ref[...]).astype(BF16)
    l2_ref[...] = l2
    l3 = mm(pooling(32, 64), l2).astype(BF16)
    l3_ref[...] = l3
    l4 = mm(pooling(16, 32), l3).astype(BF16)
    l4_ref[...] = l4
    row, col = iota2(16, 16)
    l5 = mm(pooling(16, 16), l4).astype(BF16)
    m6 = mat((row < 8) & ((row & 3) < 2) & ((col >> 1) == ((row >> 2) * 2 + (row & 3))), 0.5)
    l6 = mm(m6, l5).astype(BF16)
    m7 = mat((row < 8) & ((row & 3) == 0) & ((col >> 1) == (row >> 1)), 0.5)
    l7 = mm(m7, l6).astype(BF16)
    b5, b6, b7 = l5[0:8], l6[0:8], l7[0:8]
    base7 = ((me >> 4) ^ 1) << 4
    base6 = ((me >> 3) ^ 1) << 3
    base5 = ((me >> 2) ^ 1) << 2
    base4 = (me >> 2) << 2
    for i in range(16):
        slot_ref[base7 + i] = b7
    for i in range(8):
        slot_ref[base6 + i] = b6
    for i in range(4):
        slot_ref[base5 + i] = b5
    for i in range(4):
        slot_ref[base4 + i] = jnp.zeros((8, WIDTH), BF16)


def far_column(me, line):
    at5 = ((((me >> 2) ^ 1) << 2) + (line >> 2)) * 8 + (line & 3)
    six = line - 16
    at6 = ((((me >> 3) ^ 1) << 3) + (six >> 1)) * 8 + (six & 1)
    at7 = ((((me >> 4) ^ 1) << 4) + (line - 32)) * 8
    return jnp.where(line < 16, at5, jnp.where(line < 32, at6, at7))


def score_kernel(
    slope_ref, q_ref, c_ref, k_ref, v_ref, l1_ref, l2_ref, r3_ref, r4a_ref, r4b_ref, r_ref,
    kf_ref, vf_ref, p_ref, d_ref, s_ref,
):
    me = lax.axis_index("seq")
    row, col = iota2(FAR, PEERS * 8)
    place = far_column(me, row)
    far = r_ref[...]
    prow, pcol = iota2(16, 16)
    for out_ref, own_ref, which in ((kf_ref, k_ref, 0), (vf_ref, v_ref, 1)):
        out_ref[0:128, :] = own_ref[...]
        out_ref[128:192, :] = l1_ref[64 * which : 64 * which + 64, :]
        out_ref[192:224, :] = l2_ref[32 * which : 32 * which + 32, :]
        out_ref[224:240, :] = r3_ref[16 * which : 16 * which + 16, :]
        first = mat((prow < 8) & (pcol == prow + 8 * which), 1.0)
        second = mat((prow >= 8) & (pcol == prow - 8 + 8 * which), 1.0)
        out_ref[240:256, :] = (mm(first, r4a_ref[...]) + mm(second, r4b_ref[...])).astype(BF16)
        out_ref[256:304, :] = mm(mat(col == place + 4 * which, 1.0), far).astype(BF16)

    lane = lax.broadcasted_iota(jnp.int32, (1, TOKENS), 1)
    quarter = lane >> 5
    lower = lane < 64

    def compact(full):
        def by_quarter(blocks):
            return jnp.where(
                quarter < 2,
                jnp.where(quarter == 0, blocks[0], blocks[1]),
                jnp.where(quarter == 2, blocks[2], blocks[3]),
            )

        zero = by_quarter([full[32 * g : 32 * g + 32] for g in range(4)])
        one = by_quarter([full[128 + 16 * (g ^ 1) : 144 + 16 * (g ^ 1)] for g in range(4)])
        two = jnp.where(lower, full[208:224], full[192:208])
        return [zero, one, two] + [full[224 + 16 * i : 240 + 16 * i] for i in range(5)]

    total = [None] * HEADS
    for h in range(HEADS):
        sl = slice(h * HEAD_DIM, (h + 1) * HEAD_DIM)
        raw = mm(kf_ref[:, sl], q_ref[:, sl], ((1,), (1,)))
        step = LOG_TWO + slope_ref[h]
        parts = [piece * SCALE + level * step for level, piece in enumerate(compact(raw))]
        scores = jnp.concatenate(parts, axis=0)
        top = jnp.max(scores, axis=0, keepdims=True)
        expo = jnp.exp(scores - top)
        probs = expo * (1.0 / jnp.sum(expo, axis=0, keepdims=True))
        probs_b = probs.astype(BF16)
        dprobs = jnp.concatenate(compact(mm(vf_ref[:, sl], c_ref[:, sl], ((1,), (1,)))), axis=0)
        delta = jnp.sum(probs_b.astype(F32) * dprobs, axis=0, keepdims=True)
        dscores = probs * (dprobs - delta)
        p_ref[h] = probs_b
        d_ref[h] = dscores.astype(BF16)
        acc = None
        for level in range(1, LEVELS):
            at = 16 + 16 * level
            term = level * (dscores[at : at + 8] + dscores[at + 8 : at + 16])
            acc = term if acc is None else acc + term
        total[h] = jnp.sum(acc, axis=0, keepdims=True)
    tile = jnp.concatenate(total, axis=0)
    for i in range(s_ref.shape[0]):
        s_ref[i] = tile


def grad_kernel(
    q_ref, c_ref, kf_ref, vf_ref, p_ref, d_ref,
    dq_ref, gk_ref, gv_ref, g3_ref, g4a_ref, g4b_ref, gf_ref,
):
    lane = lax.broadcasted_iota(jnp.int32, (1, TOKENS), 1)
    quarter = lane >> 5
    lower = lane < 64
    row, col = iota2(TOKENS, 96)
    spread = jnp.where(
        (col < 64) & (col == (row >> 1)),
        0.5,
        jnp.where((col >= 64) & (col - 64 == (row >> 2)), 0.25, 0.0),
    ).astype(BF16)

    def expand(part):
        part = part.astype(F32)
        zero, one, two, rest = part[0:32], part[32:48], part[48:64], part[64:144]
        rows = [jnp.where(quarter == g, zero, 0.0) for g in range(4)]
        rows += [jnp.where(quarter == (g ^ 1), one, 0.0) for g in range(4)]
        rows += [jnp.where(lower, 0.0, two), jnp.where(lower, two, 0.0), rest]
        return jnp.concatenate(rows, axis=0).astype(BF16)

    for h in range(HEADS):
        sl = slice(h * HEAD_DIM, (h + 1) * HEAD_DIM)
        d_full = expand(d_ref[h])
        p_full = expand(p_ref[h])
        dq_ref[:, sl] = (mm(d_full, kf_ref[:, sl], ((0,), (0,))) * SCALE).astype(BF16)
        dk = mm(d_full, q_ref[:, sl]) * SCALE
        dv = mm(p_full, c_ref[:, sl])
        gk_ref[:, sl] = dk[0:128] + mm(spread, dk[128:224].astype(BF16))
        gv_ref[:, sl] = dv[0:128] + mm(spread, dv[128:224].astype(BF16))
        g3_ref[0:16, sl] = dk[224:240].astype(BF16)
        g3_ref[16:32, sl] = dv[224:240].astype(BF16)
        g4a_ref[:, sl] = jnp.concatenate([dk[240:248], dv[240:248]], axis=0).astype(BF16)
        g4b_ref[:, sl] = jnp.concatenate([dk[248:256], dv[248:256]], axis=0).astype(BF16)
        gf_ref[0:FAR, sl] = dk[256:304].astype(BF16)
        gf_ref[FAR : 2 * FAR, sl] = dv[256:304].astype(BF16)


def pack_kernel(gf_ref, s_ref, out_ref):
    me = lax.axis_index("seq")
    row, col = iota2(PEERS * 8, 2 * FAR)
    is_key = col < FAR
    place = far_column(me, jnp.where(is_key, col, col - FAR)) + jnp.where(is_key, 0, 4)
    out_ref[:, 0:WIDTH] = mm(mat(row == place, 1.0), gf_ref[...]).astype(BF16)
    value = jnp.sum(jnp.sum(s_ref[...], axis=0), axis=1, keepdims=True)
    high = value.astype(BF16).astype(F32)
    rest = value - high
    middle = rest.astype(BF16).astype(F32)
    low = rest - middle
    lane = lax.broadcasted_iota(jnp.int32, (HEADS, 128), 1)
    tile = jnp.where(
        lane == 0, high, jnp.where(lane == 1, middle, jnp.where(lane == 2, low, 0.0))
    )
    out_ref[:, WIDTH:] = jnp.concatenate([tile] * PEERS, axis=0).astype(BF16)


def final_kernel(gk_ref, gv_ref, r3_ref, r4a_ref, r4b_ref, r_ref, ok_ref, ov_ref, os_ref):
    me = lax.axis_index("seq")
    row, col = iota2(TOKENS, PEERS * 8)
    apart = (col >> 3) ^ me
    line = col & 7
    shift = jnp.where(apart >= 16, 7, jnp.where(apart >= 8, 6, 5))
    weight = jnp.where(
        apart >= 16, 2.0**-7, jnp.where(apart >= 8, 2.0**-6, jnp.where(apart >= 4, 2.0**-5, 0.0))
    )
    covers = lax.shift_right_logical(row, shift)
    row3, col3 = iota2(TOKENS, 32)
    row4, col4 = iota2(TOKENS, 16)
    for out_ref, own_ref, which in ((ok_ref, gk_ref, 0), (ov_ref, gv_ref, 1)):
        total = own_ref[...]
        total += mm(mat(covers + 4 * which == line, weight), r_ref[:, 0:WIDTH])
        total += mm(mat((row3 >> 3) + 16 * which == col3, 2.0**-3), r3_ref[...])
        both = mat((row4 >> 4) + 8 * which == col4, 2.0**-4)
        total += mm(both, r4a_ref[...]) + mm(both, r4b_ref[...])
        out_ref[...] = total.astype(BF16)
    slopes = r_ref[:, WIDTH:].astype(F32).reshape(PEERS, HEADS, 128)
    value = jnp.sum(jnp.sum(slopes, axis=0), axis=1, keepdims=True)
    srow, scol = iota2(HEADS, 128)
    line = jnp.sum(jnp.where(srow == scol, value, 0.0), axis=0, keepdims=True)
    os_ref[...] = line[:, 0:HEADS]


def call(kernel, outs, ins, flops=0, scalars=0):
    moved = sum(math.prod(s) * 2 for s, _ in outs)
    return pl.pallas_call(
        kernel,
        out_shape=[jax.ShapeDtypeStruct(s, t) for s, t in outs],
        in_specs=[pl.BlockSpec(memory_space=pltpu.SMEM)] * scalars
        + [pl.BlockSpec(memory_space=pltpu.VMEM)] * (len(ins) - scalars),
        out_specs=[pl.BlockSpec(memory_space=pltpu.VMEM)] * len(outs),
        compiler_params=pltpu.CompilerParams(vmem_limit_bytes=32 * 1024 * 1024),
        cost_estimate=pl.CostEstimate(flops=flops, bytes_accessed=2 * moved, transcendentals=0),
    )(*ins)


def swap(block, apart):
    return lax.ppermute(block, "seq", [(i, i ^ apart) for i in range(PEERS)])


def exchange(slots):
    width = slots.shape[-1]
    back = lax.all_to_all(slots.reshape(PEERS, 8, width), "seq", 0, 0)
    return back.reshape(PEERS * 8, width)


def per_device(queries, keys_in, values_in, cotangent, level_slope):
    q, k, v, c = queries[0], keys_in[0], values_in[0], cotangent[0]
    wide = WIDTH
    l1, l2, l3, l4, slots = call(
        pool_kernel,
        [((128, wide), BF16), ((64, wide), BF16), ((32, wide), BF16), ((16, wide), BF16),
         ((PEERS, 8, wide), BF16)],
        (k, v),
    )
    far = exchange(slots)
    near3 = swap(l3, 1)
    near4a = swap(l4, 2)
    near4b = swap(l4, 3)
    groups = lax.axis_size("dp")
    kf, vf, probs, dscores, slopes = call(
        score_kernel,
        [((ROWS, wide), BF16), ((ROWS, wide), BF16), ((HEADS, KEYS, TOKENS), BF16),
         ((HEADS, KEYS, TOKENS), BF16), ((groups, HEADS, 128), F32)],
        (level_slope, q, c, k, v, l1, l2, near3, near4a, near4b, far),
        scalars=1,
    )
    slopes = lax.all_to_all(slopes, "dp", 0, 0)
    dq, gk, gv, g3, g4a, g4b, gf = call(
        grad_kernel,
        [((TOKENS, wide), BF16), ((TOKENS, wide), F32), ((TOKENS, wide), F32), ((32, wide), BF16),
         ((16, wide), BF16), ((16, wide), BF16), ((2 * FAR, wide), BF16)],
        (q, c, kf, vf, probs, dscores),
    )
    (packed,) = call(pack_kernel, [((PEERS * 8, wide + 128), BF16)], (gf, slopes))
    far = exchange(packed)
    near3 = swap(g3, 1)
    near4a = swap(g4a, 2)
    near4b = swap(g4b, 3)
    dk, dv, ds = call(
        final_kernel,
        [((TOKENS, wide), BF16), ((TOKENS, wide), BF16), ((1, HEADS), F32)],
        (gk, gv, near3, near4a, near4b, far),
    )
    return dq[None], dk[None], dv[None], ds.reshape(HEADS)


def solution(mesh):
    row = P("dp", "seq", None)
    return jax.shard_map(
        per_device,
        mesh=mesh,
        in_specs=(row, row, row, row, P()),
        out_specs=(row, row, row, P()),
        check_vma=False,
    )
```

time: 269 us -> 82.1 us (0.31)
  the two profiles are of different devices: /device:TPU:6 before, /device:TPU:1 now
where the time goes in v1:
time: 82.1 us; the launch traced here: 81.4 us
  starting transfers between devices  47 us (57%)
  waiting for transfers between devices  18.6 us (23%)
  Pallas kernels  9.17 us (11%)
  local copies, waits for them, and re-layouts  5.9 us (7%)
    ppermute x6, starting transfers between devices, swap(): return lax.ppermute(block, 'seq', [(i, i ^ apart) for i in range(PEERS)])  18.9 us
    all_to_all x2, starting transfers between devices, exchange(): back = lax.all_to_all(slots.reshape(PEERS, 8, width), 'seq', 0, 0)  18.5 us
    all_to_all x1, starting transfers between devices, per_device(): slopes = lax.all_to_all(slopes, 'dp', 0, 0)  9.5 us
    pallas_call x5, Pallas kernels, call(): pl.pallas_call(kernel, out_shape=[jax.ShapeDtypeStruct(s, t) for s, t in...  9.17 us
    ppermute x6, waiting for transfers between devices, swap(): return lax.ppermute(block, 'seq', [(i, i ^ apart) for i in range(PEERS)])  8.62 us
    all_to_all x2, waiting for transfers between devices, exchange(): back = lax.all_to_all(slots.reshape(PEERS, 8, width), 'seq', 0, 0)  6.53 us
    unnamed x22, local copies, waits for them, and re-layouts  5.9 us
    all_to_all x1, waiting for transfers between devices, per_device(): slopes = lax.all_to_all(slopes, 'dp', 0, 0)  3.43 us
  transfers between devices with their start and end apart: 9, of which 6 were waited for; matrix products, arithmetic and copies ran while one was open for 0% of the time, Pallas kernels for 3%

profile of v1, /device:TPU:1, one launch (start us, length us, event | category | flops | bytes accessed | tf_op | source)
XLA Modules:
  0.0 81.4 jit_solution(9295129443094840841)
XLA Ops:
  0.6 0.0 copy-start.2
  0.6 0.9 %copy-done.2 = bf16[1,128,1024]{2,1,0:T(8,128)(2,1)S(1)} copy-done((bf16[1,128,1024]{2,1,0:T(8,128)(2,1)S(1)}, bf16[1,128,1024]{2,1,0:T(8,128)(2,1)}, u32[]{:S(2)}) %copy-start.2) | copy-done | bytes 262168
  1.6 0.9 %copy-done.4 = bf16[1,128,1024]{2,1,0:T(8,128)(2,1)S(1)} copy-done((bf16[1,128,1024]{2,1,0:T(8,128)(2,1)S(1)}, bf16[1,128,1024]{2,1,0:T(8,128)(2,1)}, u32[]{:S(2)}) %copy-start.4) | copy-done | bytes 262168
  2.5 1.8 %shard_map.84 = (bf16[128,1024]{1,0:T(8,128)(2,1)S(1)}, bf16[64,1024]{1,0:T(8,128)(2,1)S(1)}, bf16[32,1024]{1,0:T(8,128)(2,1)S(1)}, bf16[16,1024]{1,0:T(8,128)(2,1)S(1)}, bf16[32,8,1024]{2,1,0:T(8,128)(2,1)}) custom-call(bf16[128,1024]{1,0:T(8,128)(2,1)S(1)} %bitcast.17, bf16[128,1024]{1,0:T(8,128)(2,1)S(1)} %bitcast.19), custom_call_target="tpu_custom_call" | custom-call | bytes 2031616 | tf_op jit(solution)/shard_map/pallas_call | solution.py:232
  4.3 13.9 %all-to-all-start = ((bf16[32,8,1024]{2,1,0:T(8,128)(2,1)}), bf16[32,8,1024]{2,1,0:T(8,128)(2,1)S(1)}, u32[]{:S(2)}, u32[]{:S(2)}) async-start(bf16[32,8,1024]{2,1,0:T(8,128)(2,1)} %get-tuple-element.28), calls=%async_computation | async-start | bytes 1048576 | tf_op jit(solution)/shard_map/all_to_all | solution.py:249
  18.2 3.1 %collective-permute-start = (bf16[32,1024]{1,0:T(8,128)(2,1)S(1)}, bf16[32,1024]{1,0:T(8,128)(2,1)S(1)}, u32[]{:S(2)}, u32[]{:S(2)}) collective-permute-start(bf16[32,1024]{1,0:T(8,128)(2,1)S(1)} %get-tuple-element.26), channel_id=1, source_target_pairs={{0,1},{1,0},{2,3},{3,2},{4,5},{5,4},{6,7},{7,6},{8,9},{9,8},{10,11... | collective-permute-start | bytes 196616 | tf_op jit(solution)/shard_map/ppermute | solution.py:244
  21.4 3.7 %collective-permute-start.2 = (bf16[16,1024]{1,0:T(8,128)(2,1)S(1)}, bf16[16,1024]{1,0:T(8,128)(2,1)S(1)}, u32[]{:S(2)}, u32[]{:S(2)}) collective-permute-start(bf16[16,1024]{1,0:T(8,128)(2,1)S(1)} %get-tuple-element.27), channel_id=1, source_target_pairs={{0,3},{1,2},{2,1},{3,0},{4,7},{5,6},{6,5},{7,4},{8,11},{9,10},{10,... | collective-permute-start | bytes 98312 | tf_op jit(solution)/shard_map/ppermute | solution.py:244
  25.1 2.5 %collective-permute-start.1 = (bf16[16,1024]{1,0:T(8,128)(2,1)S(1)}, bf16[16,1024]{1,0:T(8,128)(2,1)S(1)}, u32[]{:S(2)}, u32[]{:S(2)}) collective-permute-start(bf16[16,1024]{1,0:T(8,128)(2,1)S(1)} %get-tuple-element.27), channel_id=1, source_target_pairs={{0,2},{1,3},{2,0},{3,1},{4,6},{5,7},{6,4},{7,5},{8,10},{9,11},{10,... | collective-permute-start | bytes 98312 | tf_op jit(solution)/shard_map/ppermute | solution.py:244
  27.6 0.0 collective-permute-done.2.r4b_ref
  27.6 4.1 %collective-permute-done.1.r4a_ref = bf16[16,1024]{1,0:T(8,128)(2,1)S(1)} collective-permute-done((bf16[16,1024]{1,0:T(8,128)(2,1)S(1)}, bf16[16,1024]{1,0:T(8,128)(2,1)S(1)}, u32[]{:S(2)}, u32[]{:S(2)}) %collective-permute-start.1) | collective-permute-done | bytes 32800 | tf_op jit(solution)/shard_map/ppermute | solution.py:244
  31.7 0.0 collective-permute-done.r3_ref
  31.7 2.8 %all-to-all-done = bf16[32,8,1024]{2,1,0:T(8,128)(2,1)S(1)} async-done(((bf16[32,8,1024]{2,1,0:T(8,128)(2,1)}), bf16[32,8,1024]{2,1,0:T(8,128)(2,1)S(1)}, u32[]{:S(2)}, u32[]{:S(2)}) %all-to-all-start) | async-done | bytes 524320 | tf_op jit(solution)/shard_map/all_to_all | solution.py:249
  34.5 0.0 copy-done
  34.5 0.6 copy-done.10
  35.1 2.4 %shard_map.85 = (bf16[304,1024]{1,0:T(8,128)(2,1)S(1)}, bf16[304,1024]{1,0:T(8,128)(2,1)S(1)}, bf16[8,144,128]{2,1,0:T(8,128)(2,1)S(1)}, bf16[8,144,128]{2,1,0:T(8,128)(2,1)S(1)}, f32[16,8,128]{2,1,0:T(8,128)}) custom-call(f32[8]{0:T(128)S(1)} %copy-done.10, bf16[128,1024]{1,0:T(8,128)(2,1)S(1)} %bitcast.13, bf16[128,1024]{1,0:T(8,128)(2,1)S(1)} %bitcast.15, ...), custom_call_target="tpu_custom_call" | custom-call | bytes 3735552 | tf_op jit(solution)/shard_map/pallas_call | solution.py:232
  37.5 0.7 copy-done.6
  38.2 0.7 copy-done.8
  39.0 9.5 %all-to-all-start.1 = ((f32[16,8,128]{2,1,0:T(8,128)}), f32[16,8,128]{2,1,0:T(8,128)S(1)}, u32[]{:S(2)}, u32[]{:S(2)}) async-start(f32[16,8,128]{2,1,0:T(8,128)} %get-tuple-element.40), calls=%async_computation.1 | async-start | bytes 131072 | tf_op jit(solution)/shard_map/all_to_all | solution.py:274
  48.5 1.0 %copy-done.7 = bf16[8,144,128]{2,1,0:T(8,128)(2,1)S(1)} copy-done((bf16[8,144,128]{2,1,0:T(8,128)(2,1)S(1)}, bf16[8,144,128]{2,1,0:T(8,128)(2,1)}, u32[]{:S(2)}) %copy-start.7) | copy-done | bytes 294936
  49.4 1.0 %copy-done.9 = bf16[8,144,128]{2,1,0:T(8,128)(2,1)S(1)} copy-done((bf16[8,144,128]{2,1,0:T(8,128)(2,1)S(1)}, bf16[8,144,128]{2,1,0:T(8,128)(2,1)}, u32[]{:S(2)}) %copy-start.9) | copy-done | bytes 294936
  50.4 2.5 %shard_map.86 = (bf16[128,1024]{1,0:T(8,128)(2,1)}, f32[128,1024]{1,0:T(8,128)S(1)}, f32[128,1024]{1,0:T(8,128)S(1)}, bf16[32,1024]{1,0:T(8,128)(2,1)S(1)}, bf16...) custom-call(bf16[128,1024]{1,0:T(8,128)(2,1)S(1)} %bitcast.14, ...), custom_call_target="tpu_custom_call" | custom-call | bytes 2228224 | tf_op jit(solution)/shard_map/pallas_call | solution.py:232
  52.8 3.4 %all-to-all-done.1.s_ref = f32[16,8,128]{2,1,0:T(8,128)S(1)} async-done(((f32[16,8,128]{2,1,0:T(8,128)}), f32[16,8,128]{2,1,0:T(8,128)S(1)}, u32[]{:S(2)}, u32[]{:S(2)}) %all-to-all-start.1) | async-done | bytes 65568 | tf_op jit(solution)/shard_map/all_to_all | solution.py:274
  56.3 1.1 %shard_map.87 = bf16[256,1152]{1,0:T(8,128)(2,1)} custom-call(bf16[96,1024]{1,0:T(8,128)(2,1)S(1)} %get-tuple-element.39.gf_ref, f32[16,8,128]{2,1,0:T(8,128)S(1)} %all-to-all-done.1.s_ref), custom_call_target="tpu_custom_call" | custom-call | bytes 1179648 | tf_op jit(solution)/shard_map/pallas_call | solution.py:232
  57.4 4.7 %all-to-all-start.2 = ((bf16[32,8,1152]{2,1,0:T(8,128)(2,1)}), bf16[32,8,1152]{2,1,0:T(8,128)(2,1)S(1)}, u32[]{:S(2)}, u32[]{:S(2)}) async-start(bf16[32,8,1152]{2,1,0:T(8,128)(2,1)} %bitcast.6), calls=%async_computation.2 | async-start | bytes 1179648 | tf_op jit(solution)/shard_map/all_to_all | solution.py:249
  62.1 3.1 %collective-permute-start.3 = (bf16[32,1024]{1,0:T(8,128)(2,1)S(1)}, bf16[32,1024]{1,0:T(8,128)(2,1)S(1)}, u32[]{:S(2)}, u32[]{:S(2)}) collective-permute-start(bf16[32,1024]{1,0:T(8,128)(2,1)S(1)} %get-tuple-element.36), channel_id=1, source_target_pairs={{0,1},{1,0},{2,3},{3,2},{4,5},{5,4},{6,7},{7,6},{8,9},{9,8},{10,11... | collective-permute-start | bytes 196616 | tf_op jit(solution)/shard_map/ppermute | solution.py:244
  65.2 4.3 %collective-permute-start.4 = (bf16[16,1024]{1,0:T(8,128)(2,1)S(1)}, bf16[16,1024]{1,0:T(8,128)(2,1)S(1)}, u32[]{:S(2)}, u32[]{:S(2)}) collective-permute-start(bf16[16,1024]{1,0:T(8,128)(2,1)S(1)} %get-tuple-element.37), channel_id=1, source_target_pairs={{0,2},{1,3},{2,0},{3,1},{4,6},{5,7},{6,4},{7,5},{8,10},{9,11},{10,... | collective-permute-start | bytes 98312 | tf_op jit(solution)/shard_map/ppermute | solution.py:244
  69.5 2.1 %collective-permute-start.5 = (bf16[16,1024]{1,0:T(8,128)(2,1)S(1)}, bf16[16,1024]{1,0:T(8,128)(2,1)S(1)}, u32[]{:S(2)}, u32[]{:S(2)}) collective-permute-start(bf16[16,1024]{1,0:T(8,128)(2,1)S(1)} %get-tuple-element.38), channel_id=1, source_target_pairs={{0,3},{1,2},{2,1},{3,0},{4,7},{5,6},{6,5},{7,4},{8,11},{9,10},{10,... | collective-permute-start | bytes 98312 | tf_op jit(solution)/shard_map/ppermute | solution.py:244
  71.7 0.4 collective-permute-done.4.r4a_ref
  72.1 4.1 %collective-permute-done.5.r4b_ref = bf16[16,1024]{1,0:T(8,128)(2,1)S(1)} collective-permute-done((bf16[16,1024]{1,0:T(8,128)(2,1)S(1)}, bf16[16,1024]{1,0:T(8,128)(2,1)S(1)}, u32[]{:S(2)}, u32[]{:S(2)}) %collective-permute-start.5) | collective-permute-done | bytes 32800 | tf_op jit(solution)/shard_map/ppermute | solution.py:244
  76.2 0.0 collective-permute-done.3.r3_ref
  76.2 3.8 %all-to-all-done.2 = bf16[32,8,1152]{2,1,0:T(8,128)(2,1)S(1)} async-done(((bf16[32,8,1152]{2,1,0:T(8,128)(2,1)}), bf16[32,8,1152]{2,1,0:T(8,128)(2,1)S(1)}, u32[]{:S(2)}, u32[]{:S(2)}) %all-to-all-start.2) | async-done | bytes 589856 | tf_op jit(solution)/shard_map/all_to_all | solution.py:249
  80.0 1.4 %shard_map.88 = (bf16[128,1024]{1,0:T(8,128)(2,1)}, bf16[128,1024]{1,0:T(8,128)(2,1)}, f32[1,8]{1,0:T(1,128)}) custom-call(f32[128,1024]{1,0:T(8,128)S(1)} %get-tuple-element.34.gk_ref, f32[128,1024]{1,0:T(8,128)S(1)} %get-tuple-element.35.gv_ref, bf16[32,1024]{1,0:T(8,128)(2,1)S(1)} %collective-permute-done.3.r3_ref, ...), custom_call_target="tpu_custom_call" | custom-call | bytes 1048608 | tf_op jit(solution)/shard_map/pallas_call | solution.py:232
  (13 shorter events, 0.0 us)
Async XLA Ops:
  0.6 1.0 %copy-start.2 = (bf16[1,128,1024]{2,1,0:T(8,128)(2,1)S(1)}, bf16[1,128,1024]{2,1,0:T(8,128)(2,1)}, u32[]{:S(2)}) copy-start(bf16[1,128,1024]{2,1,0:T(8,128)(2,1)} %param.6) | copy-start | bytes 786436
  1.6 0.9 %copy-start.4 = (bf16[1,128,1024]{2,1,0:T(8,128)(2,1)S(1)}, bf16[1,128,1024]{2,1,0:T(8,128)(2,1)}, u32[]{:S(2)}) copy-start(bf16[1,128,1024]{2,1,0:T(8,128)(2,1)} %param.7) | copy-start | bytes 786436
  4.3 30.2 %copy-start = (bf16[1,128,1024]{2,1,0:T(8,128)(2,1)S(1)}, bf16[1,128,1024]{2,1,0:T(8,128)(2,1)}, u32[]{:S(2)}) copy-start(bf16[1,128,1024]{2,1,0:T(8,128)(2,1)} %param.5) | copy-start | bytes 786436
  4.3 30.2 %copy-start.1 = (bf16[1,128,1024]{2,1,0:T(8,128)(2,1)S(1)}, bf16[1,128,1024]{2,1,0:T(8,128)(2,1)}, u32[]{:S(2)}) copy-start(bf16[1,128,1024]{2,1,0:T(8,128)(2,1)} %param.8) | copy-start | bytes 786436
  4.3 30.2 %copy-start.3 = (bf16[1,128,1024]{2,1,0:T(8,128)(2,1)S(1)}, bf16[1,128,1024]{2,1,0:T(8,128)(2,1)}, u32[]{:S(2)}) copy-start(bf16[1,128,1024]{2,1,0:T(8,128)(2,1)} %param.6) | copy-start | bytes 786436
  4.3 30.2 %copy-start.5 = (bf16[1,128,1024]{2,1,0:T(8,128)(2,1)S(1)}, bf16[1,128,1024]{2,1,0:T(8,128)(2,1)}, u32[]{:S(2)}) copy-start(bf16[1,128,1024]{2,1,0:T(8,128)(2,1)} %param.7) | copy-start | bytes 786436
  4.3 30.1 %all-to-all-start = ((bf16[32,8,1024]{2,1,0:T(8,128)(2,1)}), bf16[32,8,1024]{2,1,0:T(8,128)(2,1)S(1)}, u32[]{:S(2)}, u32[]{:S(2)}) async-start(bf16[32,8,1024]{2,1,0:T(8,128)(2,1)} %get-tuple-element.28), calls=%async_computation | async-start | bytes 1048576 | tf_op jit(solution)/shard_map/all_to_all | solution.py:249
  18.2 13.5 %collective-permute-start = (bf16[32,1024]{1,0:T(8,128)(2,1)S(1)}, bf16[32,1024]{1,0:T(8,128)(2,1)S(1)}, u32[]{:S(2)}, u32[]{:S(2)}) collective-permute-start(bf16[32,1024]{1,0:T(8,128)(2,1)S(1)} %get-tuple-element.26), channel_id=1, source_target_pairs={{0,1},{1,0},{2,3},{3,2},{4,5},{5,4},{6,7},{7,6},{8,9},{9,8},{10,11... | collective-permute-start | bytes 196616 | tf_op jit(solution)/shard_map/ppermute | solution.py:244
  21.4 6.2 %collective-permute-start.2 = (bf16[16,1024]{1,0:T(8,128)(2,1)S(1)}, bf16[16,1024]{1,0:T(8,128)(2,1)S(1)}, u32[]{:S(2)}, u32[]{:S(2)}) collective-permute-start(bf16[16,1024]{1,0:T(8,128)(2,1)S(1)} %get-tuple-element.27), channel_id=1, source_target_pairs={{0,3},{1,2},{2,1},{3,0},{4,7},{5,6},{6,5},{7,4},{8,11},{9,10},{10,... | collective-permute-start | bytes 98312 | tf_op jit(solution)/shard_map/ppermute | solution.py:244
  25.1 6.6 %collective-permute-start.1 = (bf16[16,1024]{1,0:T(8,128)(2,1)S(1)}, bf16[16,1024]{1,0:T(8,128)(2,1)S(1)}, u32[]{:S(2)}, u32[]{:S(2)}) collective-permute-start(bf16[16,1024]{1,0:T(8,128)(2,1)S(1)} %get-tuple-element.27), channel_id=1, source_target_pairs={{0,2},{1,3},{2,0},{3,1},{4,6},{5,7},{6,4},{7,5},{8,10},{9,11},{10,... | collective-permute-start | bytes 98312 | tf_op jit(solution)/shard_map/ppermute | solution.py:244
  34.5 0.7 copy-start.10
  37.5 0.7 copy-start.6
  38.2 0.7 copy-start.8
  39.0 17.3 %all-to-all-start.1 = ((f32[16,8,128]{2,1,0:T(8,128)}), f32[16,8,128]{2,1,0:T(8,128)S(1)}, u32[]{:S(2)}, u32[]{:S(2)}) async-start(f32[16,8,128]{2,1,0:T(8,128)} %get-tuple-element.40), calls=%async_computation.1 | async-start | bytes 131072 | tf_op jit(solution)/shard_map/all_to_all | solution.py:274
  48.5 1.0 %copy-start.7 = (bf16[8,144,128]{2,1,0:T(8,128)(2,1)S(1)}, bf16[8,144,128]{2,1,0:T(8,128)(2,1)}, u32[]{:S(2)}) copy-start(bf16[8,144,128]{2,1,0:T(8,128)(2,1)} %copy-done.6) | copy-start | bytes 884740
  49.4 1.0 %copy-start.9 = (bf16[8,144,128]{2,1,0:T(8,128)(2,1)S(1)}, bf16[8,144,128]{2,1,0:T(8,128)(2,1)}, u32[]{:S(2)}) copy-start(bf16[8,144,128]{2,1,0:T(8,128)(2,1)} %copy-done.8) | copy-start | bytes 884740
  57.4 22.6 %all-to-all-start.2 = ((bf16[32,8,1152]{2,1,0:T(8,128)(2,1)}), bf16[32,8,1152]{2,1,0:T(8,128)(2,1)S(1)}, u32[]{:S(2)}, u32[]{:S(2)}) async-start(bf16[32,8,1152]{2,1,0:T(8,128)(2,1)} %bitcast.6), calls=%async_computation.2 | async-start | bytes 1179648 | tf_op jit(solution)/shard_map/all_to_all | solution.py:249
  62.1 14.1 %collective-permute-start.3 = (bf16[32,1024]{1,0:T(8,128)(2,1)S(1)}, bf16[32,1024]{1,0:T(8,128)(2,1)S(1)}, u32[]{:S(2)}, u32[]{:S(2)}) collective-permute-start(bf16[32,1024]{1,0:T(8,128)(2,1)S(1)} %get-tuple-element.36), channel_id=1, source_target_pairs={{0,1},{1,0},{2,3},{3,2},{4,5},{5,4},{6,7},{7,6},{8,9},{9,8},{10,11... | collective-permute-start | bytes 196616 | tf_op jit(solution)/shard_map/ppermute | solution.py:244
  65.2 6.8 %collective-permute-start.4 = (bf16[16,1024]{1,0:T(8,128)(2,1)S(1)}, bf16[16,1024]{1,0:T(8,128)(2,1)S(1)}, u32[]{:S(2)}, u32[]{:S(2)}) collective-permute-start(bf16[16,1024]{1,0:T(8,128)(2,1)S(1)} %get-tuple-element.37), channel_id=1, source_target_pairs={{0,2},{1,3},{2,0},{3,1},{4,6},{5,7},{6,4},{7,5},{8,10},{9,11},{10,... | collective-permute-start | bytes 98312 | tf_op jit(solution)/shard_map/ppermute | solution.py:244
  69.5 6.7 %collective-permute-start.5 = (bf16[16,1024]{1,0:T(8,128)(2,1)S(1)}, bf16[16,1024]{1,0:T(8,128)(2,1)S(1)}, u32[]{:S(2)}, u32[]{:S(2)}) collective-permute-start(bf16[16,1024]{1,0:T(8,128)(2,1)S(1)} %get-tuple-element.38), channel_id=1, source_target_pairs={{0,3},{1,2},{2,1},{3,0},{4,7},{5,6},{6,5},{7,4},{8,11},{9,10},{10,... | collective-permute-start | bytes 98312 | tf_op jit(solution)/shard_map/ppermute | solution.py:244

commit v2 on v1

v2 whole, which is shorter than its diff:
```python
import math

import jax
import jax.numpy as jnp
from jax import lax
from jax.experimental import pallas as pl
from jax.experimental.pallas import tpu as pltpu
from jax.sharding import PartitionSpec as P

LOG_TWO = math.log(2.0)
HEADS = 8
HEAD_DIM = 128
WIDTH = HEADS * HEAD_DIM
TOKENS = 128
PEERS = 32
LEVELS = 8
KEYS = 144
FAR = 48
SCALE = 1.0 / math.sqrt(HEAD_DIM)
LONG = 1 << 28
F32 = jnp.float32
BF16 = jnp.bfloat16


def iota2(rows, cols):
    row = lax.broadcasted_iota(jnp.int32, (rows, cols), 0)
    col = lax.broadcasted_iota(jnp.int32, (rows, cols), 1)
    return row, col


def mat(mask, weight):
    return jnp.where(mask, weight, 0.0).astype(BF16)


def mm(left, right, dims=((1,), (0,))):
    return lax.dot_general(left, right, (dims, ((), ())), preferred_element_type=F32)


def pooling(rows, cols):
    row, col = iota2(rows, cols)
    return mat((col >> 1) == row, 0.5)


def three_parts(value):
    high = value.astype(BF16).astype(F32)
    rest = value - high
    middle = rest.astype(BF16).astype(F32)
    return high, middle, rest - middle


LOCAL = 224
STEP = 2 * LOCAL
REMOTE = 80
PROBS = 2 * REMOTE
DSCORES = PROBS + KEYS


def pool_kernel(k_hbm, v_hbm, slope_hbm, kv_ref, l3_ref, l4_ref, slot_ref, slope_ref, sems):
    me = lax.axis_index("seq")
    fetch_k = pltpu.make_async_copy(k_hbm, kv_ref.at[pl.ds(0, TOKENS)], sems.at[0])
    fetch_v = pltpu.make_async_copy(v_hbm, kv_ref.at[pl.ds(LOCAL, TOKENS)], sems.at[1])
    fetch_slope = pltpu.make_async_copy(slope_hbm, slope_ref, sems.at[2])
    fetch_k.start()
    fetch_v.start()
    fetch_slope.start()
    half = pooling(64, 128)
    quarter = pooling(32, 64)
    fetch_slope.wait()
    line = lax.broadcasted_iota(jnp.int32, (16, HEAD_DIM), 0)
    for h in range(HEADS):
        high, middle, low = three_parts(jnp.full((16, HEAD_DIM), LOG_TWO + slope_ref[h], F32))
        part = jnp.where(line == 0, high, jnp.where(line == 1, middle, jnp.where(line == 2, low, 0.0)))
        kv_ref[STEP : STEP + 16, h * HEAD_DIM : (h + 1) * HEAD_DIM] = part.astype(BF16)
    l2 = []
    for fetch, at in ((fetch_k, 0), (fetch_v, LOCAL)):
        fetch.wait()
        one = mm(half, kv_ref[at : at + 128, :]).astype(BF16)
        kv_ref[at + 128 : at + 192, :] = one
        two = mm(quarter, one).astype(BF16)
        kv_ref[at + 192 : at + 224, :] = two
        l2.append(two)
    l3 = mm(quarter, jnp.concatenate(l2, axis=0)).astype(BF16)
    l3_ref[...] = l3
    l4 = mm(pooling(16, 32), l3).astype(BF16)
    l4_ref[...] = l4
    row, col = iota2(16, 16)
    l5 = mm(pooling(16, 16), l4).astype(BF16)
    m6 = mat((row < 8) & ((row & 3) < 2) & ((col >> 1) == ((row >> 2) * 2 + (row & 3))), 0.5)
    l6 = mm(m6, l5).astype(BF16)
    m7 = mat((row < 8) & ((row & 3) == 0) & ((col >> 1) == (row >> 1)), 0.5)
    l7 = mm(m7, l6).astype(BF16)
    b5, b6, b7 = l5[0:8], l6[0:8], l7[0:8]
    base7 = ((me >> 4) ^ 1) << 4
    base6 = ((me >> 3) ^ 1) << 3
    base5 = ((me >> 2) ^ 1) << 2
    base4 = (me >> 2) << 2
    for i in range(16):
        slot_ref[base7 + i] = b7
    for i in range(8):
        slot_ref[base6 + i] = b6
    for i in range(4):
        slot_ref[base5 + i] = b5
    for i in range(4):
        slot_ref[base4 + i] = jnp.zeros((8, WIDTH), BF16)


def far_column(me, line):
    at5 = ((((me >> 2) ^ 1) << 2) + (line >> 2)) * 8 + (line & 3)
    six = line - 16
    at6 = ((((me >> 3) ^ 1) << 3) + (six >> 1)) * 8 + (six & 1)
    at7 = ((((me >> 4) ^ 1) << 4) + (line - 32)) * 8
    return jnp.where(line < 16, at5, jnp.where(line < 32, at6, at7))


def local_kernel(q_hbm, c_hbm, kv_ref, qc_ref, s_ref, sems):
    fetch_q = pltpu.make_async_copy(q_hbm, qc_ref.at[pl.ds(0, TOKENS)], sems.at[0])
    fetch_c = pltpu.make_async_copy(c_hbm, qc_ref.at[pl.ds(TOKENS, TOKENS)], sems.at[1])
    fetch_q.start()
    fetch_c.start()
    lane = lax.broadcasted_iota(jnp.int32, (1, TOKENS), 1)
    quarter = lane >> 5
    lower = lane < 64


    def compact(full):
        def by_quarter(blocks):
            return jnp.where(
                quarter < 2,
                jnp.where(quarter == 0, blocks[0], blocks[1]),
                jnp.where(quarter == 2, blocks[2], blocks[3]),
            )

        zero = by_quarter([full[32 * g : 32 * g + 32] for g in range(4)])
        one = by_quarter([full[128 + 16 * (g ^ 1) : 144 + 16 * (g ^ 1)] for g in range(4)])
        two = jnp.where(lower, full[208:224], full[192:208])
        return zero, one, two

    step_all = jnp.sum(kv_ref[STEP : STEP + 16, :].astype(F32), axis=0, keepdims=True)
    for which, fetch in enumerate((fetch_q, fetch_c)):
        fetch.wait()
        for h in range(HEADS):
            sl = slice(h * HEAD_DIM, (h + 1) * HEAD_DIM)
            keys = kv_ref[LOCAL * which : LOCAL * which + LOCAL, sl]
            raw = mm(keys, qc_ref[TOKENS * which : TOKENS * which + TOKENS, sl], ((1,), (1,)))
            zero, one, two = compact(raw)
            if which == 0:
                step = step_all[:, sl]
                zero, one, two = zero * SCALE, one * SCALE + step, two * SCALE + 2 * step
            s_ref[64 * which : 64 * which + 64, sl] = jnp.concatenate([zero, one, two], axis=0)


def score_kernel(kv_ref, qc_ref, near_ref, r3_ref, r4a_ref, r4b_ref, r_ref, w_ref, s_ref):
    me = lax.axis_index("seq")
    row, col = iota2(FAR, PEERS * 8)
    place = far_column(me, row)
    far = r_ref[...]
    prow, pcol = iota2(16, 16)
    for which in range(2):
        at = REMOTE * which
        w_ref[at : at + 16, :] = r3_ref[16 * which : 16 * which + 16, :]
        first = mat((prow < 8) & (pcol == prow + 8 * which), 1.0)
        second = mat((prow >= 8) & (pcol == prow - 8 + 8 * which), 1.0)
        four = mm(first, r4a_ref[...]) + mm(second, r4b_ref[...])
        w_ref[at + 16 : at + 32, :] = four.astype(BF16)
        w_ref[at + 32 : at + 80, :] = mm(mat(col == place + 4 * which, 1.0), far).astype(BF16)
    step_all = jnp.sum(kv_ref[STEP : STEP + 16, :].astype(F32), axis=0, keepdims=True)
    total = [None] * HEADS
    for h in range(HEADS):
        sl = slice(h * HEAD_DIM, (h + 1) * HEAD_DIM)
        raw = mm(w_ref[0:REMOTE, sl], qc_ref[0:TOKENS, sl], ((1,), (1,)))
        step = step_all[:, sl]
        parts = [near_ref[0:64, sl]]
        parts += [raw[16 * i : 16 * i + 16] * SCALE + (i + 3) * step for i in range(5)]
        scores = jnp.concatenate(parts, axis=0)
        top = jnp.max(scores, axis=0, keepdims=True)
        expo = jnp.exp(scores - top)
        probs = expo * (1.0 / jnp.sum(expo, axis=0, keepdims=True))
        probs_b = probs.astype(BF16)
        raw = mm(w_ref[REMOTE : 2 * REMOTE, sl], qc_ref[TOKENS : 2 * TOKENS, sl], ((1,), (1,)))
        dprobs = jnp.concatenate([near_ref[64:128, sl], raw], axis=0)
        delta = jnp.sum(probs_b.astype(F32) * dprobs, axis=0, keepdims=True)
        dscores = probs * (dprobs - delta)
        w_ref[PROBS : PROBS + KEYS, sl] = probs_b
        w_ref[DSCORES : DSCORES + KEYS, sl] = dscores.astype(BF16)
        acc = None
        for level in range(1, LEVELS):
            at = 16 + 16 * level
            term = level * (dscores[at : at + 8] + dscores[at + 8 : at + 16])
            acc = term if acc is None else acc + term
        total[h] = jnp.sum(acc, axis=0, keepdims=True)
    tile = jnp.concatenate(total, axis=0)
    for i in range(s_ref.shape[0]):
        s_ref[i] = tile


def grad_kernel(kv_ref, qc_ref, w_ref, dq_ref, gk_ref, gv_ref, g3_ref, g4a_ref, g4b_ref, slot_ref, gf_ref):
    me = lax.axis_index("seq")
    lane = lax.broadcasted_iota(jnp.int32, (1, TOKENS), 1)
    quarter = lane >> 5
    lower = lane < 64

    srow, scol = iota2(TOKENS, 96)
    spread = jnp.where(
        (scol < 64) & (scol == (srow >> 1)),
        0.5,
        jnp.where((scol >= 64) & (scol - 64 == (srow >> 2)), 0.25, 0.0),
    ).astype(BF16)

    def expand(part):
        part = part.astype(F32)
        zero, one, two = part[0:32], part[32:48], part[48:64]
        rows = [jnp.where(quarter == g, zero, 0.0) for g in range(4)]
        rows += [jnp.where(quarter == (g ^ 1), one, 0.0) for g in range(4)]
        rows += [jnp.where(lower, 0.0, two), jnp.where(lower, two, 0.0)]
        return jnp.concatenate(rows, axis=0).astype(BF16)

    for h in range(HEADS):
        sl = slice(h * HEAD_DIM, (h + 1) * HEAD_DIM)
        q, c = qc_ref[0:TOKENS, sl], qc_ref[TOKENS : 2 * TOKENS, sl]
        d_near = expand(w_ref[DSCORES : DSCORES + 64, sl])
        p_near = expand(w_ref[PROBS : PROBS + 64, sl])
        d_far = w_ref[DSCORES + 64 : DSCORES + KEYS, sl]
        p_far = w_ref[PROBS + 64 : PROBS + KEYS, sl]
        dq = mm(d_near, kv_ref[0:LOCAL, sl], ((0,), (0,))) + mm(d_far, w_ref[0:REMOTE, sl], ((0,), (0,)))
        dq_ref[:, sl] = (dq * SCALE).astype(BF16)
        dk = mm(d_near, q) * SCALE
        dv = mm(p_near, c)
        gk_ref[:, sl] = dk[0:128] + mm(spread, dk[128:224].astype(BF16))
        gv_ref[:, sl] = dv[0:128] + mm(spread, dv[128:224].astype(BF16))
        dk = mm(d_far, q) * SCALE
        dv = mm(p_far, c)
        g3_ref[0:16, sl] = dk[0:16].astype(BF16)
        g3_ref[16:32, sl] = dv[0:16].astype(BF16)
        g4a_ref[:, sl] = jnp.concatenate([dk[16:24], dv[16:24]], axis=0).astype(BF16)
        g4b_ref[:, sl] = jnp.concatenate([dk[24:32], dv[24:32]], axis=0).astype(BF16)
        gf_ref[0:FAR, sl] = dk[32:80].astype(BF16)
        gf_ref[FAR : 2 * FAR, sl] = dv[32:80].astype(BF16)
    row, col = iota2(PEERS * 8, 2 * FAR)
    is_key = col < FAR
    place = far_column(me, jnp.where(is_key, col, col - FAR)) + jnp.where(is_key, 0, 4)
    slot_ref[:, 0:WIDTH] = mm(mat(row == place, 1.0), gf_ref[...]).astype(BF16)
    slot_ref[:, WIDTH:] = jnp.zeros((PEERS * 8, 128), BF16)


def slope_kernel(s_ref, slot_in, slot_out, tile_ref, sem):
    value = jnp.sum(jnp.sum(s_ref[...], axis=0), axis=1, keepdims=True)
    high, middle, low = three_parts(value)
    lane = lax.broadcasted_iota(jnp.int32, (HEADS, 128), 1)
    tile = jnp.where(
        lane == 0, high, jnp.where(lane == 1, middle, jnp.where(lane == 2, low, 0.0))
    )
    tile_ref[...] = jnp.concatenate([tile] * PEERS, axis=0).astype(BF16)
    put = pltpu.make_async_copy(tile_ref, slot_out.at[:, pl.ds(WIDTH, 128)], sem)
    put.start()
    put.wait()


def final_kernel(gk_ref, gv_ref, r3_ref, r4a_ref, r4b_ref, r_ref, ok_ref, ov_ref, os_ref):
    me = lax.axis_index("seq")
    row, col = iota2(TOKENS, PEERS * 8)
    apart = (col >> 3) ^ me
    line = col & 7
    shift = jnp.where(apart >= 16, 7, jnp.where(apart >= 8, 6, 5))
    weight = jnp.where(
        apart >= 16, 2.0**-7, jnp.where(apart >= 8, 2.0**-6, jnp.where(apart >= 4, 2.0**-5, 0.0))
    )
    covers = lax.shift_right_logical(row, shift)
    row3, col3 = iota2(TOKENS, 32)
    row4, col4 = iota2(TOKENS, 16)
    for out_ref, own_ref, which in ((ok_ref, gk_ref, 0), (ov_ref, gv_ref, 1)):
        total = own_ref[...]
        total += mm(mat(covers + 4 * which == line, weight), r_ref[:, 0:WIDTH])
        total += mm(mat((row3 >> 3) + 16 * which == col3, 2.0**-3), r3_ref[...])
        both = mat((row4 >> 4) + 8 * which == col4, 2.0**-4)
        total += mm(both, r4a_ref[...]) + mm(both, r4b_ref[...])
        out_ref[...] = total.astype(BF16)
    slopes = r_ref[:, WIDTH:].astype(F32).reshape(PEERS, HEADS, 128)
    value = jnp.sum(jnp.sum(slopes, axis=0), axis=1, keepdims=True)
    srow, scol = iota2(HEADS, 128)
    line = jnp.sum(jnp.where(srow == scol, value, 0.0), axis=0, keepdims=True)
    os_ref[...] = line[:, 0:HEADS]


def call(kernel, outs, ins, places=None, out_places=None, scratch=(), cost=1 << 20, alias=None, vmem=12):
    places = places or [pltpu.VMEM] * len(ins)
    out_places = out_places or [pltpu.VMEM] * len(outs)
    return pl.pallas_call(
        kernel,
        out_shape=[jax.ShapeDtypeStruct(s, t) for s, t in outs],
        in_specs=[pl.BlockSpec(memory_space=place) for place in places],
        out_specs=[pl.BlockSpec(memory_space=place) for place in out_places],
        scratch_shapes=list(scratch),
        input_output_aliases=alias or {},
        compiler_params=pltpu.CompilerParams(vmem_limit_bytes=vmem * 1024 * 1024),
        cost_estimate=pl.CostEstimate(flops=0, bytes_accessed=cost, transcendentals=0),
    )(*ins)


def swap(block, apart):
    return lax.ppermute(block, "seq", [(i, i ^ apart) for i in range(PEERS)])


def exchange(slots):
    width = slots.shape[-1]
    back = lax.all_to_all(slots.reshape(PEERS, 8, width), "seq", 0, 0)
    return back.reshape(PEERS * 8, width)


def per_device(queries, keys_in, values_in, cotangent, level_slope):
    q, k, v, c = queries[0], keys_in[0], values_in[0], cotangent[0]
    wide = WIDTH
    kv, l3, l4, slots = call(
        pool_kernel,
        [((STEP + 16, wide), BF16), ((32, wide), BF16), ((16, wide), BF16), ((PEERS, 8, wide), BF16)],
        (k, v, level_slope),
        [pl.ANY] * 3,
        scratch=[pltpu.SMEM((HEADS,), F32), pltpu.SemaphoreType.DMA((3,))],
        vmem=58,
    )
    far = exchange(slots)
    near3 = swap(l3, 1)
    near4a = swap(l4, 2)
    near4b = swap(l4, 3)
    qc, near = call(
        local_kernel,
        [((2 * TOKENS, wide), BF16), ((128, wide), F32)],
        (q, c, kv),
        [pl.ANY, pl.ANY, pltpu.VMEM],
        scratch=[pltpu.SemaphoreType.DMA((2,))],
        cost=LONG,
    )
    groups = lax.axis_size("dp")
    work, slopes = call(
        score_kernel,
        [((DSCORES + KEYS, wide), BF16), ((groups, HEADS, 128), F32)],
        (kv, qc, near, near3, near4a, near4b, far),
    )
    slopes = lax.all_to_all(slopes, "dp", 0, 0)
    dq, gk, gv, g3, g4a, g4b, slots = call(
        grad_kernel,
        [((TOKENS, wide), BF16), ((TOKENS, wide), F32), ((TOKENS, wide), F32), ((32, wide), BF16),
         ((16, wide), BF16), ((16, wide), BF16), ((PEERS * 8, wide + 128), BF16)],
        (kv, qc, work),
        scratch=[pltpu.VMEM((2 * FAR, wide), BF16)],
    )
    (slots,) = call(
        slope_kernel,
        [((PEERS * 8, wide + 128), BF16)],
        (slopes, slots),
        [pltpu.VMEM, pl.ANY],
        [pl.ANY],
        [pltpu.VMEM((PEERS * 8, 128), BF16), pltpu.SemaphoreType.DMA(())],
        alias={1: 0},
    )
    far = exchange(slots)
    near3 = swap(g3, 1)
    near4a = swap(g4a, 2)
    near4b = swap(g4b, 3)
    dk, dv, ds = call(
        final_kernel,
        [((TOKENS, wide), BF16), ((TOKENS, wide), BF16), ((1, HEADS), F32)],
        (gk, gv, near3, near4a, near4b, far),
    )
    return dq[None], dk[None], dv[None], ds.reshape(HEADS)


def solution(mesh):
    row = P("dp", "seq", None)
    return jax.shard_map(
        per_device,
        mesh=mesh,
        in_specs=(row, row, row, row, P()),
        out_specs=(row, row, row, P()),
        check_vma=False,
    )
```

time: 82.1 us -> 79.9 us (0.973)
  local copies, waits for them, and re-layouts: 5.9 us -> 3.27 us
  waiting for transfers between devices: 18.6 us -> 17.4 us
    unnamed x22 -> x24, local copies, waits for them, and re-layouts: 5.9 us -> 3.27 us
    pallas_call x5 -> x6, Pallas kernels: 9.17 us -> 9.8 us  [call(): pl.pallas_call(kernel, out_shape=[jax.ShapeDtypeStruct(s, t) for s, t in...]
  transfers between devices with their start and end apart: 9 -> 9, of which waited for: 6 -> 6; matrix products, arithmetic and copies ran while one was open for 0% -> 0% of each run, Pallas kernels for 3% -> 5%
where the time goes in v2:
time: 79.9 us; the launch traced here: 79.1 us
  starting transfers between devices  47.8 us (60%)
  waiting for transfers between devices  17.4 us (22%)
  Pallas kernels  9.8 us (12%)
  local copies, waits for them, and re-layouts  3.27 us (4%)
  between operations  0.86 us (1%)
    all_to_all x2, starting transfers between devices, exchange(): back = lax.all_to_all(slots.reshape(PEERS, 8, width), 'seq', 0, 0)  19.3 us
    ppermute x6, starting transfers between devices, swap(): return lax.ppermute(block, 'seq', [(i, i ^ apart) for i in range(PEERS)])  18.9 us
    pallas_call x6, Pallas kernels, call(): pl.pallas_call(kernel, out_shape=[jax.ShapeDtypeStruct(s, t) for s, t in...  9.8 us
    all_to_all x1, starting transfers between devices, per_device(): slopes = lax.all_to_all(slopes, 'dp', 0, 0)  9.5 us
    ppermute x6, waiting for transfers between devices, swap(): return lax.ppermute(block, 'seq', [(i, i ^ apart) for i in range(PEERS)])  7.9 us
    all_to_all x2, waiting for transfers between devices, exchange(): back = lax.all_to_all(slots.reshape(PEERS, 8, width), 'seq', 0, 0)  5.88 us
    all_to_all x1, waiting for transfers between devices, per_device(): slopes = lax.all_to_all(slopes, 'dp', 0, 0)  3.64 us
    unnamed x24, local copies, waits for them, and re-layouts  3.27 us
  transfers between devices with their start and end apart: 9, of which 6 were waited for; matrix products, arithmetic and copies ran while one was open for 0% of the time, Pallas kernels for 5%

profile of v2, /device:TPU:1, one launch (start us, length us, event | category | flops | bytes accessed | tf_op | source)
XLA Modules:
  0.0 79.1 jit_solution(11793083727608267736)
XLA Ops:
  0.7 3.1 %shard_map.84 = (bf16[464,1024]{1,0:T(8,128)(2,1)}, bf16[32,1024]{1,0:T(8,128)(2,1)}, bf16[16,1024]{1,0:T(8,128)(2,1)}, bf16[32,8,1024]{2,1,0:T(8,128)(2,1)}) custom-call(bf16[128,1024]{1,0:T(8,128)(2,1)} %bitcast.15, bf16[128,1024]{1,0:T(8,128)(2,1)} %bitcast.16, f32[8]{0:T(128)} %slope_hbm.1), custom_call_target="tpu_custom_call" | custom-call | bytes 1048576 | tf_op jit(solution)/shard_map/pallas_call | solution.py:287
  3.7 0.0 copy-start.10
  3.8 0.0 copy-start.11
  3.8 13.9 %all-to-all-start = ((bf16[32,8,1024]{2,1,0:T(8,128)(2,1)}), bf16[32,8,1024]{2,1,0:T(8,128)(2,1)S(1)}, u32[]{:S(2)}, u32[]{:S(2)}) async-start(bf16[32,8,1024]{2,1,0:T(8,128)(2,1)} %get-tuple-element.27), calls=%async_computation | async-start | bytes 1048576 | tf_op jit(solution)/shard_map/all_to_all | solution.py:305
  17.6 3.1 %collective-permute-start = (bf16[32,1024]{1,0:T(8,128)(2,1)S(1)}, bf16[32,1024]{1,0:T(8,128)(2,1)S(1)}, u32[]{:S(2)}, u32[]{:S(2)}) collective-permute-start(bf16[32,1024]{1,0:T(8,128)(2,1)S(1)} %copy-done.10), channel_id=1, source_target_pairs={{0,1},{1,0},{2,3},{3,2},{4,5},{5,4},{6,7},{7,6},{8,9},{9,8},{10,11... | collective-permute-start | bytes 196616 | tf_op jit(solution)/shard_map/ppermute | solution.py:300
  20.8 3.7 %collective-permute-start.2 = (bf16[16,1024]{1,0:T(8,128)(2,1)S(1)}, bf16[16,1024]{1,0:T(8,128)(2,1)S(1)}, u32[]{:S(2)}, u32[]{:S(2)}) collective-permute-start(bf16[16,1024]{1,0:T(8,128)(2,1)S(1)} %copy-done.11), channel_id=1, source_target_pairs={{0,3},{1,2},{2,1},{3,0},{4,7},{5,6},{6,5},{7,4},{8,11},{9,10},{10,... | collective-permute-start | bytes 98312 | tf_op jit(solution)/shard_map/ppermute | solution.py:300
  24.5 2.5 %collective-permute-start.1 = (bf16[16,1024]{1,0:T(8,128)(2,1)S(1)}, bf16[16,1024]{1,0:T(8,128)(2,1)S(1)}, u32[]{:S(2)}, u32[]{:S(2)}) collective-permute-start(bf16[16,1024]{1,0:T(8,128)(2,1)S(1)} %copy-done.11), channel_id=1, source_target_pairs={{0,2},{1,3},{2,0},{3,1},{4,6},{5,7},{6,4},{7,5},{8,10},{9,11},{10,... | collective-permute-start | bytes 98312 | tf_op jit(solution)/shard_map/ppermute | solution.py:300
  27.1 0.7 shard_map.85
  27.8 0.0 collective-permute-done.2.r4b_ref
  27.8 3.4 %collective-permute-done.1.r4a_ref = bf16[16,1024]{1,0:T(8,128)(2,1)S(1)} collective-permute-done((bf16[16,1024]{1,0:T(8,128)(2,1)S(1)}, bf16[16,1024]{1,0:T(8,128)(2,1)S(1)}, u32[]{:S(2)}, u32[]{:S(2)}) %collective-permute-start.1) | collective-permute-done | bytes 32800 | tf_op jit(solution)/shard_map/ppermute | solution.py:300
  31.1 0.6 copy-done.4
  31.8 0.0 collective-permute-done.r3_ref
  31.8 2.2 %all-to-all-done = bf16[32,8,1024]{2,1,0:T(8,128)(2,1)S(1)} async-done(((bf16[32,8,1024]{2,1,0:T(8,128)(2,1)}), bf16[32,8,1024]{2,1,0:T(8,128)(2,1)S(1)}, u32[]{:S(2)}, u32[]{:S(2)}) %all-to-all-start) | async-done | bytes 524320 | tf_op jit(solution)/shard_map/all_to_all | solution.py:305
  33.9 0.8 copy-done.5
  34.7 1.0 %shard_map.86 = (bf16[448,1024]{1,0:T(8,128)(2,1)S(1)}, f32[16,8,128]{2,1,0:T(8,128)S(1)}) custom-call(bf16[464,1024]{1,0:T(8,128)(2,1)S(1)} %copy-done, bf16[256,1024]{1,0:T(8,128)(2,1)S(1)} %get-tuple-element.23.qc_ref, f32[128,1024]{1,0:T(8,128)S(1)} %get-tuple-element.24.near_ref, bf16[32,1024]{1,0:T(8,128)(2,1)S(1)} %collective-permute-done.r3_ref, ...), custom_call_target="tpu_custom_call" | custom-call | bytes 1048576 | tf_op jit(solution)/shard_map/pallas_call | solution.py:287
  35.6 0.0 copy-start.3
  35.7 0.6 copy-done.3
  36.3 9.5 %all-to-all-start.1 = ((f32[16,8,128]{2,1,0:T(8,128)}), f32[16,8,128]{2,1,0:T(8,128)S(1)}, u32[]{:S(2)}, u32[]{:S(2)}) async-start(f32[16,8,128]{2,1,0:T(8,128)} %copy-done.3), calls=%async_computation.1 | async-start | bytes 131072 | tf_op jit(solution)/shard_map/all_to_all | solution.py:338
  45.8 2.9 %shard_map.87 = (bf16[128,1024]{1,0:T(8,128)(2,1)}, f32[128,1024]{1,0:T(8,128)S(1)}, f32[128,1024]{1,0:T(8,128)S(1)}, bf16[32,1024]{1,0:T(8,128)(2,1)S(1)}, bf16...) custom-call(bf16[464,1024]{1,0:T(8,128)(2,1)S(1)} %copy-done, ...), custom_call_target="tpu_custom_call" | custom-call | bytes 1048576 | tf_op jit(solution)/shard_map/pallas_call | solution.py:287
  48.7 0.6 copy-done.6
  49.3 0.6 copy-done.8
  49.9 3.6 %all-to-all-done.1.s_ref = f32[16,8,128]{2,1,0:T(8,128)S(1)} async-done(((f32[16,8,128]{2,1,0:T(8,128)}), f32[16,8,128]{2,1,0:T(8,128)S(1)}, u32[]{:S(2)}, u32[]{:S(2)}) %all-to-all-start.1) | async-done | bytes 65568 | tf_op jit(solution)/shard_map/all_to_all | solution.py:338
  53.6 0.8 shard_map.88
  54.3 0.0 copy-start.7
  54.4 5.5 %all-to-all-start.2 = ((bf16[32,8,1152]{2,1,0:T(8,128)(2,1)}), bf16[32,8,1152]{2,1,0:T(8,128)(2,1)S(1)}, u32[]{:S(2)}, u32[]{:S(2)}) async-start(bf16[32,8,1152]{2,1,0:T(8,128)(2,1)} %bitcast.6), calls=%async_computation.2 | async-start | bytes 1179648 | tf_op jit(solution)/shard_map/all_to_all | solution.py:305
  59.8 3.1 %collective-permute-start.3 = (bf16[32,1024]{1,0:T(8,128)(2,1)S(1)}, bf16[32,1024]{1,0:T(8,128)(2,1)S(1)}, u32[]{:S(2)}, u32[]{:S(2)}) collective-permute-start(bf16[32,1024]{1,0:T(8,128)(2,1)S(1)} %copy-done.7), channel_id=1, source_target_pairs={{0,1},{1,0},{2,3},{3,2},{4,5},{5,4},{6,7},{7,6},{8,9},{9,8},{10,11... | collective-permute-start | bytes 196616 | tf_op jit(solution)/shard_map/ppermute | solution.py:300
  63.0 4.3 %collective-permute-start.4 = (bf16[16,1024]{1,0:T(8,128)(2,1)S(1)}, bf16[16,1024]{1,0:T(8,128)(2,1)S(1)}, u32[]{:S(2)}, u32[]{:S(2)}) collective-permute-start(bf16[16,1024]{1,0:T(8,128)(2,1)S(1)} %copy-done.9), channel_id=1, source_target_pairs={{0,2},{1,3},{2,0},{3,1},{4,6},{5,7},{6,4},{7,5},{8,10},{9,11},{10,... | collective-permute-start | bytes 98312 | tf_op jit(solution)/shard_map/ppermute | solution.py:300
  67.3 2.1 %collective-permute-start.5 = (bf16[16,1024]{1,0:T(8,128)(2,1)S(1)}, bf16[16,1024]{1,0:T(8,128)(2,1)S(1)}, u32[]{:S(2)}, u32[]{:S(2)}) collective-permute-start(bf16[16,1024]{1,0:T(8,128)(2,1)S(1)} %get-tuple-element.34), channel_id=1, source_target_pairs={{0,3},{1,2},{2,1},{3,0},{4,7},{5,6},{6,5},{7,4},{8,11},{9,10},{10,... | collective-permute-start | bytes 98312 | tf_op jit(solution)/shard_map/ppermute | solution.py:300
  69.5 0.4 collective-permute-done.4.r4a_ref
  69.9 4.1 %collective-permute-done.5.r4b_ref = bf16[16,1024]{1,0:T(8,128)(2,1)S(1)} collective-permute-done((bf16[16,1024]{1,0:T(8,128)(2,1)S(1)}, bf16[16,1024]{1,0:T(8,128)(2,1)S(1)}, u32[]{:S(2)}, u32[]{:S(2)}) %collective-permute-start.5) | collective-permute-done | bytes 32800 | tf_op jit(solution)/shard_map/ppermute | solution.py:300
  74.0 3.7 %all-to-all-done.2 = bf16[32,8,1152]{2,1,0:T(8,128)(2,1)S(1)} async-done(((bf16[32,8,1152]{2,1,0:T(8,128)(2,1)}), bf16[32,8,1152]{2,1,0:T(8,128)(2,1)S(1)}, u32[]{:S(2)}, u32[]{:S(2)}) %all-to-all-start.2) | async-done | bytes 589856 | tf_op jit(solution)/shard_map/all_to_all | solution.py:305
  77.7 1.4 %shard_map.89 = (bf16[128,1024]{1,0:T(8,128)(2,1)}, bf16[128,1024]{1,0:T(8,128)(2,1)}, f32[1,8]{1,0:T(1,128)}) custom-call(f32[128,1024]{1,0:T(8,128)S(1)} %get-tuple-element.30.gk_ref, f32[128,1024]{1,0:T(8,128)S(1)} %get-tuple-element.31.gv_ref, bf16[32,1024]{1,0:T(8,128)(2,1)S(1)} %collective-permute-done.3.r3_ref, ...), custom_call_target="tpu_custom_call" | custom-call | bytes 1048576 | tf_op jit(solution)/shard_map/pallas_call | solution.py:287
  (16 shorter events, 0.0 us)
Async XLA Ops:
  0.6 26.4 %copy-start.1 = (bf16[1,128,1024]{2,1,0:T(8,128)(2,1)S(1)}, bf16[1,128,1024]{2,1,0:T(8,128)(2,1)}, u32[]{:S(2)}) copy-start(bf16[1,128,1024]{2,1,0:T(8,128)(2,1)} %param.5) | copy-start | bytes 786436
  0.6 26.4 %copy-start.2 = (bf16[1,128,1024]{2,1,0:T(8,128)(2,1)S(1)}, bf16[1,128,1024]{2,1,0:T(8,128)(2,1)}, u32[]{:S(2)}) copy-start(bf16[1,128,1024]{2,1,0:T(8,128)(2,1)} %param.8) | copy-start | bytes 786436
  3.7 23.3 %copy-start = (bf16[464,1024]{1,0:T(8,128)(2,1)S(1)}, bf16[464,1024]{1,0:T(8,128)(2,1)}, u32[]{:S(2)}) copy-start(bf16[464,1024]{1,0:T(8,128)(2,1)} %get-tuple-element.22.kv_ref) | copy-start | bytes 2850820
  3.7 13.9 %copy-start.10 = (bf16[32,1024]{1,0:T(8,128)(2,1)S(1)}, bf16[32,1024]{1,0:T(8,128)(2,1)}, u32[]{:S(2)}) copy-start(bf16[32,1024]{1,0:T(8,128)(2,1)} %get-tuple-element.25) | copy-start | bytes 196612
  3.8 17.0 %copy-start.11 = (bf16[16,1024]{1,0:T(8,128)(2,1)S(1)}, bf16[16,1024]{1,0:T(8,128)(2,1)}, u32[]{:S(2)}) copy-start(bf16[16,1024]{1,0:T(8,128)(2,1)} %get-tuple-element.26) | copy-start | bytes 98308
  3.8 30.1 %all-to-all-start = ((bf16[32,8,1024]{2,1,0:T(8,128)(2,1)}), bf16[32,8,1024]{2,1,0:T(8,128)(2,1)S(1)}, u32[]{:S(2)}, u32[]{:S(2)}) async-start(bf16[32,8,1024]{2,1,0:T(8,128)(2,1)} %get-tuple-element.27), calls=%async_computation | async-start | bytes 1048576 | tf_op jit(solution)/shard_map/all_to_all | solution.py:305
  17.6 14.1 %collective-permute-start = (bf16[32,1024]{1,0:T(8,128)(2,1)S(1)}, bf16[32,1024]{1,0:T(8,128)(2,1)S(1)}, u32[]{:S(2)}, u32[]{:S(2)}) collective-permute-start(bf16[32,1024]{1,0:T(8,128)(2,1)S(1)} %copy-done.10), channel_id=1, source_target_pairs={{0,1},{1,0},{2,3},{3,2},{4,5},{5,4},{6,7},{7,6},{8,9},{9,8},{10,11... | collective-permute-start | bytes 196616 | tf_op jit(solution)/shard_map/ppermute | solution.py:300
  20.8 7.0 %collective-permute-start.2 = (bf16[16,1024]{1,0:T(8,128)(2,1)S(1)}, bf16[16,1024]{1,0:T(8,128)(2,1)S(1)}, u32[]{:S(2)}, u32[]{:S(2)}) collective-permute-start(bf16[16,1024]{1,0:T(8,128)(2,1)S(1)} %copy-done.11), channel_id=1, source_target_pairs={{0,3},{1,2},{2,1},{3,0},{4,7},{5,6},{6,5},{7,4},{8,11},{9,10},{10,... | collective-permute-start | bytes 98312 | tf_op jit(solution)/shard_map/ppermute | solution.py:300
  24.5 6.6 %collective-permute-start.1 = (bf16[16,1024]{1,0:T(8,128)(2,1)S(1)}, bf16[16,1024]{1,0:T(8,128)(2,1)S(1)}, u32[]{:S(2)}, u32[]{:S(2)}) collective-permute-start(bf16[16,1024]{1,0:T(8,128)(2,1)S(1)} %copy-done.11), channel_id=1, source_target_pairs={{0,2},{1,3},{2,0},{3,1},{4,6},{5,7},{6,4},{7,5},{8,10},{9,11},{10,... | collective-permute-start | bytes 98312 | tf_op jit(solution)/shard_map/ppermute | solution.py:300
  31.1 0.6 copy-start.4
  33.9 0.8 copy-start.5
  35.6 0.6 copy-start.3
  36.3 17.3 %all-to-all-start.1 = ((f32[16,8,128]{2,1,0:T(8,128)}), f32[16,8,128]{2,1,0:T(8,128)S(1)}, u32[]{:S(2)}, u32[]{:S(2)}) async-start(f32[16,8,128]{2,1,0:T(8,128)} %copy-done.3), calls=%async_computation.1 | async-start | bytes 131072 | tf_op jit(solution)/shard_map/all_to_all | solution.py:338
  48.7 0.6 copy-start.6
  49.3 0.6 copy-start.8
  54.3 5.5 %copy-start.7 = (bf16[32,1024]{1,0:T(8,128)(2,1)S(1)}, bf16[32,1024]{1,0:T(8,128)(2,1)}, u32[]{:S(2)}) copy-start(bf16[32,1024]{1,0:T(8,128)(2,1)} %copy-done.6) | copy-start | bytes 196612
  54.4 8.6 %copy-start.9 = (bf16[16,1024]{1,0:T(8,128)(2,1)S(1)}, bf16[16,1024]{1,0:T(8,128)(2,1)}, u32[]{:S(2)}) copy-start(bf16[16,1024]{1,0:T(8,128)(2,1)} %copy-done.8) | copy-start | bytes 98308
  54.4 23.3 %all-to-all-start.2 = ((bf16[32,8,1152]{2,1,0:T(8,128)(2,1)}), bf16[32,8,1152]{2,1,0:T(8,128)(2,1)S(1)}, u32[]{:S(2)}, u32[]{:S(2)}) async-start(bf16[32,8,1152]{2,1,0:T(8,128)(2,1)} %bitcast.6), calls=%async_computation.2 | async-start | bytes 1179648 | tf_op jit(solution)/shard_map/all_to_all | solution.py:305
  59.8 14.1 %collective-permute-start.3 = (bf16[32,1024]{1,0:T(8,128)(2,1)S(1)}, bf16[32,1024]{1,0:T(8,128)(2,1)S(1)}, u32[]{:S(2)}, u32[]{:S(2)}) collective-permute-start(bf16[32,1024]{1,0:T(8,128)(2,1)S(1)} %copy-done.7), channel_id=1, source_target_pairs={{0,1},{1,0},{2,3},{3,2},{4,5},{5,4},{6,7},{7,6},{8,9},{9,8},{10,11... | collective-permute-start | bytes 196616 | tf_op jit(solution)/shard_map/ppermute | solution.py:300
  63.0 6.9 %collective-permute-start.4 = (bf16[16,1024]{1,0:T(8,128)(2,1)S(1)}, bf16[16,1024]{1,0:T(8,128)(2,1)S(1)}, u32[]{:S(2)}, u32[]{:S(2)}) collective-permute-start(bf16[16,1024]{1,0:T(8,128)(2,1)S(1)} %copy-done.9), channel_id=1, source_target_pairs={{0,2},{1,3},{2,0},{3,1},{4,6},{5,7},{6,4},{7,5},{8,10},{9,11},{10,... | collective-permute-start | bytes 98312 | tf_op jit(solution)/shard_map/ppermute | solution.py:300
  67.3 6.7 %collective-permute-start.5 = (bf16[16,1024]{1,0:T(8,128)(2,1)S(1)}, bf16[16,1024]{1,0:T(8,128)(2,1)S(1)}, u32[]{:S(2)}, u32[]{:S(2)}) collective-permute-start(bf16[16,1024]{1,0:T(8,128)(2,1)S(1)} %get-tuple-element.34), channel_id=1, source_target_pairs={{0,3},{1,2},{2,1},{3,0},{4,7},{5,6},{6,5},{7,4},{8,11},{9,10},{10,... | collective-permute-start | bytes 98312 | tf_op jit(solution)/shard_map/ppermute | solution.py:300

commit v3 on v2

--- a/solution.py
+++ b/solution.py
@@ -49,16 +49,22 @@
 
 
 LOCAL = 224
-STEP = 2 * LOCAL
+COARSE = 96
+STEP = 2 * COARSE
 REMOTE = 80
 PROBS = 2 * REMOTE
 DSCORES = PROBS + KEYS
-
-
-def pool_kernel(k_hbm, v_hbm, slope_hbm, kv_ref, l3_ref, l4_ref, slot_ref, slope_ref, sems):
+QUERY = LOCAL
+COTANGENT = LOCAL + TOKENS
+STEPS = LOCAL + 2 * TOKENS
+
+
+def pool_kernel(
+    k_hbm, v_hbm, slope_hbm, low_ref, l3_ref, l4_ref, slot_ref, k_ref, v_ref, slope_ref, sems
+):
     me = lax.axis_index("seq")
-    fetch_k = pltpu.make_async_copy(k_hbm, kv_ref.at[pl.ds(0, TOKENS)], sems.at[0])
-    fetch_v = pltpu.make_async_copy(v_hbm, kv_ref.at[pl.ds(LOCAL, TOKENS)], sems.at[1])
+    fetch_k = pltpu.make_async_copy(k_hbm, k_ref, sems.at[0])
+    fetch_v = pltpu.make_async_copy(v_hbm, v_ref, sems.at[1])
     fetch_slope = pltpu.make_async_copy(slope_hbm, slope_ref, sems.at[2])
     fetch_k.start()
     fetch_v.start()
@@ -70,14 +76,14 @@
     for h in range(HEADS):
         high, middle, low = three_parts(jnp.full((16, HEAD_DIM), LOG_TWO + slope_ref[h], F32))
         part = jnp.where(line == 0, high, jnp.where(line == 1, middle, jnp.where(line == 2, low, 0.0)))
-        kv_ref[STEP : STEP + 16, h * HEAD_DIM : (h + 1) * HEAD_DIM] = part.astype(BF16)
+        low_ref[STEP : STEP + 16, h * HEAD_DIM : (h + 1) * HEAD_DIM] = part.astype(BF16)
     l2 = []
-    for fetch, at in ((fetch_k, 0), (fetch_v, LOCAL)):
+    for fetch, held, at in ((fetch_k, k_ref, 0), (fetch_v, v_ref, COARSE)):
         fetch.wait()
-        one = mm(half, kv_ref[at : at + 128, :]).astype(BF16)
-        kv_ref[at + 128 : at + 192, :] = one
+        one = mm(half, held[...]).astype(BF16)
+        low_ref[at : at + 64, :] = one
         two = mm(quarter, one).astype(BF16)
-        kv_ref[at + 192 : at + 224, :] = two
+        low_ref[at + 64 : at + 96, :] = two
         l2.append(two)
     l3 = mm(quarter, jnp.concatenate(l2, axis=0)).astype(BF16)
     l3_ref[...] = l3
@@ -112,11 +118,19 @@
     return jnp.where(line < 16, at5, jnp.where(line < 32, at6, at7))
 
 
-def local_kernel(q_hbm, c_hbm, kv_ref, qc_ref, s_ref, sems):
-    fetch_q = pltpu.make_async_copy(q_hbm, qc_ref.at[pl.ds(0, TOKENS)], sems.at[0])
-    fetch_c = pltpu.make_async_copy(c_hbm, qc_ref.at[pl.ds(TOKENS, TOKENS)], sems.at[1])
-    fetch_q.start()
-    fetch_c.start()
+def local_kernel(q_hbm, c_hbm, k_hbm, v_hbm, low_ref, loc_ref, s_ref, v_ref, sems):
+    moves = (
+        (k_hbm, loc_ref.at[pl.ds(0, TOKENS)]),
+        (q_hbm, loc_ref.at[pl.ds(QUERY, TOKENS)]),
+        (v_hbm, v_ref.at[pl.ds(0, TOKENS)]),
+        (c_hbm, loc_ref.at[pl.ds(COTANGENT, TOKENS)]),
+    )
+    fetches = [pltpu.make_async_copy(a, b, sems.at[i]) for i, (a, b) in enumerate(moves)]
+    for fetch in fetches:
+        fetch.start()
+    loc_ref[TOKENS:LOCAL, :] = low_ref[0:COARSE, :]
+    v_ref[TOKENS:LOCAL, :] = low_ref[COARSE : 2 * COARSE, :]
+    loc_ref[STEPS : STEPS + 16, :] = low_ref[STEP : STEP + 16, :]
     lane = lax.broadcasted_iota(jnp.int32, (1, TOKENS), 1)
     quarter = lane >> 5
     lower = lane < 64
@@ -135,13 +149,13 @@
         two = jnp.where(lower, full[208:224], full[192:208])
         return zero, one, two
 
-    step_all = jnp.sum(kv_ref[STEP : STEP + 16, :].astype(F32), axis=0, keepdims=True)
-    for which, fetch in enumerate((fetch_q, fetch_c)):
-        fetch.wait()
+    step_all = jnp.sum(low_ref[STEP : STEP + 16, :].astype(F32), axis=0, keepdims=True)
+    for which, (held, at) in enumerate(((loc_ref, QUERY), (v_ref, COTANGENT))):
+        fetches[2 * which].wait()
+        fetches[2 * which + 1].wait()
         for h in range(HEADS):
             sl = slice(h * HEAD_DIM, (h + 1) * HEAD_DIM)
-            keys = kv_ref[LOCAL * which : LOCAL * which + LOCAL, sl]
-            raw = mm(keys, qc_ref[TOKENS * which : TOKENS * which + TOKENS, sl], ((1,), (1,)))
+            raw = mm(held[0:LOCAL, sl], loc_ref[at : at + TOKENS, sl], ((1,), (1,)))
             zero, one, two = compact(raw)
             if which == 0:
                 step = step_all[:, sl]
@@ -149,7 +163,7 @@
             s_ref[64 * which : 64 * which + 64, sl] = jnp.concatenate([zero, one, two], axis=0)
 
 
-def score_kernel(kv_ref, qc_ref, near_ref, r3_ref, r4a_ref, r4b_ref, r_ref, w_ref, s_ref):
+def score_kernel(loc_ref, near_ref, r3_ref, r4a_ref, r4b_ref, r_ref, w_ref, s_ref):
     me = lax.axis_index("seq")
     row, col = iota2(FAR, PEERS * 8)
     place = far_column(me, row)
@@ -163,11 +177,11 @@
         four = mm(first, r4a_ref[...]) + mm(second, r4b_ref[...])
         w_ref[at + 16 : at + 32, :] = four.astype(BF16)
         w_ref[at + 32 : at + 80, :] = mm(mat(col == place + 4 * which, 1.0), far).astype(BF16)
-    step_all = jnp.sum(kv_ref[STEP : STEP + 16, :].astype(F32), axis=0, keepdims=True)
+    step_all = jnp.sum(loc_ref[STEPS : STEPS + 16, :].astype(F32), axis=0, keepdims=True)
     total = [None] * HEADS
     for h in range(HEADS):
         sl = slice(h * HEAD_DIM, (h + 1) * HEAD_DIM)
-        raw = mm(w_ref[0:REMOTE, sl], qc_ref[0:TOKENS, sl], ((1,), (1,)))
+        raw = mm(w_ref[0:REMOTE, sl], loc_ref[QUERY : QUERY + TOKENS, sl], ((1,), (1,)))
         step = step_all[:, sl]
         parts = [near_ref[0:64, sl]]
         parts += [raw[16 * i : 16 * i + 16] * SCALE + (i + 3) * step for i in range(5)]
@@ -176,7 +190,7 @@
         expo = jnp.exp(scores - top)
         probs = expo * (1.0 / jnp.sum(expo, axis=0, keepdims=True))
         probs_b = probs.astype(BF16)
-        raw = mm(w_ref[REMOTE : 2 * REMOTE, sl], qc_ref[TOKENS : 2 * TOKENS, sl], ((1,), (1,)))
+        raw = mm(w_ref[REMOTE : 2 * REMOTE, sl], loc_ref[COTANGENT : COTANGENT + TOKENS, sl], ((1,), (1,)))
         dprobs = jnp.concatenate([near_ref[64:128, sl], raw], axis=0)
         delta = jnp.sum(probs_b.astype(F32) * dprobs, axis=0, keepdims=True)
         dscores = probs * (dprobs - delta)
@@ -193,7 +207,7 @@
         s_ref[i] = tile
 
 
-def grad_kernel(kv_ref, qc_ref, w_ref, dq_ref, gk_ref, gv_ref, g3_ref, g4a_ref, g4b_ref, slot_ref, gf_ref):
+def grad_kernel(loc_ref, w_ref, dq_ref, gk_ref, gv_ref, g3_ref, g4a_ref, g4b_ref, slot_ref, gf_ref):
     me = lax.axis_index("seq")
     lane = lax.broadcasted_iota(jnp.int32, (1, TOKENS), 1)
     quarter = lane >> 5
@@ -216,12 +230,12 @@
 
     for h in range(HEADS):
         sl = slice(h * HEAD_DIM, (h + 1) * HEAD_DIM)
-        q, c = qc_ref[0:TOKENS, sl], qc_ref[TOKENS : 2 * TOKENS, sl]
+        q, c = loc_ref[QUERY : QUERY + TOKENS, sl], loc_ref[COTANGENT : COTANGENT + TOKENS, sl]
         d_near = expand(w_ref[DSCORES : DSCORES + 64, sl])
         p_near = expand(w_ref[PROBS : PROBS + 64, sl])
         d_far = w_ref[DSCORES + 64 : DSCORES + KEYS, sl]
         p_far = w_ref[PROBS + 64 : PROBS + KEYS, sl]
-        dq = mm(d_near, kv_ref[0:LOCAL, sl], ((0,), (0,))) + mm(d_far, w_ref[0:REMOTE, sl], ((0,), (0,)))
+        dq = mm(d_near, loc_ref[0:LOCAL, sl], ((0,), (0,))) + mm(d_far, w_ref[0:REMOTE, sl], ((0,), (0,)))
         dq_ref[:, sl] = (dq * SCALE).astype(BF16)
         dk = mm(d_near, q) * SCALE
         dv = mm(p_near, c)
@@ -309,38 +323,39 @@
 def per_device(queries, keys_in, values_in, cotangent, level_slope):
     q, k, v, c = queries[0], keys_in[0], values_in[0], cotangent[0]
     wide = WIDTH
-    kv, l3, l4, slots = call(
+    block = pltpu.VMEM((TOKENS, wide), BF16)
+    low, l3, l4, slots = call(
         pool_kernel,
         [((STEP + 16, wide), BF16), ((32, wide), BF16), ((16, wide), BF16), ((PEERS, 8, wide), BF16)],
         (k, v, level_slope),
         [pl.ANY] * 3,
-        scratch=[pltpu.SMEM((HEADS,), F32), pltpu.SemaphoreType.DMA((3,))],
+        scratch=[block, block, pltpu.SMEM((HEADS,), F32), pltpu.SemaphoreType.DMA((3,))],
         vmem=58,
     )
     far = exchange(slots)
     near3 = swap(l3, 1)
     near4a = swap(l4, 2)
     near4b = swap(l4, 3)
-    qc, near = call(
+    loc, near = call(
         local_kernel,
-        [((2 * TOKENS, wide), BF16), ((128, wide), F32)],
-        (q, c, kv),
-        [pl.ANY, pl.ANY, pltpu.VMEM],
-        scratch=[pltpu.SemaphoreType.DMA((2,))],
+        [((STEPS + 16, wide), BF16), ((128, wide), F32)],
+        (q, c, k, v, low),
+        [pl.ANY] * 4 + [pltpu.VMEM],
+        scratch=[pltpu.VMEM((LOCAL, wide), BF16), pltpu.SemaphoreType.DMA((4,))],
         cost=LONG,
     )
     groups = lax.axis_size("dp")
     work, slopes = call(
         score_kernel,
         [((DSCORES + KEYS, wide), BF16), ((groups, HEADS, 128), F32)],
-        (kv, qc, near, near3, near4a, near4b, far),
+        (loc, near, near3, near4a, near4b, far),
     )
     slopes = lax.all_to_all(slopes, "dp", 0, 0)
     dq, gk, gv, g3, g4a, g4b, slots = call(
         grad_kernel,
         [((TOKENS, wide), BF16), ((TOKENS, wide), F32), ((TOKENS, wide), F32), ((32, wide), BF16),
          ((16, wide), BF16), ((16, wide), BF16), ((PEERS * 8, wide + 128), BF16)],
-        (kv, qc, work),
+        (loc, work),
         scratch=[pltpu.VMEM((2 * FAR, wide), BF16)],
     )
     (slots,) = call(

time: 79.9 us -> 78.3 us (0.980)
  local copies, waits for them, and re-layouts: 3.27 us -> 0.98 us
  waiting for transfers between devices: 17.4 us -> 18.3 us
  starting transfers between devices: 47.8 us -> 47 us
    unnamed x24 -> x14, local copies, waits for them, and re-layouts: 3.27 us -> 0.98 us
    all_to_all x1, waiting for transfers between devices: 3.64 us -> 4.89 us  [per_device(): slopes = lax.all_to_all(slopes, 'dp', 0, 0)]
    ppermute x6, waiting for transfers between devices: 7.9 us -> 6.86 us  [swap(): return lax.ppermute(block, 'seq', [(i, i ^ apart) for i in range(PEERS)])]
where the time goes in v3:
time: 78.3 us; the launch traced here: 77.6 us
  starting transfers between devices  47 us (60%)
  waiting for transfers between devices  18.3 us (23%)
  Pallas kernels  10.5 us (13%)
  local copies, waits for them, and re-layouts  0.98 us (1%)
  between operations  0.83 us (1%)
    ppermute x6, starting transfers between devices, swap(): return lax.ppermute(block, 'seq', [(i, i ^ apart) for i in range(PEERS)])  18.9 us
    all_to_all x2, starting transfers between devices, exchange(): back = lax.all_to_all(slots.reshape(PEERS, 8, width), 'seq', 0, 0)  18.6 us
    pallas_call x6, Pallas kernels, call(): pl.pallas_call(kernel, out_shape=[jax.ShapeDtypeStruct(s, t) for s, t in...  10.5 us
    all_to_all x1, starting transfers between devices, per_device(): slopes = lax.all_to_all(slopes, 'dp', 0, 0)  9.51 us
    ppermute x6, waiting for transfers between devices, swap(): return lax.ppermute(block, 'seq', [(i, i ^ apart) for i in range(PEERS)])  6.86 us
    all_to_all x2, waiting for transfers between devices, exchange(): back = lax.all_to_all(slots.reshape(PEERS, 8, width), 'seq', 0, 0)  6.51 us
    all_to_all x1, waiting for transfers between devices, per_device(): slopes = lax.all_to_all(slopes, 'dp', 0, 0)  4.89 us
  transfers between devices with their start and end apart: 9, of which 6 were waited for; matrix products, arithmetic and copies ran while one was open for 0% of the time, Pallas kernels for 5%

profile of v3, /device:TPU:1, one launch (start us, length us, event | category | flops | bytes accessed | tf_op | source)
XLA Modules:
  0.0 77.6 jit_solution(3793527341010246922)
XLA Ops:
  0.6 0.0 copy-start.3
  0.6 3.1 %shard_map.84 = (bf16[208,1024]{1,0:T(8,128)(2,1)}, bf16[32,1024]{1,0:T(8,128)(2,1)}, bf16[16,1024]{1,0:T(8,128)(2,1)}, bf16[32,8,1024]{2,1,0:T(8,128)(2,1)}) custom-call(bf16[128,1024]{1,0:T(8,128)(2,1)} %bitcast.13, bf16[128,1024]{1,0:T(8,128)(2,1)} %bitcast.15, f32[8]{0:T(128)} %slope_hbm.1), custom_call_target="tpu_custom_call" | custom-call | bytes 1048576 | tf_op jit(solution)/shard_map/pallas_call | solution.py:301
  3.7 0.0 copy-start.5
  3.7 0.0 copy-start.6
  3.7 0.0 copy-start
  3.8 0.0 copy-start.1
  3.8 13.9 %all-to-all-start = ((bf16[32,8,1024]{2,1,0:T(8,128)(2,1)}), bf16[32,8,1024]{2,1,0:T(8,128)(2,1)S(1)}, u32[]{:S(2)}, u32[]{:S(2)}) async-start(bf16[32,8,1024]{2,1,0:T(8,128)(2,1)} %get-tuple-element.27), calls=%async_computation | async-start | bytes 1048576 | tf_op jit(solution)/shard_map/all_to_all | solution.py:319
  17.7 3.1 %collective-permute-start = (bf16[32,1024]{1,0:T(8,128)(2,1)S(1)}, bf16[32,1024]{1,0:T(8,128)(2,1)S(1)}, u32[]{:S(2)}, u32[]{:S(2)}) collective-permute-start(bf16[32,1024]{1,0:T(8,128)(2,1)S(1)} %copy-done.5), channel_id=1, source_target_pairs={{0,1},{1,0},{2,3},{3,2},{4,5},{5,4},{6,7},{7,6},{8,9},{9,8},{10,11... | collective-permute-start | bytes 196616 | tf_op jit(solution)/shard_map/ppermute | solution.py:314
  20.8 0.0 copy-done.6
  20.8 3.7 %collective-permute-start.2 = (bf16[16,1024]{1,0:T(8,128)(2,1)S(1)}, bf16[16,1024]{1,0:T(8,128)(2,1)S(1)}, u32[]{:S(2)}, u32[]{:S(2)}) collective-permute-start(bf16[16,1024]{1,0:T(8,128)(2,1)S(1)} %copy-done.6), channel_id=1, source_target_pairs={{0,3},{1,2},{2,1},{3,0},{4,7},{5,6},{6,5},{7,4},{8,11},{9,10},{10,... | collective-permute-start | bytes 98312 | tf_op jit(solution)/shard_map/ppermute | solution.py:314
  24.5 2.5 %collective-permute-start.1 = (bf16[16,1024]{1,0:T(8,128)(2,1)S(1)}, bf16[16,1024]{1,0:T(8,128)(2,1)S(1)}, u32[]{:S(2)}, u32[]{:S(2)}) collective-permute-start(bf16[16,1024]{1,0:T(8,128)(2,1)S(1)} %copy-done.6), channel_id=1, source_target_pairs={{0,2},{1,3},{2,0},{3,1},{4,6},{5,7},{6,4},{7,5},{8,10},{9,11},{10,... | collective-permute-start | bytes 98312 | tf_op jit(solution)/shard_map/ppermute | solution.py:314
  27.1 0.0 copy-start.4
  27.1 0.9 %copy-done.4 = bf16[1,128,1024]{2,1,0:T(8,128)(2,1)S(1)} copy-done((bf16[1,128,1024]{2,1,0:T(8,128)(2,1)S(1)}, bf16[1,128,1024]{2,1,0:T(8,128)(2,1)}, u32[]{:S(2)}) %copy-start.4) | copy-done | bytes 262168
  28.0 0.8 shard_map.85
  28.8 0.0 collective-permute-done.2.r4b_ref
  28.8 2.3 %collective-permute-done.1.r4a_ref = bf16[16,1024]{1,0:T(8,128)(2,1)S(1)} collective-permute-done((bf16[16,1024]{1,0:T(8,128)(2,1)S(1)}, bf16[16,1024]{1,0:T(8,128)(2,1)S(1)}, u32[]{:S(2)}, u32[]{:S(2)}) %collective-permute-start.1) | collective-permute-done | bytes 32800 | tf_op jit(solution)/shard_map/ppermute | solution.py:314
  31.2 0.0 collective-permute-done.r3_ref
  31.2 2.8 %all-to-all-done = bf16[32,8,1024]{2,1,0:T(8,128)(2,1)S(1)} async-done(((bf16[32,8,1024]{2,1,0:T(8,128)(2,1)}), bf16[32,8,1024]{2,1,0:T(8,128)(2,1)S(1)}, u32[]{:S(2)}, u32[]{:S(2)}) %all-to-all-start) | async-done | bytes 524320 | tf_op jit(solution)/shard_map/all_to_all | solution.py:319
  33.9 1.6 %shard_map.86 = (bf16[448,1024]{1,0:T(8,128)(2,1)S(1)}, f32[16,8,128]{2,1,0:T(8,128)}) custom-call(bf16[496,1024]{1,0:T(8,128)(2,1)S(1)} %get-tuple-element.23.loc_ref, f32[128,1024]{1,0:T(8,128)S(1)} %get-tuple-element.24.near_ref, bf16[32,1024]{1,0:T(8,128)(2,1)S(1)} %collective-permute-done.r3_ref, bf16[16,1024]{1,0:T(8,128)(2,1)S(1)} %collective-permute-done.1.r4a_ref, ...), custom_call_target="tpu_custom_call" | custom-call | bytes 1048576 | tf_op jit(solution)/shard_map/pallas_call | solution.py:301
  35.5 9.5 %all-to-all-start.1 = ((f32[16,8,128]{2,1,0:T(8,128)}), f32[16,8,128]{2,1,0:T(8,128)S(1)}, u32[]{:S(2)}, u32[]{:S(2)}) async-start(f32[16,8,128]{2,1,0:T(8,128)} %get-tuple-element.35), calls=%async_computation.1 | async-start | bytes 131072 | tf_op jit(solution)/shard_map/all_to_all | solution.py:353
  45.0 2.9 %shard_map.87 = (bf16[128,1024]{1,0:T(8,128)(2,1)}, f32[128,1024]{1,0:T(8,128)S(1)}, f32[128,1024]{1,0:T(8,128)S(1)}, bf16[32,1024]{1,0:T(8,128)(2,1)S(1)}, bf16...) custom-call(bf16[496,1024]{1,0:T(8,128)(2,1)S(1)} %get-tuple-element.23.loc_ref, ...), custom_call_target="tpu_custom_call" | custom-call | bytes 1048576 | tf_op jit(solution)/shard_map/pallas_call | solution.py:301
  47.9 4.9 %all-to-all-done.1.s_ref = f32[16,8,128]{2,1,0:T(8,128)S(1)} async-done(((f32[16,8,128]{2,1,0:T(8,128)}), f32[16,8,128]{2,1,0:T(8,128)S(1)}, u32[]{:S(2)}, u32[]{:S(2)}) %all-to-all-start.1) | async-done | bytes 65568 | tf_op jit(solution)/shard_map/all_to_all | solution.py:353
  52.8 0.7 shard_map.88
  53.6 4.7 %all-to-all-start.2 = ((bf16[32,8,1152]{2,1,0:T(8,128)(2,1)}), bf16[32,8,1152]{2,1,0:T(8,128)(2,1)S(1)}, u32[]{:S(2)}, u32[]{:S(2)}) async-start(bf16[32,8,1152]{2,1,0:T(8,128)(2,1)} %bitcast.6), calls=%async_computation.2 | async-start | bytes 1179648 | tf_op jit(solution)/shard_map/all_to_all | solution.py:319
  58.3 3.1 %collective-permute-start.3 = (bf16[32,1024]{1,0:T(8,128)(2,1)S(1)}, bf16[32,1024]{1,0:T(8,128)(2,1)S(1)}, u32[]{:S(2)}, u32[]{:S(2)}) collective-permute-start(bf16[32,1024]{1,0:T(8,128)(2,1)S(1)} %get-tuple-element.32), channel_id=1, source_target_pairs={{0,1},{1,0},{2,3},{3,2},{4,5},{5,4},{6,7},{7,6},{8,9},{9,8},{10,11... | collective-permute-start | bytes 196616 | tf_op jit(solution)/shard_map/ppermute | solution.py:314
  61.4 4.3 %collective-permute-start.4 = (bf16[16,1024]{1,0:T(8,128)(2,1)S(1)}, bf16[16,1024]{1,0:T(8,128)(2,1)S(1)}, u32[]{:S(2)}, u32[]{:S(2)}) collective-permute-start(bf16[16,1024]{1,0:T(8,128)(2,1)S(1)} %get-tuple-element.33), channel_id=1, source_target_pairs={{0,2},{1,3},{2,0},{3,1},{4,6},{5,7},{6,4},{7,5},{8,10},{9,11},{10,... | collective-permute-start | bytes 98312 | tf_op jit(solution)/shard_map/ppermute | solution.py:314
  65.8 2.1 %collective-permute-start.5 = (bf16[16,1024]{1,0:T(8,128)(2,1)S(1)}, bf16[16,1024]{1,0:T(8,128)(2,1)S(1)}, u32[]{:S(2)}, u32[]{:S(2)}) collective-permute-start(bf16[16,1024]{1,0:T(8,128)(2,1)S(1)} %get-tuple-element.34), channel_id=1, source_target_pairs={{0,3},{1,2},{2,1},{3,0},{4,7},{5,6},{6,5},{7,4},{8,11},{9,10},{10,... | collective-permute-start | bytes 98312 | tf_op jit(solution)/shard_map/ppermute | solution.py:314
  67.9 0.2 collective-permute-done.4.r4a_ref
  68.1 4.3 %collective-permute-done.5.r4b_ref = bf16[16,1024]{1,0:T(8,128)(2,1)S(1)} collective-permute-done((bf16[16,1024]{1,0:T(8,128)(2,1)S(1)}, bf16[16,1024]{1,0:T(8,128)(2,1)S(1)}, u32[]{:S(2)}, u32[]{:S(2)}) %collective-permute-start.5) | collective-permute-done | bytes 32800 | tf_op jit(solution)/shard_map/ppermute | solution.py:314
  72.4 0.0 collective-permute-done.3.r3_ref
  72.4 3.8 %all-to-all-done.2 = bf16[32,8,1152]{2,1,0:T(8,128)(2,1)S(1)} async-done(((bf16[32,8,1152]{2,1,0:T(8,128)(2,1)}), bf16[32,8,1152]{2,1,0:T(8,128)(2,1)S(1)}, u32[]{:S(2)}, u32[]{:S(2)}) %all-to-all-start.2) | async-done | bytes 589856 | tf_op jit(solution)/shard_map/all_to_all | solution.py:319
  76.2 1.4 %shard_map.89 = (bf16[128,1024]{1,0:T(8,128)(2,1)}, bf16[128,1024]{1,0:T(8,128)(2,1)}, f32[1,8]{1,0:T(1,128)}) custom-call(f32[128,1024]{1,0:T(8,128)S(1)} %get-tuple-element.30.gk_ref, f32[128,1024]{1,0:T(8,128)S(1)} %get-tuple-element.31.gv_ref, bf16[32,1024]{1,0:T(8,128)(2,1)S(1)} %collective-permute-done.3.r3_ref, ...), custom_call_target="tpu_custom_call" | custom-call | bytes 1048576 | tf_op jit(solution)/shard_map/pallas_call | solution.py:301
  (6 shorter events, 0.0 us)
Async XLA Ops:
  0.6 26.4 %copy-start.3 = (bf16[1,128,1024]{2,1,0:T(8,128)(2,1)S(1)}, bf16[1,128,1024]{2,1,0:T(8,128)(2,1)}, u32[]{:S(2)}) copy-start(bf16[1,128,1024]{2,1,0:T(8,128)(2,1)} %param.5) | copy-start | bytes 786436
  3.7 13.9 %copy-start.5 = (bf16[32,1024]{1,0:T(8,128)(2,1)S(1)}, bf16[32,1024]{1,0:T(8,128)(2,1)}, u32[]{:S(2)}) copy-start(bf16[32,1024]{1,0:T(8,128)(2,1)} %get-tuple-element.25) | copy-start | bytes 196612
  3.7 17.1 %copy-start.6 = (bf16[16,1024]{1,0:T(8,128)(2,1)S(1)}, bf16[16,1024]{1,0:T(8,128)(2,1)}, u32[]{:S(2)}) copy-start(bf16[16,1024]{1,0:T(8,128)(2,1)} %get-tuple-element.26) | copy-start | bytes 98308
  3.7 23.3 %copy-start = (bf16[1,128,1024]{2,1,0:T(8,128)(2,1)S(1)}, bf16[1,128,1024]{2,1,0:T(8,128)(2,1)}, u32[]{:S(2)}) copy-start(bf16[1,128,1024]{2,1,0:T(8,128)(2,1)} %param.6) | copy-start | bytes 786436
  3.8 23.3 %copy-start.1 = (bf16[1,128,1024]{2,1,0:T(8,128)(2,1)S(1)}, bf16[1,128,1024]{2,1,0:T(8,128)(2,1)}, u32[]{:S(2)}) copy-start(bf16[1,128,1024]{2,1,0:T(8,128)(2,1)} %param.7) | copy-start | bytes 786436
  3.8 23.3 %copy-start.2 = (bf16[208,1024]{1,0:T(8,128)(2,1)S(1)}, bf16[208,1024]{1,0:T(8,128)(2,1)}, u32[]{:S(2)}) copy-start(bf16[208,1024]{1,0:T(8,128)(2,1)} %get-tuple-element.22.low_ref) | copy-start | bytes 1277956
  3.8 30.1 %all-to-all-start = ((bf16[32,8,1024]{2,1,0:T(8,128)(2,1)}), bf16[32,8,1024]{2,1,0:T(8,128)(2,1)S(1)}, u32[]{:S(2)}, u32[]{:S(2)}) async-start(bf16[32,8,1024]{2,1,0:T(8,128)(2,1)} %get-tuple-element.27), calls=%async_computation | async-start | bytes 1048576 | tf_op jit(solution)/shard_map/all_to_all | solution.py:319
  17.7 13.5 %collective-permute-start = (bf16[32,1024]{1,0:T(8,128)(2,1)S(1)}, bf16[32,1024]{1,0:T(8,128)(2,1)S(1)}, u32[]{:S(2)}, u32[]{:S(2)}) collective-permute-start(bf16[32,1024]{1,0:T(8,128)(2,1)S(1)} %copy-done.5), channel_id=1, source_target_pairs={{0,1},{1,0},{2,3},{3,2},{4,5},{5,4},{6,7},{7,6},{8,9},{9,8},{10,11... | collective-permute-start | bytes 196616 | tf_op jit(solution)/shard_map/ppermute | solution.py:314
  20.8 8.0 %collective-permute-start.2 = (bf16[16,1024]{1,0:T(8,128)(2,1)S(1)}, bf16[16,1024]{1,0:T(8,128)(2,1)S(1)}, u32[]{:S(2)}, u32[]{:S(2)}) collective-permute-start(bf16[16,1024]{1,0:T(8,128)(2,1)S(1)} %copy-done.6), channel_id=1, source_target_pairs={{0,3},{1,2},{2,1},{3,0},{4,7},{5,6},{6,5},{7,4},{8,11},{9,10},{10,... | collective-permute-start | bytes 98312 | tf_op jit(solution)/shard_map/ppermute | solution.py:314
  24.5 6.6 %collective-permute-start.1 = (bf16[16,1024]{1,0:T(8,128)(2,1)S(1)}, bf16[16,1024]{1,0:T(8,128)(2,1)S(1)}, u32[]{:S(2)}, u32[]{:S(2)}) collective-permute-start(bf16[16,1024]{1,0:T(8,128)(2,1)S(1)} %copy-done.6), channel_id=1, source_target_pairs={{0,2},{1,3},{2,0},{3,1},{4,6},{5,7},{6,4},{7,5},{8,10},{9,11},{10,... | collective-permute-start | bytes 98312 | tf_op jit(solution)/shard_map/ppermute | solution.py:314
  27.1 1.0 %copy-start.4 = (bf16[1,128,1024]{2,1,0:T(8,128)(2,1)S(1)}, bf16[1,128,1024]{2,1,0:T(8,128)(2,1)}, u32[]{:S(2)}) copy-start(bf16[1,128,1024]{2,1,0:T(8,128)(2,1)} %param.8) | copy-start | bytes 786436
  35.5 17.3 %all-to-all-start.1 = ((f32[16,8,128]{2,1,0:T(8,128)}), f32[16,8,128]{2,1,0:T(8,128)S(1)}, u32[]{:S(2)}, u32[]{:S(2)}) async-start(f32[16,8,128]{2,1,0:T(8,128)} %get-tuple-element.35), calls=%async_computation.1 | async-start | bytes 131072 | tf_op jit(solution)/shard_map/all_to_all | solution.py:353
  53.6 22.6 %all-to-all-start.2 = ((bf16[32,8,1152]{2,1,0:T(8,128)(2,1)}), bf16[32,8,1152]{2,1,0:T(8,128)(2,1)S(1)}, u32[]{:S(2)}, u32[]{:S(2)}) async-start(bf16[32,8,1152]{2,1,0:T(8,128)(2,1)} %bitcast.6), calls=%async_computation.2 | async-start | bytes 1179648 | tf_op jit(solution)/shard_map/all_to_all | solution.py:319
  58.3 14.1 %collective-permute-start.3 = (bf16[32,1024]{1,0:T(8,128)(2,1)S(1)}, bf16[32,1024]{1,0:T(8,128)(2,1)S(1)}, u32[]{:S(2)}, u32[]{:S(2)}) collective-permute-start(bf16[32,1024]{1,0:T(8,128)(2,1)S(1)} %get-tuple-element.32), channel_id=1, source_target_pairs={{0,1},{1,0},{2,3},{3,2},{4,5},{5,4},{6,7},{7,6},{8,9},{9,8},{10,11... | collective-permute-start | bytes 196616 | tf_op jit(solution)/shard_map/ppermute | solution.py:314
  61.4 6.6 %collective-permute-start.4 = (bf16[16,1024]{1,0:T(8,128)(2,1)S(1)}, bf16[16,1024]{1,0:T(8,128)(2,1)S(1)}, u32[]{:S(2)}, u32[]{:S(2)}) collective-permute-start(bf16[16,1024]{1,0:T(8,128)(2,1)S(1)} %get-tuple-element.33), channel_id=1, source_target_pairs={{0,2},{1,3},{2,0},{3,1},{4,6},{5,7},{6,4},{7,5},{8,10},{9,11},{10,... | collective-permute-start | bytes 98312 | tf_op jit(solution)/shard_map/ppermute | solution.py:314
  65.8 6.7 %collective-permute-start.5 = (bf16[16,1024]{1,0:T(8,128)(2,1)S(1)}, bf16[16,1024]{1,0:T(8,128)(2,1)S(1)}, u32[]{:S(2)}, u32[]{:S(2)}) collective-permute-start(bf16[16,1024]{1,0:T(8,128)(2,1)S(1)} %get-tuple-element.34), channel_id=1, source_target_pairs={{0,3},{1,2},{2,1},{3,0},{4,7},{5,6},{6,5},{7,4},{8,11},{9,10},{10,... | collective-permute-start | bytes 98312 | tf_op jit(solution)/shard_map/ppermute | solution.py:314

commit v4 on v3

--- a/solution.py
+++ b/solution.py
@@ -207,7 +207,21 @@
         s_ref[i] = tile
 
 
-def grad_kernel(loc_ref, w_ref, dq_ref, gk_ref, gv_ref, g3_ref, g4a_ref, g4b_ref, slot_ref, gf_ref):
+def far_grad_kernel(loc_ref, w_ref, g3_ref, g4a_ref, g4b_ref, gf_ref):
+    for h in range(HEADS):
+        sl = slice(h * HEAD_DIM, (h + 1) * HEAD_DIM)
+        q, c = loc_ref[QUERY : QUERY + TOKENS, sl], loc_ref[COTANGENT : COTANGENT + TOKENS, sl]
+        dk = mm(w_ref[DSCORES + 64 : DSCORES + KEYS, sl], q) * SCALE
+        dv = mm(w_ref[PROBS + 64 : PROBS + KEYS, sl], c)
+        g3_ref[0:16, sl] = dk[0:16].astype(BF16)
+        g3_ref[16:32, sl] = dv[0:16].astype(BF16)
+        g4a_ref[:, sl] = jnp.concatenate([dk[16:24], dv[16:24]], axis=0).astype(BF16)
+        g4b_ref[:, sl] = jnp.concatenate([dk[24:32], dv[24:32]], axis=0).astype(BF16)
+        gf_ref[0:FAR, sl] = dk[32:80].astype(BF16)
+        gf_ref[FAR : 2 * FAR, sl] = dv[32:80].astype(BF16)
+
+
+def grad_kernel(loc_ref, w_ref, gf_ref, dq_ref, gk_ref, gv_ref, slot_ref):
     me = lax.axis_index("seq")
     lane = lax.broadcasted_iota(jnp.int32, (1, TOKENS), 1)
     quarter = lane >> 5
@@ -234,21 +248,12 @@
         d_near = expand(w_ref[DSCORES : DSCORES + 64, sl])
         p_near = expand(w_ref[PROBS : PROBS + 64, sl])
         d_far = w_ref[DSCORES + 64 : DSCORES + KEYS, sl]
-        p_far = w_ref[PROBS + 64 : PROBS + KEYS, sl]
         dq = mm(d_near, loc_ref[0:LOCAL, sl], ((0,), (0,))) + mm(d_far, w_ref[0:REMOTE, sl], ((0,), (0,)))
         dq_ref[:, sl] = (dq * SCALE).astype(BF16)
         dk = mm(d_near, q) * SCALE
         dv = mm(p_near, c)
         gk_ref[:, sl] = dk[0:128] + mm(spread, dk[128:224].astype(BF16))
         gv_ref[:, sl] = dv[0:128] + mm(spread, dv[128:224].astype(BF16))
-        dk = mm(d_far, q) * SCALE
-        dv = mm(p_far, c)
-        g3_ref[0:16, sl] = dk[0:16].astype(BF16)
-        g3_ref[16:32, sl] = dv[0:16].astype(BF16)
-        g4a_ref[:, sl] = jnp.concatenate([dk[16:24], dv[16:24]], axis=0).astype(BF16)
-        g4b_ref[:, sl] = jnp.concatenate([dk[24:32], dv[24:32]], axis=0).astype(BF16)
-        gf_ref[0:FAR, sl] = dk[32:80].astype(BF16)
-        gf_ref[FAR : 2 * FAR, sl] = dv[32:80].astype(BF16)
     row, col = iota2(PEERS * 8, 2 * FAR)
     is_key = col < FAR
     place = far_column(me, jnp.where(is_key, col, col - FAR)) + jnp.where(is_key, 0, 4)
@@ -256,7 +261,7 @@
     slot_ref[:, WIDTH:] = jnp.zeros((PEERS * 8, 128), BF16)
 
 
-def slope_kernel(s_ref, slot_in, slot_out, tile_ref, sem):
+def slope_kernel(s_ref, near_in, slot_in, slot_out, tile_ref, sem):
     value = jnp.sum(jnp.sum(s_ref[...], axis=0), axis=1, keepdims=True)
     high, middle, low = three_parts(value)
     lane = lax.broadcasted_iota(jnp.int32, (HEADS, 128), 1)
@@ -351,24 +356,29 @@
         (loc, near, near3, near4a, near4b, far),
     )
     slopes = lax.all_to_all(slopes, "dp", 0, 0)
-    dq, gk, gv, g3, g4a, g4b, slots = call(
+    g3, g4a, g4b, gf = call(
+        far_grad_kernel,
+        [((32, wide), BF16), ((16, wide), BF16), ((16, wide), BF16), ((2 * FAR, wide), BF16)],
+        (loc, work),
+    )
+    near3 = swap(g3, 1)
+    dq, gk, gv, slots = call(
         grad_kernel,
-        [((TOKENS, wide), BF16), ((TOKENS, wide), F32), ((TOKENS, wide), F32), ((32, wide), BF16),
-         ((16, wide), BF16), ((16, wide), BF16), ((PEERS * 8, wide + 128), BF16)],
-        (loc, work),
-        scratch=[pltpu.VMEM((2 * FAR, wide), BF16)],
+        [((TOKENS, wide), BF16), ((TOKENS, wide), F32), ((TOKENS, wide), F32),
+         ((PEERS * 8, wide + 128), BF16)],
+        (loc, work, gf),
+        cost=LONG,
     )
     (slots,) = call(
         slope_kernel,
         [((PEERS * 8, wide + 128), BF16)],
-        (slopes, slots),
-        [pltpu.VMEM, pl.ANY],
+        (slopes, near3, slots),
+        [pltpu.VMEM, pl.ANY, pl.ANY],
         [pl.ANY],
         [pltpu.VMEM((PEERS * 8, 128), BF16), pltpu.SemaphoreType.DMA(())],
-        alias={1: 0},
+        alias={2: 0},
     )
     far = exchange(slots)
-    near3 = swap(g3, 1)
     near4a = swap(g4a, 2)
     near4b = swap(g4b, 3)
     dk, dv, ds = call(

time: 78.3 us -> 78.3 us (level)
    all_to_all x2, waiting for transfers between devices: 6.51 us -> 9.68 us  [exchange(): back = lax.all_to_all(slots.reshape(PEERS, 8, width), 'seq', 0, 0)]
    all_to_all x1, waiting for transfers between devices: 4.89 us -> 1.92 us  [per_device(): slopes = lax.all_to_all(slopes, 'dp', 0, 0)]
    ppermute x6, waiting for transfers between devices: 6.86 us -> 6.07 us  [swap(): return lax.ppermute(block, 'seq', [(i, i ^ apart) for i in range(PEERS)])]
    pallas_call x6 -> x7, Pallas kernels: 10.5 us -> 10.6 us  [call(): pl.pallas_call(kernel, out_shape=[jax.ShapeDtypeStruct(s, t) for s, t in...]
where the time goes in v4:
time: 78.3 us; the launch traced here: 77.6 us
  starting transfers between devices  47.4 us (61%)
  waiting for transfers between devices  17.7 us (23%)
  Pallas kernels  10.6 us (14%)
  local copies, waits for them, and re-layouts  0.98 us (1%)
  between operations  0.85 us (1%)
    ppermute x6, starting transfers between devices, swap(): return lax.ppermute(block, 'seq', [(i, i ^ apart) for i in range(PEERS)])  19.4 us
    all_to_all x2, starting transfers between devices, exchange(): back = lax.all_to_all(slots.reshape(PEERS, 8, width), 'seq', 0, 0)  18.6 us
    pallas_call x7, Pallas kernels, call(): pl.pallas_call(kernel, out_shape=[jax.ShapeDtypeStruct(s, t) for s, t in...  10.6 us
    all_to_all x2, waiting for transfers between devices, exchange(): back = lax.all_to_all(slots.reshape(PEERS, 8, width), 'seq', 0, 0)  9.68 us
    all_to_all x1, starting transfers between devices, per_device(): slopes = lax.all_to_all(slopes, 'dp', 0, 0)  9.5 us
    ppermute x6, waiting for transfers between devices, swap(): return lax.ppermute(block, 'seq', [(i, i ^ apart) for i in range(PEERS)])  6.07 us
    all_to_all x1, waiting for transfers between devices, per_device(): slopes = lax.all_to_all(slopes, 'dp', 0, 0)  1.92 us
  transfers between devices with their start and end apart: 9, of which 6 were waited for; matrix products, arithmetic and copies ran while one was open for 0% of the time, Pallas kernels for 5%

profile of v4, /device:TPU:1, one launch (start us, length us, event | category | flops | bytes accessed | tf_op | source)
XLA Modules:
  0.0 77.6 jit_solution(9740334178113701552)
XLA Ops:
  0.6 3.1 %shard_map.84 = (bf16[208,1024]{1,0:T(8,128)(2,1)}, bf16[32,1024]{1,0:T(8,128)(2,1)}, bf16[16,1024]{1,0:T(8,128)(2,1)}, bf16[32,8,1024]{2,1,0:T(8,128)(2,1)}) custom-call(bf16[128,1024]{1,0:T(8,128)(2,1)} %bitcast.13, bf16[128,1024]{1,0:T(8,128)(2,1)} %bitcast.15, f32[8]{0:T(128)} %slope_hbm.1), custom_call_target="tpu_custom_call" | custom-call | bytes 1048576 | tf_op jit(solution)/shard_map/pallas_call | solution.py:306
  3.7 0.0 copy-start.5
  3.7 0.0 copy-start.6
  3.7 0.0 copy-start
  3.8 0.0 copy-start.1
  3.8 13.9 %all-to-all-start = ((bf16[32,8,1024]{2,1,0:T(8,128)(2,1)}), bf16[32,8,1024]{2,1,0:T(8,128)(2,1)S(1)}, u32[]{:S(2)}, u32[]{:S(2)}) async-start(bf16[32,8,1024]{2,1,0:T(8,128)(2,1)} %get-tuple-element.28), calls=%async_computation | async-start | bytes 1048576 | tf_op jit(solution)/shard_map/all_to_all | solution.py:324
  17.7 3.1 %collective-permute-start = (bf16[32,1024]{1,0:T(8,128)(2,1)S(1)}, bf16[32,1024]{1,0:T(8,128)(2,1)S(1)}, u32[]{:S(2)}, u32[]{:S(2)}) collective-permute-start(bf16[32,1024]{1,0:T(8,128)(2,1)S(1)} %copy-done.5), channel_id=1, source_target_pairs={{0,1},{1,0},{2,3},{3,2},{4,5},{5,4},{6,7},{7,6},{8,9},{9,8},{10,11... | collective-permute-start | bytes 196616 | tf_op jit(solution)/shard_map/ppermute | solution.py:319
  20.8 0.0 copy-done.6
  20.8 3.7 %collective-permute-start.2 = (bf16[16,1024]{1,0:T(8,128)(2,1)S(1)}, bf16[16,1024]{1,0:T(8,128)(2,1)S(1)}, u32[]{:S(2)}, u32[]{:S(2)}) collective-permute-start(bf16[16,1024]{1,0:T(8,128)(2,1)S(1)} %copy-done.6), channel_id=1, source_target_pairs={{0,3},{1,2},{2,1},{3,0},{4,7},{5,6},{6,5},{7,4},{8,11},{9,10},{10,... | collective-permute-start | bytes 98312 | tf_op jit(solution)/shard_map/ppermute | solution.py:319
  24.5 2.5 %collective-permute-start.1 = (bf16[16,1024]{1,0:T(8,128)(2,1)S(1)}, bf16[16,1024]{1,0:T(8,128)(2,1)S(1)}, u32[]{:S(2)}, u32[]{:S(2)}) collective-permute-start(bf16[16,1024]{1,0:T(8,128)(2,1)S(1)} %copy-done.6), channel_id=1, source_target_pairs={{0,2},{1,3},{2,0},{3,1},{4,6},{5,7},{6,4},{7,5},{8,10},{9,11},{10,... | collective-permute-start | bytes 98312 | tf_op jit(solution)/shard_map/ppermute | solution.py:319
  27.1 0.0 copy-start.4
  27.1 0.9 %copy-done.4 = bf16[1,128,1024]{2,1,0:T(8,128)(2,1)S(1)} copy-done((bf16[1,128,1024]{2,1,0:T(8,128)(2,1)S(1)}, bf16[1,128,1024]{2,1,0:T(8,128)(2,1)}, u32[]{:S(2)}) %copy-start.4) | copy-done | bytes 262168
  28.0 0.8 shard_map.85
  28.8 0.0 collective-permute-done.2.r4b_ref
  28.8 2.3 %collective-permute-done.1.r4a_ref = bf16[16,1024]{1,0:T(8,128)(2,1)S(1)} collective-permute-done((bf16[16,1024]{1,0:T(8,128)(2,1)S(1)}, bf16[16,1024]{1,0:T(8,128)(2,1)S(1)}, u32[]{:S(2)}, u32[]{:S(2)}) %collective-permute-start.1) | collective-permute-done | bytes 32800 | tf_op jit(solution)/shard_map/ppermute | solution.py:319
  31.2 0.0 collective-permute-done.r3_ref
  31.2 2.8 %all-to-all-done = bf16[32,8,1024]{2,1,0:T(8,128)(2,1)S(1)} async-done(((bf16[32,8,1024]{2,1,0:T(8,128)(2,1)}), bf16[32,8,1024]{2,1,0:T(8,128)(2,1)S(1)}, u32[]{:S(2)}, u32[]{:S(2)}) %all-to-all-start) | async-done | bytes 524320 | tf_op jit(solution)/shard_map/all_to_all | solution.py:324
  33.9 1.6 %shard_map.86 = (bf16[448,1024]{1,0:T(8,128)(2,1)S(1)}, f32[16,8,128]{2,1,0:T(8,128)}) custom-call(bf16[496,1024]{1,0:T(8,128)(2,1)S(1)} %get-tuple-element.24.loc_ref, f32[128,1024]{1,0:T(8,128)S(1)} %get-tuple-element.25.near_ref, bf16[32,1024]{1,0:T(8,128)(2,1)S(1)} %collective-permute-done.r3_ref, bf16[16,1024]{1,0:T(8,128)(2,1)S(1)} %collective-permute-done.1.r4a_ref, ...), custom_call_target="tpu_custom_call" | custom-call | bytes 1048576 | tf_op jit(solution)/shard_map/pallas_call | solution.py:306
  35.5 9.5 %all-to-all-start.1 = ((f32[16,8,128]{2,1,0:T(8,128)}), f32[16,8,128]{2,1,0:T(8,128)S(1)}, u32[]{:S(2)}, u32[]{:S(2)}) async-start(f32[16,8,128]{2,1,0:T(8,128)} %get-tuple-element.37), calls=%async_computation.1 | async-start | bytes 131072 | tf_op jit(solution)/shard_map/all_to_all | solution.py:358
  45.0 0.3 shard_map.87
  45.4 2.6 %collective-permute-start.3 = (bf16[32,1024]{1,0:T(8,128)(2,1)S(1)}, bf16[32,1024]{1,0:T(8,128)(2,1)S(1)}, u32[]{:S(2)}, u32[]{:S(2)}) collective-permute-start(bf16[32,1024]{1,0:T(8,128)(2,1)S(1)} %get-tuple-element.34), channel_id=1, source_target_pairs={{0,1},{1,0},{2,3},{3,2},{4,5},{5,4},{6,7},{7,6},{8,9},{9,8},{10,11... | collective-permute-start | bytes 196616 | tf_op jit(solution)/shard_map/ppermute | solution.py:319
  47.9 2.7 %shard_map.88 = (bf16[128,1024]{1,0:T(8,128)(2,1)}, f32[128,1024]{1,0:T(8,128)S(1)}, f32[128,1024]{1,0:T(8,128)S(1)}, bf16[256,1152]{1,0:T(8,128)(2,1)}) custom-call(bf16[496,1024]{1,0:T(8,128)(2,1)S(1)} %get-tuple-element.24.loc_ref, bf16[448,1024]{1,0:T(8,128)(2,1)S(1)} %get-tuple-element.29.w_ref, bf16[96,1024]{1,0:T(8,128)(2,1)S(1)} %get-tuple-element.30.gf_ref), custom_call_target="tpu_custom_call" | custom-call | bytes 268435456 | tf_op jit(solution)/shard_map/pallas_call | solution.py:306
  50.7 0.2 collective-permute-done.3.near_in.r3_ref
  50.9 1.9 %all-to-all-done.1.s_ref = f32[16,8,128]{2,1,0:T(8,128)S(1)} async-done(((f32[16,8,128]{2,1,0:T(8,128)}), f32[16,8,128]{2,1,0:T(8,128)S(1)}, u32[]{:S(2)}, u32[]{:S(2)}) %all-to-all-start.1) | async-done | bytes 65568 | tf_op jit(solution)/shard_map/all_to_all | solution.py:358
  52.8 0.7 shard_map.89
  53.6 4.7 %all-to-all-start.2 = ((bf16[32,8,1152]{2,1,0:T(8,128)(2,1)}), bf16[32,8,1152]{2,1,0:T(8,128)(2,1)S(1)}, u32[]{:S(2)}, u32[]{:S(2)}) async-start(bf16[32,8,1152]{2,1,0:T(8,128)(2,1)} %bitcast.6), calls=%async_computation.2 | async-start | bytes 1179648 | tf_op jit(solution)/shard_map/all_to_all | solution.py:324
  58.3 4.6 %collective-permute-start.4 = (bf16[16,1024]{1,0:T(8,128)(2,1)S(1)}, bf16[16,1024]{1,0:T(8,128)(2,1)S(1)}, u32[]{:S(2)}, u32[]{:S(2)}) collective-permute-start(bf16[16,1024]{1,0:T(8,128)(2,1)S(1)} %get-tuple-element.35), channel_id=1, source_target_pairs={{0,2},{1,3},{2,0},{3,1},{4,6},{5,7},{6,4},{7,5},{8,10},{9,11},{10,... | collective-permute-start | bytes 98312 | tf_op jit(solution)/shard_map/ppermute | solution.py:319
  63.0 2.8 %collective-permute-start.5 = (bf16[16,1024]{1,0:T(8,128)(2,1)S(1)}, bf16[16,1024]{1,0:T(8,128)(2,1)S(1)}, u32[]{:S(2)}, u32[]{:S(2)}) collective-permute-start(bf16[16,1024]{1,0:T(8,128)(2,1)S(1)} %get-tuple-element.36), channel_id=1, source_target_pairs={{0,3},{1,2},{2,1},{3,0},{4,7},{5,6},{6,5},{7,4},{8,11},{9,10},{10,... | collective-permute-start | bytes 98312 | tf_op jit(solution)/shard_map/ppermute | solution.py:319
  65.8 0.0 collective-permute-done.4.r4a_ref
  65.8 3.5 %collective-permute-done.5.r4b_ref = bf16[16,1024]{1,0:T(8,128)(2,1)S(1)} collective-permute-done((bf16[16,1024]{1,0:T(8,128)(2,1)S(1)}, bf16[16,1024]{1,0:T(8,128)(2,1)S(1)}, u32[]{:S(2)}, u32[]{:S(2)}) %collective-permute-start.5) | collective-permute-done | bytes 32800 | tf_op jit(solution)/shard_map/ppermute | solution.py:319
  69.3 6.9 %all-to-all-done.2 = bf16[32,8,1152]{2,1,0:T(8,128)(2,1)S(1)} async-done(((bf16[32,8,1152]{2,1,0:T(8,128)(2,1)}), bf16[32,8,1152]{2,1,0:T(8,128)(2,1)S(1)}, u32[]{:S(2)}, u32[]{:S(2)}) %all-to-all-start.2) | async-done | bytes 589856 | tf_op jit(solution)/shard_map/all_to_all | solution.py:324
  76.2 1.4 %shard_map.90 = (bf16[128,1024]{1,0:T(8,128)(2,1)}, bf16[128,1024]{1,0:T(8,128)(2,1)}, f32[1,8]{1,0:T(1,128)}) custom-call(f32[128,1024]{1,0:T(8,128)S(1)} %get-tuple-element.32.gk_ref, f32[128,1024]{1,0:T(8,128)S(1)} %get-tuple-element.33.gv_ref, bf16[32,1024]{1,0:T(8,128)(2,1)S(1)} %collective-permute-done.3.near_in.r3_ref, ...), custom_call_target="tpu_custom_call" | custom-call | bytes 1048576 | tf_op jit(solution)/shard_map/pallas_call | solution.py:306
  (7 shorter events, 0.0 us)
Async XLA Ops:
  0.6 26.4 %copy-start.3 = (bf16[1,128,1024]{2,1,0:T(8,128)(2,1)S(1)}, bf16[1,128,1024]{2,1,0:T(8,128)(2,1)}, u32[]{:S(2)}) copy-start(bf16[1,128,1024]{2,1,0:T(8,128)(2,1)} %param.5) | copy-start | bytes 786436
  3.7 13.9 %copy-start.5 = (bf16[32,1024]{1,0:T(8,128)(2,1)S(1)}, bf16[32,1024]{1,0:T(8,128)(2,1)}, u32[]{:S(2)}) copy-start(bf16[32,1024]{1,0:T(8,128)(2,1)} %get-tuple-element.26) | copy-start | bytes 196612
  3.7 17.1 %copy-start.6 = (bf16[16,1024]{1,0:T(8,128)(2,1)S(1)}, bf16[16,1024]{1,0:T(8,128)(2,1)}, u32[]{:S(2)}) copy-start(bf16[16,1024]{1,0:T(8,128)(2,1)} %get-tuple-element.27) | copy-start | bytes 98308
  3.7 23.3 %copy-start = (bf16[1,128,1024]{2,1,0:T(8,128)(2,1)S(1)}, bf16[1,128,1024]{2,1,0:T(8,128)(2,1)}, u32[]{:S(2)}) copy-start(bf16[1,128,1024]{2,1,0:T(8,128)(2,1)} %param.6) | copy-start | bytes 786436
  3.8 23.3 %copy-start.1 = (bf16[1,128,1024]{2,1,0:T(8,128)(2,1)S(1)}, bf16[1,128,1024]{2,1,0:T(8,128)(2,1)}, u32[]{:S(2)}) copy-start(bf16[1,128,1024]{2,1,0:T(8,128)(2,1)} %param.7) | copy-start | bytes 786436
  3.8 23.3 %copy-start.2 = (bf16[208,1024]{1,0:T(8,128)(2,1)S(1)}, bf16[208,1024]{1,0:T(8,128)(2,1)}, u32[]{:S(2)}) copy-start(bf16[208,1024]{1,0:T(8,128)(2,1)} %get-tuple-element.23.low_ref) | copy-start | bytes 1277956
  3.8 30.1 %all-to-all-start = ((bf16[32,8,1024]{2,1,0:T(8,128)(2,1)}), bf16[32,8,1024]{2,1,0:T(8,128)(2,1)S(1)}, u32[]{:S(2)}, u32[]{:S(2)}) async-start(bf16[32,8,1024]{2,1,0:T(8,128)(2,1)} %get-tuple-element.28), calls=%async_computation | async-start | bytes 1048576 | tf_op jit(solution)/shard_map/all_to_all | solution.py:324
  17.7 13.5 %collective-permute-start = (bf16[32,1024]{1,0:T(8,128)(2,1)S(1)}, bf16[32,1024]{1,0:T(8,128)(2,1)S(1)}, u32[]{:S(2)}, u32[]{:S(2)}) collective-permute-start(bf16[32,1024]{1,0:T(8,128)(2,1)S(1)} %copy-done.5), channel_id=1, source_target_pairs={{0,1},{1,0},{2,3},{3,2},{4,5},{5,4},{6,7},{7,6},{8,9},{9,8},{10,11... | collective-permute-start | bytes 196616 | tf_op jit(solution)/shard_map/ppermute | solution.py:319
  20.8 8.0 %collective-permute-start.2 = (bf16[16,1024]{1,0:T(8,128)(2,1)S(1)}, bf16[16,1024]{1,0:T(8,128)(2,1)S(1)}, u32[]{:S(2)}, u32[]{:S(2)}) collective-permute-start(bf16[16,1024]{1,0:T(8,128)(2,1)S(1)} %copy-done.6), channel_id=1, source_target_pairs={{0,3},{1,2},{2,1},{3,0},{4,7},{5,6},{6,5},{7,4},{8,11},{9,10},{10,... | collective-permute-start | bytes 98312 | tf_op jit(solution)/shard_map/ppermute | solution.py:319
  24.5 6.6 %collective-permute-start.1 = (bf16[16,1024]{1,0:T(8,128)(2,1)S(1)}, bf16[16,1024]{1,0:T(8,128)(2,1)S(1)}, u32[]{:S(2)}, u32[]{:S(2)}) collective-permute-start(bf16[16,1024]{1,0:T(8,128)(2,1)S(1)} %copy-done.6), channel_id=1, source_target_pairs={{0,2},{1,3},{2,0},{3,1},{4,6},{5,7},{6,4},{7,5},{8,10},{9,11},{10,... | collective-permute-start | bytes 98312 | tf_op jit(solution)/shard_map/ppermute | solution.py:319
  27.1 1.0 %copy-start.4 = (bf16[1,128,1024]{2,1,0:T(8,128)(2,1)S(1)}, bf16[1,128,1024]{2,1,0:T(8,128)(2,1)}, u32[]{:S(2)}) copy-start(bf16[1,128,1024]{2,1,0:T(8,128)(2,1)} %param.8) | copy-start | bytes 786436
  35.5 17.3 %all-to-all-start.1 = ((f32[16,8,128]{2,1,0:T(8,128)}), f32[16,8,128]{2,1,0:T(8,128)S(1)}, u32[]{:S(2)}, u32[]{:S(2)}) async-start(f32[16,8,128]{2,1,0:T(8,128)} %get-tuple-element.37), calls=%async_computation.1 | async-start | bytes 131072 | tf_op jit(solution)/shard_map/all_to_all | solution.py:358
  45.4 5.6 %collective-permute-start.3 = (bf16[32,1024]{1,0:T(8,128)(2,1)S(1)}, bf16[32,1024]{1,0:T(8,128)(2,1)S(1)}, u32[]{:S(2)}, u32[]{:S(2)}) collective-permute-start(bf16[32,1024]{1,0:T(8,128)(2,1)S(1)} %get-tuple-element.34), channel_id=1, source_target_pairs={{0,1},{1,0},{2,3},{3,2},{4,5},{5,4},{6,7},{7,6},{8,9},{9,8},{10,11... | collective-permute-start | bytes 196616 | tf_op jit(solution)/shard_map/ppermute | solution.py:319
  53.6 22.6 %all-to-all-start.2 = ((bf16[32,8,1152]{2,1,0:T(8,128)(2,1)}), bf16[32,8,1152]{2,1,0:T(8,128)(2,1)S(1)}, u32[]{:S(2)}, u32[]{:S(2)}) async-start(bf16[32,8,1152]{2,1,0:T(8,128)(2,1)} %bitcast.6), calls=%async_computation.2 | async-start | bytes 1179648 | tf_op jit(solution)/shard_map/all_to_all | solution.py:324
  58.3 7.5 %collective-permute-start.4 = (bf16[16,1024]{1,0:T(8,128)(2,1)S(1)}, bf16[16,1024]{1,0:T(8,128)(2,1)S(1)}, u32[]{:S(2)}, u32[]{:S(2)}) collective-permute-start(bf16[16,1024]{1,0:T(8,128)(2,1)S(1)} %get-tuple-element.35), channel_id=1, source_target_pairs={{0,2},{1,3},{2,0},{3,1},{4,6},{5,7},{6,4},{7,5},{8,10},{9,11},{10,... | collective-permute-start | bytes 98312 | tf_op jit(solution)/shard_map/ppermute | solution.py:319
  63.0 6.3 %collective-permute-start.5 = (bf16[16,1024]{1,0:T(8,128)(2,1)S(1)}, bf16[16,1024]{1,0:T(8,128)(2,1)S(1)}, u32[]{:S(2)}, u32[]{:S(2)}) collective-permute-start(bf16[16,1024]{1,0:T(8,128)(2,1)S(1)} %get-tuple-element.36), channel_id=1, source_target_pairs={{0,3},{1,2},{2,1},{3,0},{4,7},{5,6},{6,5},{7,4},{8,11},{9,10},{10,... | collective-permute-start | bytes 98312 | tf_op jit(solution)/shard_map/ppermute | solution.py:319

commit v5 on v4

--- a/solution.py
+++ b/solution.py
@@ -54,6 +54,7 @@
 REMOTE = 80
 PROBS = 2 * REMOTE
 DSCORES = PROBS + KEYS
+HALF = WIDTH // 2
 QUERY = LOCAL
 COTANGENT = LOCAL + TOKENS
 STEPS = LOCAL + 2 * TOKENS
@@ -207,7 +208,7 @@
         s_ref[i] = tile
 
 
-def far_grad_kernel(loc_ref, w_ref, g3_ref, g4a_ref, g4b_ref, gf_ref):
+def far_grad_kernel(loc_ref, w_ref, g3_ref, g4a_ref, g4b_ref, g5_ref, gf_ref):
     for h in range(HEADS):
         sl = slice(h * HEAD_DIM, (h + 1) * HEAD_DIM)
         q, c = loc_ref[QUERY : QUERY + TOKENS, sl], loc_ref[COTANGENT : COTANGENT + TOKENS, sl]
@@ -217,8 +218,10 @@
         g3_ref[16:32, sl] = dv[0:16].astype(BF16)
         g4a_ref[:, sl] = jnp.concatenate([dk[16:24], dv[16:24]], axis=0).astype(BF16)
         g4b_ref[:, sl] = jnp.concatenate([dk[24:32], dv[24:32]], axis=0).astype(BF16)
-        gf_ref[0:FAR, sl] = dk[32:80].astype(BF16)
-        gf_ref[FAR : 2 * FAR, sl] = dv[32:80].astype(BF16)
+        g5_ref[0:16, sl] = dk[32:48].astype(BF16)
+        g5_ref[16:32, sl] = dv[32:48].astype(BF16)
+        gf_ref[0:32, sl] = dk[48:80].astype(BF16)
+        gf_ref[32:64, sl] = dv[48:80].astype(BF16)
 
 
 def grad_kernel(loc_ref, w_ref, gf_ref, dq_ref, gk_ref, gv_ref, slot_ref):
@@ -254,14 +257,20 @@
         dv = mm(p_near, c)
         gk_ref[:, sl] = dk[0:128] + mm(spread, dk[128:224].astype(BF16))
         gv_ref[:, sl] = dv[0:128] + mm(spread, dv[128:224].astype(BF16))
-    row, col = iota2(PEERS * 8, 2 * FAR)
-    is_key = col < FAR
-    place = far_column(me, jnp.where(is_key, col, col - FAR)) + jnp.where(is_key, 0, 4)
-    slot_ref[:, 0:WIDTH] = mm(mat(row == place, 1.0), gf_ref[...]).astype(BF16)
-    slot_ref[:, WIDTH:] = jnp.zeros((PEERS * 8, 128), BF16)
-
-
-def slope_kernel(s_ref, near_in, slot_in, slot_out, tile_ref, sem):
+    row, col = iota2(PEERS * 8, 64)
+    is_key = col < 32
+    line = jnp.where(is_key, col, col - 32) + 16
+    place = far_column(me, line) + jnp.where(is_key, 0, 2)
+    first = mm(mat(row == place, 1.0), gf_ref[:, 0:HALF])
+    second = mm(mat(row == place + 4, 1.0), gf_ref[:, HALF:WIDTH])
+    slot_ref[:, 0:HALF] = (first + second).astype(BF16)
+    slot_ref[:, HALF:] = jnp.zeros((PEERS * 8, 128), BF16)
+
+
+def slope_kernel(
+    s_ref, r5_ref, g3_ref, g4a_ref, g4b_ref, slot_in, pair_ref, a_ref, b_ref, slot_out, tile_ref, sem
+):
+    me = lax.axis_index("seq")
     value = jnp.sum(jnp.sum(s_ref[...], axis=0), axis=1, keepdims=True)
     high, middle, low = three_parts(value)
     lane = lax.broadcasted_iota(jnp.int32, (HEADS, 128), 1)
@@ -269,31 +278,46 @@
         lane == 0, high, jnp.where(lane == 1, middle, jnp.where(lane == 2, low, 0.0))
     )
     tile_ref[...] = jnp.concatenate([tile] * PEERS, axis=0).astype(BF16)
-    put = pltpu.make_async_copy(tile_ref, slot_out.at[:, pl.ds(WIDTH, 128)], sem)
+    put = pltpu.make_async_copy(tile_ref, slot_out.at[:, pl.ds(HALF, 128)], sem)
     put.start()
+    row, col = iota2(16, 32)
+    for apart, own_ref, out_ref in ((1, g3_ref, pair_ref), (2, g4a_ref, a_ref), (3, g4b_ref, b_ref)):
+        size = own_ref.shape[0]
+        out_ref[0:size, :] = own_ref[...]
+        at = ((me & 3) ^ apart) * 4
+        pick = ((row < 4) & (col == at + row)) | ((row >= 4) & (row < 8) & (col == at + row + 12))
+        out_ref[size : size + 16, :] = mm(mat(pick, 1.0), r5_ref[...]).astype(BF16)
     put.wait()
 
 
-def final_kernel(gk_ref, gv_ref, r3_ref, r4a_ref, r4b_ref, r_ref, ok_ref, ov_ref, os_ref):
+def final_kernel(
+    gk_ref, gv_ref, pair_ref, a_ref, b_ref, r5_ref, r_ref, ok_ref, ov_ref, os_ref
+):
     me = lax.axis_index("seq")
     row, col = iota2(TOKENS, PEERS * 8)
     apart = (col >> 3) ^ me
     line = col & 7
-    shift = jnp.where(apart >= 16, 7, jnp.where(apart >= 8, 6, 5))
-    weight = jnp.where(
-        apart >= 16, 2.0**-7, jnp.where(apart >= 8, 2.0**-6, jnp.where(apart >= 4, 2.0**-5, 0.0))
-    )
+    shift = jnp.where(apart >= 16, 7, 6)
+    weight = jnp.where(apart >= 16, 2.0**-7, jnp.where(apart >= 8, 2.0**-6, 0.0))
     covers = lax.shift_right_logical(row, shift)
-    row3, col3 = iota2(TOKENS, 32)
-    row4, col4 = iota2(TOKENS, 16)
+    row3, col3 = iota2(TOKENS, 48)
+    row4, col4 = iota2(TOKENS, 32)
     for out_ref, own_ref, which in ((ok_ref, gk_ref, 0), (ov_ref, gv_ref, 1)):
-        total = own_ref[...]
-        total += mm(mat(covers + 4 * which == line, weight), r_ref[:, 0:WIDTH])
-        total += mm(mat((row3 >> 3) + 16 * which == col3, 2.0**-3), r3_ref[...])
-        both = mat((row4 >> 4) + 8 * which == col4, 2.0**-4)
-        total += mm(both, r4a_ref[...]) + mm(both, r4b_ref[...])
-        out_ref[...] = total.astype(BF16)
-    slopes = r_ref[:, WIDTH:].astype(F32).reshape(PEERS, HEADS, 128)
+        near = own_ref[...]
+        three = jnp.where((row3 >> 3) + 16 * which == col3, 2.0**-3, 0.0)
+        five = jnp.where((row3 >> 5) + 32 + 4 * which == col3, 2.0**-5, 0.0)
+        near += mm((three + five).astype(BF16), pair_ref[...])
+        four = jnp.where((row4 >> 4) + 8 * which == col4, 2.0**-4, 0.0)
+        five = jnp.where((row4 >> 5) + 16 + 4 * which == col4, 2.0**-5, 0.0)
+        both = (four + five).astype(BF16)
+        near += mm(both, a_ref[...]) + mm(both, b_ref[...])
+        mine = mat((row4 >> 5) + 4 * (me & 3) + 16 * which == col4, 2.0**-5)
+        near += mm(mine, r5_ref[...])
+        for half in range(2):
+            sl = slice(HALF * half, HALF * half + HALF)
+            far = mat(covers + 2 * which + 4 * half == line, weight)
+            out_ref[:, sl] = (near[:, sl] + mm(far, r_ref[:, 0:HALF])).astype(BF16)
+    slopes = r_ref[:, HALF:].astype(F32).reshape(PEERS, HEADS, 128)
     value = jnp.sum(jnp.sum(slopes, axis=0), axis=1, keepdims=True)
     srow, scol = iota2(HEADS, 128)
     line = jnp.sum(jnp.where(srow == scol, value, 0.0), axis=0, keepdims=True)
@@ -356,35 +380,36 @@
         (loc, near, near3, near4a, near4b, far),
     )
     slopes = lax.all_to_all(slopes, "dp", 0, 0)
-    g3, g4a, g4b, gf = call(
+    g3, g4a, g4b, g5, gf = call(
         far_grad_kernel,
-        [((32, wide), BF16), ((16, wide), BF16), ((16, wide), BF16), ((2 * FAR, wide), BF16)],
+        [((32, wide), BF16), ((16, wide), BF16), ((16, wide), BF16), ((32, wide), BF16), ((64, wide), BF16)],
         (loc, work),
     )
-    near3 = swap(g3, 1)
+    near5 = swap(g5, 4)
     dq, gk, gv, slots = call(
         grad_kernel,
         [((TOKENS, wide), BF16), ((TOKENS, wide), F32), ((TOKENS, wide), F32),
-         ((PEERS * 8, wide + 128), BF16)],
+         ((PEERS * 8, HALF + 128), BF16)],
         (loc, work, gf),
         cost=LONG,
     )
-    (slots,) = call(
+    pair, four_a, four_b, slots = call(
         slope_kernel,
-        [((PEERS * 8, wide + 128), BF16)],
-        (slopes, near3, slots),
-        [pltpu.VMEM, pl.ANY, pl.ANY],
-        [pl.ANY],
+        [((48, wide), BF16), ((32, wide), BF16), ((32, wide), BF16), ((PEERS * 8, HALF + 128), BF16)],
+        (slopes, near5, g3, g4a, g4b, slots),
+        [pltpu.VMEM] * 5 + [pl.ANY],
+        [pltpu.VMEM] * 3 + [pl.ANY],
         [pltpu.VMEM((PEERS * 8, 128), BF16), pltpu.SemaphoreType.DMA(())],
-        alias={2: 0},
+        alias={5: 3},
     )
     far = exchange(slots)
-    near4a = swap(g4a, 2)
-    near4b = swap(g4b, 3)
+    pair = swap(pair, 1)
+    four_a = swap(four_a, 2)
+    four_b = swap(four_b, 3)
     dk, dv, ds = call(
         final_kernel,
         [((TOKENS, wide), BF16), ((TOKENS, wide), BF16), ((1, HEADS), F32)],
-        (gk, gv, near3, near4a, near4b, far),
+        (gk, gv, pair, four_a, four_b, near5, far),
     )
     return dq[None], dk[None], dv[None], ds.reshape(HEADS)
 

time: 78.3 us -> 74.4 us (0.950)
  waiting for transfers between devices: 17.7 us -> 11.4 us
  starting transfers between devices: 47.4 us -> 49.9 us
    all_to_all x2, waiting for transfers between devices: 9.68 us -> 2.76 us  [exchange(): back = lax.all_to_all(slots.reshape(PEERS, 8, width), 'seq', 0, 0)]
    ppermute x6 -> x7, starting transfers between devices: 19.4 us -> 21.9 us  [swap(): return lax.ppermute(block, 'seq', [(i, i ^ apart) for i in range(PEERS)])]
    ppermute x6 -> x7, waiting for transfers between devices: 6.07 us -> 6.69 us  [swap(): return lax.ppermute(block, 'seq', [(i, i ^ apart) for i in range(PEERS)])]
  transfers between devices with their start and end apart: 9 -> 10, of which waited for: 6 -> 5; matrix products, arithmetic and copies ran while one was open for 0% -> 0% of each run, Pallas kernels for 5% -> 5%
where the time goes in v5:
time: 74.4 us; the launch traced here: 73.8 us
  starting transfers between devices  49.9 us (67%)
  waiting for transfers between devices  11.4 us (15%)
  Pallas kernels  10.7 us (14%)
  local copies, waits for them, and re-layouts  0.98 us (1%)
  between operations  0.85 us (1%)
    ppermute x7, starting transfers between devices, swap(): return lax.ppermute(block, 'seq', [(i, i ^ apart) for i in range(PEERS)])  21.9 us
    all_to_all x2, starting transfers between devices, exchange(): back = lax.all_to_all(slots.reshape(PEERS, 8, width), 'seq', 0, 0)  18.6 us
    pallas_call x7, Pallas kernels, call(): pl.pallas_call(kernel, out_shape=[jax.ShapeDtypeStruct(s, t) for s, t in...  10.7 us
    all_to_all x1, starting transfers between devices, per_device(): slopes = lax.all_to_all(slopes, 'dp', 0, 0)  9.5 us
    ppermute x7, waiting for transfers between devices, swap(): return lax.ppermute(block, 'seq', [(i, i ^ apart) for i in range(PEERS)])  6.69 us
    all_to_all x2, waiting for transfers between devices, exchange(): back = lax.all_to_all(slots.reshape(PEERS, 8, width), 'seq', 0, 0)  2.76 us
    all_to_all x1, waiting for transfers between devices, per_device(): slopes = lax.all_to_all(slopes, 'dp', 0, 0)  1.89 us
  transfers between devices with their start and end apart: 10, of which 5 were waited for; matrix products, arithmetic and copies ran while one was open for 0% of the time, Pallas kernels for 5%

profile of v5, /device:TPU:1, one launch (start us, length us, event | category | flops | bytes accessed | tf_op | source)
XLA Modules:
  0.0 73.8 jit_solution(12666993040711392464)
XLA Ops:
  0.6 3.1 %shard_map.84 = (bf16[208,1024]{1,0:T(8,128)(2,1)}, bf16[32,1024]{1,0:T(8,128)(2,1)}, bf16[16,1024]{1,0:T(8,128)(2,1)}, bf16[32,8,1024]{2,1,0:T(8,128)(2,1)}) custom-call(bf16[128,1024]{1,0:T(8,128)(2,1)} %bitcast.13, bf16[128,1024]{1,0:T(8,128)(2,1)} %bitcast.15, f32[8]{0:T(128)} %slope_hbm.1), custom_call_target="tpu_custom_call" | custom-call | bytes 1048576 | tf_op jit(solution)/shard_map/pallas_call | solution.py:330
  3.7 0.0 copy-start.5
  3.7 0.0 copy-start.6
  3.7 0.0 copy-start
  3.7 0.0 copy-start.1
  3.8 13.9 %all-to-all-start = ((bf16[32,8,1024]{2,1,0:T(8,128)(2,1)}), bf16[32,8,1024]{2,1,0:T(8,128)(2,1)S(1)}, u32[]{:S(2)}, u32[]{:S(2)}) async-start(bf16[32,8,1024]{2,1,0:T(8,128)(2,1)} %get-tuple-element.33), calls=%async_computation | async-start | bytes 1048576 | tf_op jit(solution)/shard_map/all_to_all | solution.py:348
  17.7 3.1 %collective-permute-start = (bf16[32,1024]{1,0:T(8,128)(2,1)S(1)}, bf16[32,1024]{1,0:T(8,128)(2,1)S(1)}, u32[]{:S(2)}, u32[]{:S(2)}) collective-permute-start(bf16[32,1024]{1,0:T(8,128)(2,1)S(1)} %copy-done.5), channel_id=1, source_target_pairs={{0,1},{1,0},{2,3},{3,2},{4,5},{5,4},{6,7},{7,6},{8,9},{9,8},{10,11... | collective-permute-start | bytes 196616 | tf_op jit(solution)/shard_map/ppermute | solution.py:343
  20.8 3.7 %collective-permute-start.2 = (bf16[16,1024]{1,0:T(8,128)(2,1)S(1)}, bf16[16,1024]{1,0:T(8,128)(2,1)S(1)}, u32[]{:S(2)}, u32[]{:S(2)}) collective-permute-start(bf16[16,1024]{1,0:T(8,128)(2,1)S(1)} %copy-done.6), channel_id=1, source_target_pairs={{0,3},{1,2},{2,1},{3,0},{4,7},{5,6},{6,5},{7,4},{8,11},{9,10},{10,... | collective-permute-start | bytes 98312 | tf_op jit(solution)/shard_map/ppermute | solution.py:343
  24.5 2.5 %collective-permute-start.1 = (bf16[16,1024]{1,0:T(8,128)(2,1)S(1)}, bf16[16,1024]{1,0:T(8,128)(2,1)S(1)}, u32[]{:S(2)}, u32[]{:S(2)}) collective-permute-start(bf16[16,1024]{1,0:T(8,128)(2,1)S(1)} %copy-done.6), channel_id=1, source_target_pairs={{0,2},{1,3},{2,0},{3,1},{4,6},{5,7},{6,4},{7,5},{8,10},{9,11},{10,... | collective-permute-start | bytes 98312 | tf_op jit(solution)/shard_map/ppermute | solution.py:343
  27.1 0.0 copy-start.4
  27.1 0.9 %copy-done.4 = bf16[1,128,1024]{2,1,0:T(8,128)(2,1)S(1)} copy-done((bf16[1,128,1024]{2,1,0:T(8,128)(2,1)S(1)}, bf16[1,128,1024]{2,1,0:T(8,128)(2,1)}, u32[]{:S(2)}) %copy-start.4) | copy-done | bytes 262168
  28.0 0.8 %shard_map.85 = (bf16[496,1024]{1,0:T(8,128)(2,1)S(1)}, f32[128,1024]{1,0:T(8,128)S(1)}) custom-call(bf16[128,1024]{1,0:T(8,128)(2,1)S(1)} %bitcast.17, bf16[128,1024]{1,0:T(8,128)(2,1)S(1)} %bitcast.18, bf16[128,1024]{1,0:T(8,128)(2,1)S(1)} %bitcast.14, bf16[128,1024]{1,0:T(8,128)(2,1)S(1)} %bitcast.16, bf16[208,1024]{1,0:T(8,128)(2,1)S(1)} %copy-done.2), custom_call_target="tpu_custom_call" | custom-call | bytes 268435456 | tf_op jit(solution)/shard_map/pallas_call | solution.py:330
  28.8 0.0 collective-permute-done.2.r4b_ref
  28.8 2.3 %collective-permute-done.1.r4a_ref = bf16[16,1024]{1,0:T(8,128)(2,1)S(1)} collective-permute-done((bf16[16,1024]{1,0:T(8,128)(2,1)S(1)}, bf16[16,1024]{1,0:T(8,128)(2,1)S(1)}, u32[]{:S(2)}, u32[]{:S(2)}) %collective-permute-start.1) | collective-permute-done | bytes 32800 | tf_op jit(solution)/shard_map/ppermute | solution.py:343
  31.2 0.0 collective-permute-done.r3_ref
  31.2 2.8 %all-to-all-done = bf16[32,8,1024]{2,1,0:T(8,128)(2,1)S(1)} async-done(((bf16[32,8,1024]{2,1,0:T(8,128)(2,1)}), bf16[32,8,1024]{2,1,0:T(8,128)(2,1)S(1)}, u32[]{:S(2)}, u32[]{:S(2)}) %all-to-all-start) | async-done | bytes 524320 | tf_op jit(solution)/shard_map/all_to_all | solution.py:348
  33.9 1.6 %shard_map.86 = (bf16[448,1024]{1,0:T(8,128)(2,1)S(1)}, f32[16,8,128]{2,1,0:T(8,128)}) custom-call(bf16[496,1024]{1,0:T(8,128)(2,1)S(1)} %get-tuple-element.29.loc_ref, f32[128,1024]{1,0:T(8,128)S(1)} %get-tuple-element.30.near_ref, bf16[32,1024]{1,0:T(8,128)(2,1)S(1)} %collective-permute-done.r3_ref, bf16[16,1024]{1,0:T(8,128)(2,1)S(1)} %collective-permute-done.1.r4a_ref, ...), custom_call_target="tpu_custom_call" | custom-call | bytes 1048576 | tf_op jit(solution)/shard_map/pallas_call | solution.py:330
  35.5 9.5 %all-to-all-start.1 = ((f32[16,8,128]{2,1,0:T(8,128)}), f32[16,8,128]{2,1,0:T(8,128)S(1)}, u32[]{:S(2)}, u32[]{:S(2)}) async-start(f32[16,8,128]{2,1,0:T(8,128)} %get-tuple-element.39), calls=%async_computation.1 | async-start | bytes 131072 | tf_op jit(solution)/shard_map/all_to_all | solution.py:382
  45.0 0.3 shard_map.87
  45.3 2.9 %collective-permute-start.3 = (bf16[32,1024]{1,0:T(8,128)(2,1)S(1)}, bf16[32,1024]{1,0:T(8,128)(2,1)S(1)}, u32[]{:S(2)}, u32[]{:S(2)}) collective-permute-start(bf16[32,1024]{1,0:T(8,128)(2,1)S(1)} %get-tuple-element.40), channel_id=1, source_target_pairs={{0,4},{1,5},{2,6},{3,7},{4,0},{5,1},{6,2},{7,3},{8,12},{9,13},{10,... | collective-permute-start | bytes 196616 | tf_op jit(solution)/shard_map/ppermute | solution.py:343
  48.3 2.6 %shard_map.88 = (bf16[128,1024]{1,0:T(8,128)(2,1)}, f32[128,1024]{1,0:T(8,128)S(1)}, f32[128,1024]{1,0:T(8,128)S(1)}, bf16[256,640]{1,0:T(8,128)(2,1)}) custom-call(bf16[496,1024]{1,0:T(8,128)(2,1)S(1)} %get-tuple-element.29.loc_ref, bf16[448,1024]{1,0:T(8,128)(2,1)S(1)} %get-tuple-element.34.w_ref, bf16[64,1024]{1,0:T(8,128)(2,1)S(1)} %get-tuple-element.35.gf_ref), custom_call_target="tpu_custom_call" | custom-call | bytes 268435456 | tf_op jit(solution)/shard_map/pallas_call | solution.py:330
  50.9 0.0 collective-permute-done.3.r5_ref
  50.9 1.9 %all-to-all-done.1.s_ref = f32[16,8,128]{2,1,0:T(8,128)S(1)} async-done(((f32[16,8,128]{2,1,0:T(8,128)}), f32[16,8,128]{2,1,0:T(8,128)S(1)}, u32[]{:S(2)}, u32[]{:S(2)}) %all-to-all-start.1) | async-done | bytes 65568 | tf_op jit(solution)/shard_map/all_to_all | solution.py:382
  52.8 0.8 %shard_map.89 = (bf16[48,1024]{1,0:T(8,128)(2,1)S(1)}, bf16[32,1024]{1,0:T(8,128)(2,1)S(1)}, bf16[32,1024]{1,0:T(8,128)(2,1)S(1)}, bf16[256,640]{1,0:T(8,128)(2,1)}) custom-call(f32[16,8,128]{2,1,0:T(8,128)S(1)} %all-to-all-done.1.s_ref, bf16[32,1024]{1,0:T(8,128)(2,1)S(1)} %collective-permute-done.3.r5_ref, ...), custom_call_target="tpu_custom_call", output_to_operand_aliasing={{3}: (5, {})} | custom-call | bytes 1048576 | tf_op jit(solution)/shard_map/pallas_call | solution.py:330
  53.6 4.7 %all-to-all-start.2 = ((bf16[32,8,640]{2,1,0:T(8,128)(2,1)}), bf16[32,8,640]{2,1,0:T(8,128)(2,1)S(1)}, u32[]{:S(2)}, u32[]{:S(2)}) async-start(bf16[32,8,640]{2,1,0:T(8,128)(2,1)} %bitcast.6), calls=%async_computation.2 | async-start | bytes 655360 | tf_op jit(solution)/shard_map/all_to_all | solution.py:348
  58.3 3.1 %collective-permute-start.4 = (bf16[48,1024]{1,0:T(8,128)(2,1)S(1)}, bf16[48,1024]{1,0:T(8,128)(2,1)S(1)}, u32[]{:S(2)}, u32[]{:S(2)}) collective-permute-start(bf16[48,1024]{1,0:T(8,128)(2,1)S(1)} %get-tuple-element.45), channel_id=1, source_target_pairs={{0,1},{1,0},{2,3},{3,2},{4,5},{5,4},{6,7},{7,6},{8,9},{9,8},{10,11... | collective-permute-start | bytes 294920 | tf_op jit(solution)/shard_map/ppermute | solution.py:343
  61.5 4.3 %collective-permute-start.5 = (bf16[32,1024]{1,0:T(8,128)(2,1)S(1)}, bf16[32,1024]{1,0:T(8,128)(2,1)S(1)}, u32[]{:S(2)}, u32[]{:S(2)}) collective-permute-start(bf16[32,1024]{1,0:T(8,128)(2,1)S(1)} %get-tuple-element.46), channel_id=1, source_target_pairs={{0,2},{1,3},{2,0},{3,1},{4,6},{5,7},{6,4},{7,5},{8,10},{9,11},{10,... | collective-permute-start | bytes 196616 | tf_op jit(solution)/shard_map/ppermute | solution.py:343
  65.8 2.1 %collective-permute-start.6 = (bf16[32,1024]{1,0:T(8,128)(2,1)S(1)}, bf16[32,1024]{1,0:T(8,128)(2,1)S(1)}, u32[]{:S(2)}, u32[]{:S(2)}) collective-permute-start(bf16[32,1024]{1,0:T(8,128)(2,1)S(1)} %get-tuple-element.47), channel_id=1, source_target_pairs={{0,3},{1,2},{2,1},{3,0},{4,7},{5,6},{6,5},{7,4},{8,11},{9,10},{10,... | collective-permute-start | bytes 196616 | tf_op jit(solution)/shard_map/ppermute | solution.py:343
  67.9 2.5 %collective-permute-done.5.a_ref = bf16[32,1024]{1,0:T(8,128)(2,1)S(1)} collective-permute-done((bf16[32,1024]{1,0:T(8,128)(2,1)S(1)}, bf16[32,1024]{1,0:T(8,128)(2,1)S(1)}, u32[]{:S(2)}, u32[]{:S(2)}) %collective-permute-start.5) | collective-permute-done | bytes 65568 | tf_op jit(solution)/shard_map/ppermute | solution.py:343
  70.4 1.9 %collective-permute-done.6.b_ref = bf16[32,1024]{1,0:T(8,128)(2,1)S(1)} collective-permute-done((bf16[32,1024]{1,0:T(8,128)(2,1)S(1)}, bf16[32,1024]{1,0:T(8,128)(2,1)S(1)}, u32[]{:S(2)}, u32[]{:S(2)}) %collective-permute-start.6) | collective-permute-done | bytes 65568 | tf_op jit(solution)/shard_map/ppermute | solution.py:343
  72.3 0.0 collective-permute-done.4.pair_ref
  72.3 1.5 %shard_map.90 = (bf16[128,1024]{1,0:T(8,128)(2,1)}, bf16[128,1024]{1,0:T(8,128)(2,1)}, f32[1,8]{1,0:T(1,128)}) custom-call(f32[128,1024]{1,0:T(8,128)S(1)} %get-tuple-element.37.gk_ref, f32[128,1024]{1,0:T(8,128)S(1)} %get-tuple-element.38.gv_ref, bf16[48,1024]{1,0:T(8,128)(2,1)S(1)} %collective-permute-done.4.pair_ref, ...), custom_call_target="tpu_custom_call" | custom-call | bytes 1048576 | tf_op jit(solution)/shard_map/pallas_call | solution.py:330
  (9 shorter events, 0.0 us)
Async XLA Ops:
  0.6 26.4 %copy-start.3 = (bf16[1,128,1024]{2,1,0:T(8,128)(2,1)S(1)}, bf16[1,128,1024]{2,1,0:T(8,128)(2,1)}, u32[]{:S(2)}) copy-start(bf16[1,128,1024]{2,1,0:T(8,128)(2,1)} %param.5) | copy-start | bytes 786436
  3.7 13.9 %copy-start.5 = (bf16[32,1024]{1,0:T(8,128)(2,1)S(1)}, bf16[32,1024]{1,0:T(8,128)(2,1)}, u32[]{:S(2)}) copy-start(bf16[32,1024]{1,0:T(8,128)(2,1)} %get-tuple-element.31) | copy-start | bytes 196612
  3.7 17.1 %copy-start.6 = (bf16[16,1024]{1,0:T(8,128)(2,1)S(1)}, bf16[16,1024]{1,0:T(8,128)(2,1)}, u32[]{:S(2)}) copy-start(bf16[16,1024]{1,0:T(8,128)(2,1)} %get-tuple-element.32) | copy-start | bytes 98308
  3.7 23.3 %copy-start = (bf16[1,128,1024]{2,1,0:T(8,128)(2,1)S(1)}, bf16[1,128,1024]{2,1,0:T(8,128)(2,1)}, u32[]{:S(2)}) copy-start(bf16[1,128,1024]{2,1,0:T(8,128)(2,1)} %param.6) | copy-start | bytes 786436
  3.7 23.3 %copy-start.1 = (bf16[1,128,1024]{2,1,0:T(8,128)(2,1)S(1)}, bf16[1,128,1024]{2,1,0:T(8,128)(2,1)}, u32[]{:S(2)}) copy-start(bf16[1,128,1024]{2,1,0:T(8,128)(2,1)} %param.7) | copy-start | bytes 786436
  3.8 23.3 %copy-start.2 = (bf16[208,1024]{1,0:T(8,128)(2,1)S(1)}, bf16[208,1024]{1,0:T(8,128)(2,1)}, u32[]{:S(2)}) copy-start(bf16[208,1024]{1,0:T(8,128)(2,1)} %get-tuple-element.28.low_ref) | copy-start | bytes 1277956
  3.8 30.1 %all-to-all-start = ((bf16[32,8,1024]{2,1,0:T(8,128)(2,1)}), bf16[32,8,1024]{2,1,0:T(8,128)(2,1)S(1)}, u32[]{:S(2)}, u32[]{:S(2)}) async-start(bf16[32,8,1024]{2,1,0:T(8,128)(2,1)} %get-tuple-element.33), calls=%async_computation | async-start | bytes 1048576 | tf_op jit(solution)/shard_map/all_to_all | solution.py:348
  17.7 13.5 %collective-permute-start = (bf16[32,1024]{1,0:T(8,128)(2,1)S(1)}, bf16[32,1024]{1,0:T(8,128)(2,1)S(1)}, u32[]{:S(2)}, u32[]{:S(2)}) collective-permute-start(bf16[32,1024]{1,0:T(8,128)(2,1)S(1)} %copy-done.5), channel_id=1, source_target_pairs={{0,1},{1,0},{2,3},{3,2},{4,5},{5,4},{6,7},{7,6},{8,9},{9,8},{10,11... | collective-permute-start | bytes 196616 | tf_op jit(solution)/shard_map/ppermute | solution.py:343
  20.8 8.0 %collective-permute-start.2 = (bf16[16,1024]{1,0:T(8,128)(2,1)S(1)}, bf16[16,1024]{1,0:T(8,128)(2,1)S(1)}, u32[]{:S(2)}, u32[]{:S(2)}) collective-permute-start(bf16[16,1024]{1,0:T(8,128)(2,1)S(1)} %copy-done.6), channel_id=1, source_target_pairs={{0,3},{1,2},{2,1},{3,0},{4,7},{5,6},{6,5},{7,4},{8,11},{9,10},{10,... | collective-permute-start | bytes 98312 | tf_op jit(solution)/shard_map/ppermute | solution.py:343
  24.5 6.6 %collective-permute-start.1 = (bf16[16,1024]{1,0:T(8,128)(2,1)S(1)}, bf16[16,1024]{1,0:T(8,128)(2,1)S(1)}, u32[]{:S(2)}, u32[]{:S(2)}) collective-permute-start(bf16[16,1024]{1,0:T(8,128)(2,1)S(1)} %copy-done.6), channel_id=1, source_target_pairs={{0,2},{1,3},{2,0},{3,1},{4,6},{5,7},{6,4},{7,5},{8,10},{9,11},{10,... | collective-permute-start | bytes 98312 | tf_op jit(solution)/shard_map/ppermute | solution.py:343
  27.1 1.0 %copy-start.4 = (bf16[1,128,1024]{2,1,0:T(8,128)(2,1)S(1)}, bf16[1,128,1024]{2,1,0:T(8,128)(2,1)}, u32[]{:S(2)}) copy-start(bf16[1,128,1024]{2,1,0:T(8,128)(2,1)} %param.8) | copy-start | bytes 786436
  35.5 17.3 %all-to-all-start.1 = ((f32[16,8,128]{2,1,0:T(8,128)}), f32[16,8,128]{2,1,0:T(8,128)S(1)}, u32[]{:S(2)}, u32[]{:S(2)}) async-start(f32[16,8,128]{2,1,0:T(8,128)} %get-tuple-element.39), calls=%async_computation.1 | async-start | bytes 131072 | tf_op jit(solution)/shard_map/all_to_all | solution.py:382
  45.3 5.6 %collective-permute-start.3 = (bf16[32,1024]{1,0:T(8,128)(2,1)S(1)}, bf16[32,1024]{1,0:T(8,128)(2,1)S(1)}, u32[]{:S(2)}, u32[]{:S(2)}) collective-permute-start(bf16[32,1024]{1,0:T(8,128)(2,1)S(1)} %get-tuple-element.40), channel_id=1, source_target_pairs={{0,4},{1,5},{2,6},{3,7},{4,0},{5,1},{6,2},{7,3},{8,12},{9,13},{10,... | collective-permute-start | bytes 196616 | tf_op jit(solution)/shard_map/ppermute | solution.py:343
  53.6 18.7 %all-to-all-start.2 = ((bf16[32,8,640]{2,1,0:T(8,128)(2,1)}), bf16[32,8,640]{2,1,0:T(8,128)(2,1)S(1)}, u32[]{:S(2)}, u32[]{:S(2)}) async-start(bf16[32,8,640]{2,1,0:T(8,128)(2,1)} %bitcast.6), calls=%async_computation.2 | async-start | bytes 655360 | tf_op jit(solution)/shard_map/all_to_all | solution.py:348
  58.3 14.0 %collective-permute-start.4 = (bf16[48,1024]{1,0:T(8,128)(2,1)S(1)}, bf16[48,1024]{1,0:T(8,128)(2,1)S(1)}, u32[]{:S(2)}, u32[]{:S(2)}) collective-permute-start(bf16[48,1024]{1,0:T(8,128)(2,1)S(1)} %get-tuple-element.45), channel_id=1, source_target_pairs={{0,1},{1,0},{2,3},{3,2},{4,5},{5,4},{6,7},{7,6},{8,9},{9,8},{10,11... | collective-permute-start | bytes 294920 | tf_op jit(solution)/shard_map/ppermute | solution.py:343
  61.5 9.0 %collective-permute-start.5 = (bf16[32,1024]{1,0:T(8,128)(2,1)S(1)}, bf16[32,1024]{1,0:T(8,128)(2,1)S(1)}, u32[]{:S(2)}, u32[]{:S(2)}) collective-permute-start(bf16[32,1024]{1,0:T(8,128)(2,1)S(1)} %get-tuple-element.46), channel_id=1, source_target_pairs={{0,2},{1,3},{2,0},{3,1},{4,6},{5,7},{6,4},{7,5},{8,10},{9,11},{10,... | collective-permute-start | bytes 196616 | tf_op jit(solution)/shard_map/ppermute | solution.py:343
  65.8 6.5 %collective-permute-start.6 = (bf16[32,1024]{1,0:T(8,128)(2,1)S(1)}, bf16[32,1024]{1,0:T(8,128)(2,1)S(1)}, u32[]{:S(2)}, u32[]{:S(2)}) collective-permute-start(bf16[32,1024]{1,0:T(8,128)(2,1)S(1)} %get-tuple-element.47), channel_id=1, source_target_pairs={{0,3},{1,2},{2,1},{3,0},{4,7},{5,6},{6,5},{7,4},{8,11},{9,10},{10,... | collective-permute-start | bytes 196616 | tf_op jit(solution)/shard_map/ppermute | solution.py:343

commit v6 on v5

--- a/solution.py
+++ b/solution.py
@@ -208,7 +208,8 @@
         s_ref[i] = tile
 
 
-def far_grad_kernel(loc_ref, w_ref, g3_ref, g4a_ref, g4b_ref, g5_ref, gf_ref):
+def far_grad_kernel(loc_ref, w_ref, g3_ref, cross_ref, g5_ref, gf_ref):
+    upper = ((lax.axis_index("seq") >> 1) & 1) == 1
     for h in range(HEADS):
         sl = slice(h * HEAD_DIM, (h + 1) * HEAD_DIM)
         q, c = loc_ref[QUERY : QUERY + TOKENS, sl], loc_ref[COTANGENT : COTANGENT + TOKENS, sl]
@@ -216,10 +217,12 @@
         dv = mm(w_ref[PROBS + 64 : PROBS + KEYS, sl], c)
         g3_ref[0:16, sl] = dk[0:16].astype(BF16)
         g3_ref[16:32, sl] = dv[0:16].astype(BF16)
-        g4a_ref[:, sl] = jnp.concatenate([dk[16:24], dv[16:24]], axis=0).astype(BF16)
-        g4b_ref[:, sl] = jnp.concatenate([dk[24:32], dv[24:32]], axis=0).astype(BF16)
-        g5_ref[0:16, sl] = dk[32:48].astype(BF16)
-        g5_ref[16:32, sl] = dv[32:48].astype(BF16)
+        cross_ref[0:16, sl] = jnp.concatenate([dk[16:24], dv[16:24]], axis=0).astype(BF16)
+        cross_ref[16:32, sl] = jnp.concatenate([dk[24:32], dv[24:32]], axis=0).astype(BF16)
+        low = jnp.concatenate([dk[32:40], dv[32:40]], axis=0)
+        high = jnp.concatenate([dk[40:48], dv[40:48]], axis=0)
+        cross_ref[32:48, sl] = jnp.where(upper, low, high).astype(BF16)
+        g5_ref[:, sl] = jnp.where(upper, high, low).astype(BF16)
         gf_ref[0:32, sl] = dk[48:80].astype(BF16)
         gf_ref[32:64, sl] = dv[48:80].astype(BF16)
 
@@ -267,10 +270,7 @@
     slot_ref[:, HALF:] = jnp.zeros((PEERS * 8, 128), BF16)
 
 
-def slope_kernel(
-    s_ref, r5_ref, g3_ref, g4a_ref, g4b_ref, slot_in, pair_ref, a_ref, b_ref, slot_out, tile_ref, sem
-):
-    me = lax.axis_index("seq")
+def slope_kernel(s_ref, cross_ref, g5_ref, slot_in, five_ref, slot_out, tile_ref, sem):
     value = jnp.sum(jnp.sum(s_ref[...], axis=0), axis=1, keepdims=True)
     high, middle, low = three_parts(value)
     lane = lax.broadcasted_iota(jnp.int32, (HEADS, 128), 1)
@@ -280,18 +280,22 @@
     tile_ref[...] = jnp.concatenate([tile] * PEERS, axis=0).astype(BF16)
     put = pltpu.make_async_copy(tile_ref, slot_out.at[:, pl.ds(HALF, 128)], sem)
     put.start()
+    five_ref[0:16, :] = g5_ref[...]
+    five_ref[16:32, :] = cross_ref[32:48, :]
+    put.wait()
+
+
+def pair_kernel(g3_ref, cross_ref, five_ref, out_ref):
+    at = ((lax.axis_index("seq") & 1) ^ 1) * 4
+    out_ref[0:32, :] = g3_ref[...]
+    out_ref[32:48, :] = cross_ref[16:32, :]
     row, col = iota2(16, 32)
-    for apart, own_ref, out_ref in ((1, g3_ref, pair_ref), (2, g4a_ref, a_ref), (3, g4b_ref, b_ref)):
-        size = own_ref.shape[0]
-        out_ref[0:size, :] = own_ref[...]
-        at = ((me & 3) ^ apart) * 4
-        pick = ((row < 4) & (col == at + row)) | ((row >= 4) & (row < 8) & (col == at + row + 12))
-        out_ref[size : size + 16, :] = mm(mat(pick, 1.0), r5_ref[...]).astype(BF16)
-    put.wait()
+    source = ((row >> 2) & 1) * 16 + (row >> 3) * 8 + at + (row & 3)
+    out_ref[48:64, :] = mm(mat(col == source, 1.0), five_ref[...]).astype(BF16)
 
 
 def final_kernel(
-    gk_ref, gv_ref, pair_ref, a_ref, b_ref, r5_ref, r_ref, ok_ref, ov_ref, os_ref
+    gk_ref, gv_ref, pair_ref, cross_ref, five_ref, r_ref, ok_ref, ov_ref, os_ref
 ):
     me = lax.axis_index("seq")
     row, col = iota2(TOKENS, PEERS * 8)
@@ -300,19 +304,20 @@
     shift = jnp.where(apart >= 16, 7, 6)
     weight = jnp.where(apart >= 16, 2.0**-7, jnp.where(apart >= 8, 2.0**-6, 0.0))
     covers = lax.shift_right_logical(row, shift)
-    row3, col3 = iota2(TOKENS, 48)
-    row4, col4 = iota2(TOKENS, 32)
+    row1, col1 = iota2(TOKENS, 64)
+    row2, col2 = iota2(TOKENS, 48)
+    row5, col5 = iota2(TOKENS, 32)
     for out_ref, own_ref, which in ((ok_ref, gk_ref, 0), (ov_ref, gv_ref, 1)):
         near = own_ref[...]
-        three = jnp.where((row3 >> 3) + 16 * which == col3, 2.0**-3, 0.0)
-        five = jnp.where((row3 >> 5) + 32 + 4 * which == col3, 2.0**-5, 0.0)
-        near += mm((three + five).astype(BF16), pair_ref[...])
-        four = jnp.where((row4 >> 4) + 8 * which == col4, 2.0**-4, 0.0)
-        five = jnp.where((row4 >> 5) + 16 + 4 * which == col4, 2.0**-5, 0.0)
-        both = (four + five).astype(BF16)
-        near += mm(both, a_ref[...]) + mm(both, b_ref[...])
-        mine = mat((row4 >> 5) + 4 * (me & 3) + 16 * which == col4, 2.0**-5)
-        near += mm(mine, r5_ref[...])
+        three = jnp.where((row1 >> 3) + 16 * which == col1, 2.0**-3, 0.0)
+        four = jnp.where((row1 >> 4) + 32 + 8 * which == col1, 2.0**-4, 0.0)
+        held = (col1 >> 3) == 6 + which
+        five = jnp.where(held & ((row1 >> 5) == (col1 & 3)), 2.0**-5, 0.0)
+        near += mm((three + four + five).astype(BF16), pair_ref[...])
+        near += mm(mat((row2 >> 4) + 8 * which == col2, 2.0**-4), cross_ref[...])
+        held = ((col5 >> 3) & 1) == which
+        mine = held & ((col5 & 7) == (me & 1) * 4 + (row5 >> 5))
+        near += mm(mat(mine, 2.0**-5), five_ref[...])
         for half in range(2):
             sl = slice(HALF * half, HALF * half + HALF)
             far = mat(covers + 2 * which + 4 * half == line, weight)
@@ -380,12 +385,12 @@
         (loc, near, near3, near4a, near4b, far),
     )
     slopes = lax.all_to_all(slopes, "dp", 0, 0)
-    g3, g4a, g4b, g5, gf = call(
+    g3, cross, g5, gf = call(
         far_grad_kernel,
-        [((32, wide), BF16), ((16, wide), BF16), ((16, wide), BF16), ((32, wide), BF16), ((64, wide), BF16)],
+        [((32, wide), BF16), ((48, wide), BF16), ((16, wide), BF16), ((64, wide), BF16)],
         (loc, work),
     )
-    near5 = swap(g5, 4)
+    cross = swap(cross, 2)
     dq, gk, gv, slots = call(
         grad_kernel,
         [((TOKENS, wide), BF16), ((TOKENS, wide), F32), ((TOKENS, wide), F32),
@@ -393,23 +398,23 @@
         (loc, work, gf),
         cost=LONG,
     )
-    pair, four_a, four_b, slots = call(
+    five, slots = call(
         slope_kernel,
-        [((48, wide), BF16), ((32, wide), BF16), ((32, wide), BF16), ((PEERS * 8, HALF + 128), BF16)],
-        (slopes, near5, g3, g4a, g4b, slots),
-        [pltpu.VMEM] * 5 + [pl.ANY],
+        [((32, wide), BF16), ((PEERS * 8, HALF + 128), BF16)],
+        (slopes, cross, g5, slots),
         [pltpu.VMEM] * 3 + [pl.ANY],
+        [pltpu.VMEM, pl.ANY],
         [pltpu.VMEM((PEERS * 8, 128), BF16), pltpu.SemaphoreType.DMA(())],
-        alias={5: 3},
+        alias={3: 1},
     )
     far = exchange(slots)
+    five = swap(five, 4)
+    (pair,) = call(pair_kernel, [((64, wide), BF16)], (g3, cross, five))
     pair = swap(pair, 1)
-    four_a = swap(four_a, 2)
-    four_b = swap(four_b, 3)
     dk, dv, ds = call(
         final_kernel,
         [((TOKENS, wide), BF16), ((TOKENS, wide), BF16), ((1, HEADS), F32)],
-        (gk, gv, pair, four_a, four_b, near5, far),
+        (gk, gv, pair, cross, five, far),
     )
     return dq[None], dk[None], dv[None], ds.reshape(HEADS)
 

time: 74.4 us -> 77.4 us (1.040)
  the two profiles are of different devices: /device:TPU:1 before, /device:TPU:2 now
where the time goes in v6:
time: 77.4 us; the launch traced here: 76.9 us
  starting transfers between devices  46.3 us (60%)
  waiting for transfers between devices  18 us (23%)
  Pallas kernels  10.7 us (14%)
  local copies, waits for them, and re-layouts  0.98 us (1%)
  between operations  0.85 us (1%)
    ppermute x6, starting transfers between devices, swap(): return lax.ppermute(block, 'seq', [(i, i ^ apart) for i in range(PEERS)])  19.6 us
    all_to_all x2, starting transfers between devices, exchange(): back = lax.all_to_all(slots.reshape(PEERS, 8, width), 'seq', 0, 0)  19.5 us
    ppermute x6, waiting for transfers between devices, swap(): return lax.ppermute(block, 'seq', [(i, i ^ apart) for i in range(PEERS)])  15.3 us
    pallas_call x8, Pallas kernels, call(): pl.pallas_call(kernel, out_shape=[jax.ShapeDtypeStruct(s, t) for s, t in...  10.7 us
    all_to_all x1, starting transfers between devices, per_device(): slopes = lax.all_to_all(slopes, 'dp', 0, 0)  7.2 us
    all_to_all x2, waiting for transfers between devices, exchange(): back = lax.all_to_all(slots.reshape(PEERS, 8, width), 'seq', 0, 0)  2.69 us
  transfers between devices with their start and end apart: 9, of which 5 were waited for; matrix products, arithmetic and copies ran while one was open for 0% of the time, Pallas kernels for 5%

profile of v6, /device:TPU:2, one launch (start us, length us, event | category | flops | bytes accessed | tf_op | source)
XLA Modules:
  0.0 76.9 jit_solution(6425179338637357246)
XLA Ops:
  0.6 3.1 %shard_map.84 = (bf16[208,1024]{1,0:T(8,128)(2,1)}, bf16[32,1024]{1,0:T(8,128)(2,1)}, bf16[16,1024]{1,0:T(8,128)(2,1)}, bf16[32,8,1024]{2,1,0:T(8,128)(2,1)}) custom-call(bf16[128,1024]{1,0:T(8,128)(2,1)} %bitcast.13, bf16[128,1024]{1,0:T(8,128)(2,1)} %bitcast.15, f32[8]{0:T(128)} %slope_hbm.1), custom_call_target="tpu_custom_call" | custom-call | bytes 1048576 | tf_op jit(solution)/shard_map/pallas_call | solution.py:335
  3.7 0.0 copy-start.5
  3.7 0.0 copy-start.6
  3.7 0.0 copy-start
  3.8 0.0 copy-start.1
  3.8 13.6 %all-to-all-start = ((bf16[32,8,1024]{2,1,0:T(8,128)(2,1)}), bf16[32,8,1024]{2,1,0:T(8,128)(2,1)S(1)}, u32[]{:S(2)}, u32[]{:S(2)}) async-start(bf16[32,8,1024]{2,1,0:T(8,128)(2,1)} %get-tuple-element.30), calls=%async_computation | async-start | bytes 1048576 | tf_op jit(solution)/shard_map/all_to_all | solution.py:353
  17.4 2.1 %collective-permute-start = (bf16[32,1024]{1,0:T(8,128)(2,1)S(1)}, bf16[32,1024]{1,0:T(8,128)(2,1)S(1)}, u32[]{:S(2)}, u32[]{:S(2)}) collective-permute-start(bf16[32,1024]{1,0:T(8,128)(2,1)S(1)} %copy-done.5), channel_id=1, source_target_pairs={{0,1},{1,0},{2,3},{3,2},{4,5},{5,4},{6,7},{7,6},{8,9},{9,8},{10,11... | collective-permute-start | bytes 196616 | tf_op jit(solution)/shard_map/ppermute | solution.py:348
  19.6 4.3 %collective-permute-start.2 = (bf16[16,1024]{1,0:T(8,128)(2,1)S(1)}, bf16[16,1024]{1,0:T(8,128)(2,1)S(1)}, u32[]{:S(2)}, u32[]{:S(2)}) collective-permute-start(bf16[16,1024]{1,0:T(8,128)(2,1)S(1)} %copy-done.6), channel_id=1, source_target_pairs={{0,3},{1,2},{2,1},{3,0},{4,7},{5,6},{6,5},{7,4},{8,11},{9,10},{10,... | collective-permute-start | bytes 98312 | tf_op jit(solution)/shard_map/ppermute | solution.py:348
  23.9 3.4 %collective-permute-start.1 = (bf16[16,1024]{1,0:T(8,128)(2,1)S(1)}, bf16[16,1024]{1,0:T(8,128)(2,1)S(1)}, u32[]{:S(2)}, u32[]{:S(2)}) collective-permute-start(bf16[16,1024]{1,0:T(8,128)(2,1)S(1)} %copy-done.6), channel_id=1, source_target_pairs={{0,2},{1,3},{2,0},{3,1},{4,6},{5,7},{6,4},{7,5},{8,10},{9,11},{10,... | collective-permute-start | bytes 98312 | tf_op jit(solution)/shard_map/ppermute | solution.py:348
  27.3 0.0 copy-start.4
  27.3 0.9 %copy-done.4 = bf16[1,128,1024]{2,1,0:T(8,128)(2,1)S(1)} copy-done((bf16[1,128,1024]{2,1,0:T(8,128)(2,1)S(1)}, bf16[1,128,1024]{2,1,0:T(8,128)(2,1)}, u32[]{:S(2)}) %copy-start.4) | copy-done | bytes 262168
  28.3 0.8 shard_map.85
  29.0 0.0 collective-permute-done.2.r4b_ref
  29.0 2.5 %collective-permute-done.1.r4a_ref = bf16[16,1024]{1,0:T(8,128)(2,1)S(1)} collective-permute-done((bf16[16,1024]{1,0:T(8,128)(2,1)S(1)}, bf16[16,1024]{1,0:T(8,128)(2,1)S(1)}, u32[]{:S(2)}, u32[]{:S(2)}) %collective-permute-start.1) | collective-permute-done | bytes 32800 | tf_op jit(solution)/shard_map/ppermute | solution.py:348
  31.5 0.0 collective-permute-done.r3_ref
  31.5 2.7 %all-to-all-done = bf16[32,8,1024]{2,1,0:T(8,128)(2,1)S(1)} async-done(((bf16[32,8,1024]{2,1,0:T(8,128)(2,1)}), bf16[32,8,1024]{2,1,0:T(8,128)(2,1)S(1)}, u32[]{:S(2)}, u32[]{:S(2)}) %all-to-all-start) | async-done | bytes 524320 | tf_op jit(solution)/shard_map/all_to_all | solution.py:353
  34.2 1.6 %shard_map.86 = (bf16[448,1024]{1,0:T(8,128)(2,1)S(1)}, f32[16,8,128]{2,1,0:T(8,128)}) custom-call(bf16[496,1024]{1,0:T(8,128)(2,1)S(1)} %get-tuple-element.26.loc_ref, f32[128,1024]{1,0:T(8,128)S(1)} %get-tuple-element.27.near_ref, bf16[32,1024]{1,0:T(8,128)(2,1)S(1)} %collective-permute-done.r3_ref, bf16[16,1024]{1,0:T(8,128)(2,1)S(1)} %collective-permute-done.1.r4a_ref, ...), custom_call_target="tpu_custom_call" | custom-call | bytes 1048576 | tf_op jit(solution)/shard_map/pallas_call | solution.py:335
  35.8 7.2 %all-to-all-start.1 = ((f32[16,8,128]{2,1,0:T(8,128)}), f32[16,8,128]{2,1,0:T(8,128)S(1)}, u32[]{:S(2)}, u32[]{:S(2)}) async-start(f32[16,8,128]{2,1,0:T(8,128)} %get-tuple-element.38), calls=%async_computation.1 | async-start | bytes 131072 | tf_op jit(solution)/shard_map/all_to_all | solution.py:387
  43.0 0.3 shard_map.87
  43.4 4.0 %collective-permute-start.3 = (bf16[48,1024]{1,0:T(8,128)(2,1)S(1)}, bf16[48,1024]{1,0:T(8,128)(2,1)S(1)}, u32[]{:S(2)}, u32[]{:S(2)}) collective-permute-start(bf16[48,1024]{1,0:T(8,128)(2,1)S(1)} %get-tuple-element.37), channel_id=1, source_target_pairs={{0,2},{1,3},{2,0},{3,1},{4,6},{5,7},{6,4},{7,5},{8,10},{9,11},{10,... | collective-permute-start | bytes 294920 | tf_op jit(solution)/shard_map/ppermute | solution.py:348
  47.4 2.6 %shard_map.88 = (bf16[128,1024]{1,0:T(8,128)(2,1)}, f32[128,1024]{1,0:T(8,128)S(1)}, f32[128,1024]{1,0:T(8,128)S(1)}, bf16[256,640]{1,0:T(8,128)(2,1)}) custom-call(bf16[496,1024]{1,0:T(8,128)(2,1)S(1)} %get-tuple-element.26.loc_ref, bf16[448,1024]{1,0:T(8,128)(2,1)S(1)} %get-tuple-element.31.w_ref, bf16[64,1024]{1,0:T(8,128)(2,1)S(1)} %get-tuple-element.32.gf_ref), custom_call_target="tpu_custom_call" | custom-call | bytes 268435456 | tf_op jit(solution)/shard_map/pallas_call | solution.py:335
  50.0 1.9 %collective-permute-done.3.cross_ref = bf16[48,1024]{1,0:T(8,128)(2,1)S(1)} collective-permute-done((bf16[48,1024]{1,0:T(8,128)(2,1)S(1)}, bf16[48,1024]{1,0:T(8,128)(2,1)S(1)}, u32[]{:S(2)}, u32[]{:S(2)}) %collective-permute-start.3) | collective-permute-done | bytes 98336 | tf_op jit(solution)/shard_map/ppermute | solution.py:348
  51.9 0.0 all-to-all-done.1.s_ref
  51.9 0.8 shard_map.89
  52.7 5.9 %all-to-all-start.2 = ((bf16[32,8,640]{2,1,0:T(8,128)(2,1)}), bf16[32,8,640]{2,1,0:T(8,128)(2,1)S(1)}, u32[]{:S(2)}, u32[]{:S(2)}) async-start(bf16[32,8,640]{2,1,0:T(8,128)(2,1)} %bitcast.6), calls=%async_computation.2 | async-start | bytes 655360 | tf_op jit(solution)/shard_map/all_to_all | solution.py:353
  58.6 3.4 %collective-permute-start.4 = (bf16[32,1024]{1,0:T(8,128)(2,1)S(1)}, bf16[32,1024]{1,0:T(8,128)(2,1)S(1)}, u32[]{:S(2)}, u32[]{:S(2)}) collective-permute-start(bf16[32,1024]{1,0:T(8,128)(2,1)S(1)} %get-tuple-element.41), channel_id=1, source_target_pairs={{0,4},{1,5},{2,6},{3,7},{4,0},{5,1},{6,2},{7,3},{8,12},{9,13},{10,... | collective-permute-start | bytes 196616 | tf_op jit(solution)/shard_map/ppermute | solution.py:348
  61.9 6.5 %collective-permute-done.4.five_ref = bf16[32,1024]{1,0:T(8,128)(2,1)S(1)} collective-permute-done((bf16[32,1024]{1,0:T(8,128)(2,1)S(1)}, bf16[32,1024]{1,0:T(8,128)(2,1)S(1)}, u32[]{:S(2)}, u32[]{:S(2)}) %collective-permute-start.4) | collective-permute-done | bytes 65568 | tf_op jit(solution)/shard_map/ppermute | solution.py:348
  68.5 0.1 shard_map.90
  68.6 2.5 %collective-permute-start.5 = (bf16[64,1024]{1,0:T(8,128)(2,1)S(1)}, bf16[64,1024]{1,0:T(8,128)(2,1)S(1)}, u32[]{:S(2)}, u32[]{:S(2)}) collective-permute-start(bf16[64,1024]{1,0:T(8,128)(2,1)S(1)} %shard_map.90), channel_id=1, source_target_pairs={{0,1},{1,0},{2,3},{3,2},{4,5},{5,4},{6,7},{7,6},{8,9},{9,8},{10,11... | collective-permute-start | bytes 393224 | tf_op jit(solution)/shard_map/ppermute | solution.py:348
  71.1 4.4 %collective-permute-done.5.pair_ref = bf16[64,1024]{1,0:T(8,128)(2,1)S(1)} collective-permute-done((bf16[64,1024]{1,0:T(8,128)(2,1)S(1)}, bf16[64,1024]{1,0:T(8,128)(2,1)S(1)}, u32[]{:S(2)}, u32[]{:S(2)}) %collective-permute-start.5) | collective-permute-done | bytes 131104 | tf_op jit(solution)/shard_map/ppermute | solution.py:348
  75.5 0.0 all-to-all-done.2
  75.5 1.4 %shard_map.91 = (bf16[128,1024]{1,0:T(8,128)(2,1)}, bf16[128,1024]{1,0:T(8,128)(2,1)}, f32[1,8]{1,0:T(1,128)}) custom-call(f32[128,1024]{1,0:T(8,128)S(1)} %get-tuple-element.34.gk_ref, f32[128,1024]{1,0:T(8,128)S(1)} %get-tuple-element.35.gv_ref, bf16[64,1024]{1,0:T(8,128)(2,1)S(1)} %collective-permute-done.5.pair_ref, ...), custom_call_target="tpu_custom_call" | custom-call | bytes 1048576 | tf_op jit(solution)/shard_map/pallas_call | solution.py:335
  (8 shorter events, 0.0 us)
Async XLA Ops:
  0.6 26.6 %copy-start.3 = (bf16[1,128,1024]{2,1,0:T(8,128)(2,1)S(1)}, bf16[1,128,1024]{2,1,0:T(8,128)(2,1)}, u32[]{:S(2)}) copy-start(bf16[1,128,1024]{2,1,0:T(8,128)(2,1)} %param.5) | copy-start | bytes 786436
  3.7 13.7 %copy-start.5 = (bf16[32,1024]{1,0:T(8,128)(2,1)S(1)}, bf16[32,1024]{1,0:T(8,128)(2,1)}, u32[]{:S(2)}) copy-start(bf16[32,1024]{1,0:T(8,128)(2,1)} %get-tuple-element.28) | copy-start | bytes 196612
  3.7 15.8 %copy-start.6 = (bf16[16,1024]{1,0:T(8,128)(2,1)S(1)}, bf16[16,1024]{1,0:T(8,128)(2,1)}, u32[]{:S(2)}) copy-start(bf16[16,1024]{1,0:T(8,128)(2,1)} %get-tuple-element.29) | copy-start | bytes 98308
  3.7 23.5 %copy-start = (bf16[1,128,1024]{2,1,0:T(8,128)(2,1)S(1)}, bf16[1,128,1024]{2,1,0:T(8,128)(2,1)}, u32[]{:S(2)}) copy-start(bf16[1,128,1024]{2,1,0:T(8,128)(2,1)} %param.6) | copy-start | bytes 786436
  3.8 23.5 %copy-start.1 = (bf16[1,128,1024]{2,1,0:T(8,128)(2,1)S(1)}, bf16[1,128,1024]{2,1,0:T(8,128)(2,1)}, u32[]{:S(2)}) copy-start(bf16[1,128,1024]{2,1,0:T(8,128)(2,1)} %param.7) | copy-start | bytes 786436
  3.8 23.5 %copy-start.2 = (bf16[208,1024]{1,0:T(8,128)(2,1)S(1)}, bf16[208,1024]{1,0:T(8,128)(2,1)}, u32[]{:S(2)}) copy-start(bf16[208,1024]{1,0:T(8,128)(2,1)} %get-tuple-element.25.low_ref) | copy-start | bytes 1277956
  3.8 30.4 %all-to-all-start = ((bf16[32,8,1024]{2,1,0:T(8,128)(2,1)}), bf16[32,8,1024]{2,1,0:T(8,128)(2,1)S(1)}, u32[]{:S(2)}, u32[]{:S(2)}) async-start(bf16[32,8,1024]{2,1,0:T(8,128)(2,1)} %get-tuple-element.30), calls=%async_computation | async-start | bytes 1048576 | tf_op jit(solution)/shard_map/all_to_all | solution.py:353
  17.4 14.1 %collective-permute-start = (bf16[32,1024]{1,0:T(8,128)(2,1)S(1)}, bf16[32,1024]{1,0:T(8,128)(2,1)S(1)}, u32[]{:S(2)}, u32[]{:S(2)}) collective-permute-start(bf16[32,1024]{1,0:T(8,128)(2,1)S(1)} %copy-done.5), channel_id=1, source_target_pairs={{0,1},{1,0},{2,3},{3,2},{4,5},{5,4},{6,7},{7,6},{8,9},{9,8},{10,11... | collective-permute-start | bytes 196616 | tf_op jit(solution)/shard_map/ppermute | solution.py:348
  19.6 9.5 %collective-permute-start.2 = (bf16[16,1024]{1,0:T(8,128)(2,1)S(1)}, bf16[16,1024]{1,0:T(8,128)(2,1)S(1)}, u32[]{:S(2)}, u32[]{:S(2)}) collective-permute-start(bf16[16,1024]{1,0:T(8,128)(2,1)S(1)} %copy-done.6), channel_id=1, source_target_pairs={{0,3},{1,2},{2,1},{3,0},{4,7},{5,6},{6,5},{7,4},{8,11},{9,10},{10,... | collective-permute-start | bytes 98312 | tf_op jit(solution)/shard_map/ppermute | solution.py:348
  23.9 7.7 %collective-permute-start.1 = (bf16[16,1024]{1,0:T(8,128)(2,1)S(1)}, bf16[16,1024]{1,0:T(8,128)(2,1)S(1)}, u32[]{:S(2)}, u32[]{:S(2)}) collective-permute-start(bf16[16,1024]{1,0:T(8,128)(2,1)S(1)} %copy-done.6), channel_id=1, source_target_pairs={{0,2},{1,3},{2,0},{3,1},{4,6},{5,7},{6,4},{7,5},{8,10},{9,11},{10,... | collective-permute-start | bytes 98312 | tf_op jit(solution)/shard_map/ppermute | solution.py:348
  27.3 1.0 %copy-start.4 = (bf16[1,128,1024]{2,1,0:T(8,128)(2,1)S(1)}, bf16[1,128,1024]{2,1,0:T(8,128)(2,1)}, u32[]{:S(2)}) copy-start(bf16[1,128,1024]{2,1,0:T(8,128)(2,1)} %param.8) | copy-start | bytes 786436
  35.8 16.1 %all-to-all-start.1 = ((f32[16,8,128]{2,1,0:T(8,128)}), f32[16,8,128]{2,1,0:T(8,128)S(1)}, u32[]{:S(2)}, u32[]{:S(2)}) async-start(f32[16,8,128]{2,1,0:T(8,128)} %get-tuple-element.38), calls=%async_computation.1 | async-start | bytes 131072 | tf_op jit(solution)/shard_map/all_to_all | solution.py:387
  43.4 8.5 %collective-permute-start.3 = (bf16[48,1024]{1,0:T(8,128)(2,1)S(1)}, bf16[48,1024]{1,0:T(8,128)(2,1)S(1)}, u32[]{:S(2)}, u32[]{:S(2)}) collective-permute-start(bf16[48,1024]{1,0:T(8,128)(2,1)S(1)} %get-tuple-element.37), channel_id=1, source_target_pairs={{0,2},{1,3},{2,0},{3,1},{4,6},{5,7},{6,4},{7,5},{8,10},{9,11},{10,... | collective-permute-start | bytes 294920 | tf_op jit(solution)/shard_map/ppermute | solution.py:348
  52.7 22.8 %all-to-all-start.2 = ((bf16[32,8,640]{2,1,0:T(8,128)(2,1)}), bf16[32,8,640]{2,1,0:T(8,128)(2,1)S(1)}, u32[]{:S(2)}, u32[]{:S(2)}) async-start(bf16[32,8,640]{2,1,0:T(8,128)(2,1)} %bitcast.6), calls=%async_computation.2 | async-start | bytes 655360 | tf_op jit(solution)/shard_map/all_to_all | solution.py:353
  58.6 9.9 %collective-permute-start.4 = (bf16[32,1024]{1,0:T(8,128)(2,1)S(1)}, bf16[32,1024]{1,0:T(8,128)(2,1)S(1)}, u32[]{:S(2)}, u32[]{:S(2)}) collective-permute-start(bf16[32,1024]{1,0:T(8,128)(2,1)S(1)} %get-tuple-element.41), channel_id=1, source_target_pairs={{0,4},{1,5},{2,6},{3,7},{4,0},{5,1},{6,2},{7,3},{8,12},{9,13},{10,... | collective-permute-start | bytes 196616 | tf_op jit(solution)/shard_map/ppermute | solution.py:348
  68.6 6.9 %collective-permute-start.5 = (bf16[64,1024]{1,0:T(8,128)(2,1)S(1)}, bf16[64,1024]{1,0:T(8,128)(2,1)S(1)}, u32[]{:S(2)}, u32[]{:S(2)}) collective-permute-start(bf16[64,1024]{1,0:T(8,128)(2,1)S(1)} %shard_map.90), channel_id=1, source_target_pairs={{0,1},{1,0},{2,3},{3,2},{4,5},{5,4},{6,7},{7,6},{8,9},{9,8},{10,11... | collective-permute-start | bytes 393224 | tf_op jit(solution)/shard_map/ppermute | solution.py:348

commit v7 on v5

--- a/solution.py
+++ b/solution.py
@@ -49,8 +49,6 @@
 
 
 LOCAL = 224
-COARSE = 96
-STEP = 2 * COARSE
 REMOTE = 80
 PROBS = 2 * REMOTE
 DSCORES = PROBS + KEYS
@@ -60,32 +58,19 @@
 STEPS = LOCAL + 2 * TOKENS
 
 
-def pool_kernel(
-    k_hbm, v_hbm, slope_hbm, low_ref, l3_ref, l4_ref, slot_ref, k_ref, v_ref, slope_ref, sems
-):
+def pool_kernel(k_hbm, v_hbm, l3_ref, l4_ref, slot_ref, k_ref, v_ref, sems):
     me = lax.axis_index("seq")
     fetch_k = pltpu.make_async_copy(k_hbm, k_ref, sems.at[0])
     fetch_v = pltpu.make_async_copy(v_hbm, v_ref, sems.at[1])
-    fetch_slope = pltpu.make_async_copy(slope_hbm, slope_ref, sems.at[2])
     fetch_k.start()
     fetch_v.start()
-    fetch_slope.start()
     half = pooling(64, 128)
     quarter = pooling(32, 64)
-    fetch_slope.wait()
-    line = lax.broadcasted_iota(jnp.int32, (16, HEAD_DIM), 0)
-    for h in range(HEADS):
-        high, middle, low = three_parts(jnp.full((16, HEAD_DIM), LOG_TWO + slope_ref[h], F32))
-        part = jnp.where(line == 0, high, jnp.where(line == 1, middle, jnp.where(line == 2, low, 0.0)))
-        low_ref[STEP : STEP + 16, h * HEAD_DIM : (h + 1) * HEAD_DIM] = part.astype(BF16)
     l2 = []
-    for fetch, held, at in ((fetch_k, k_ref, 0), (fetch_v, v_ref, COARSE)):
+    for fetch, held in ((fetch_k, k_ref), (fetch_v, v_ref)):
         fetch.wait()
         one = mm(half, held[...]).astype(BF16)
-        low_ref[at : at + 64, :] = one
-        two = mm(quarter, one).astype(BF16)
-        low_ref[at + 64 : at + 96, :] = two
-        l2.append(two)
+        l2.append(mm(quarter, one).astype(BF16))
     l3 = mm(quarter, jnp.concatenate(l2, axis=0)).astype(BF16)
     l3_ref[...] = l3
     l4 = mm(pooling(16, 32), l3).astype(BF16)
@@ -119,19 +104,24 @@
     return jnp.where(line < 16, at5, jnp.where(line < 32, at6, at7))
 
 
-def local_kernel(q_hbm, c_hbm, k_hbm, v_hbm, low_ref, loc_ref, s_ref, v_ref, sems):
+def local_kernel(q_hbm, c_hbm, k_hbm, v_hbm, slope_hbm, loc_ref, s_ref, v_ref, slope_ref, sems):
     moves = (
         (k_hbm, loc_ref.at[pl.ds(0, TOKENS)]),
         (q_hbm, loc_ref.at[pl.ds(QUERY, TOKENS)]),
         (v_hbm, v_ref.at[pl.ds(0, TOKENS)]),
         (c_hbm, loc_ref.at[pl.ds(COTANGENT, TOKENS)]),
+        (slope_hbm, slope_ref),
     )
     fetches = [pltpu.make_async_copy(a, b, sems.at[i]) for i, (a, b) in enumerate(moves)]
     for fetch in fetches:
         fetch.start()
-    loc_ref[TOKENS:LOCAL, :] = low_ref[0:COARSE, :]
-    v_ref[TOKENS:LOCAL, :] = low_ref[COARSE : 2 * COARSE, :]
-    loc_ref[STEPS : STEPS + 16, :] = low_ref[STEP : STEP + 16, :]
+    part_at = lax.broadcasted_iota(jnp.int32, (16, HEAD_DIM), 0)
+    fetches[4].wait()
+    for h in range(HEADS):
+        high, middle, low = three_parts(jnp.full((16, HEAD_DIM), LOG_TWO + slope_ref[h], F32))
+        part = jnp.where(part_at == 1, middle, jnp.where(part_at == 2, low, 0.0))
+        part = jnp.where(part_at == 0, high, part)
+        loc_ref[STEPS : STEPS + 16, h * HEAD_DIM : (h + 1) * HEAD_DIM] = part.astype(BF16)
     lane = lax.broadcasted_iota(jnp.int32, (1, TOKENS), 1)
     quarter = lane >> 5
     lower = lane < 64
@@ -150,9 +140,13 @@
         two = jnp.where(lower, full[208:224], full[192:208])
         return zero, one, two
 
-    step_all = jnp.sum(low_ref[STEP : STEP + 16, :].astype(F32), axis=0, keepdims=True)
+    step_all = jnp.sum(loc_ref[STEPS : STEPS + 16, :].astype(F32), axis=0, keepdims=True)
+    half_mat, quarter_mat = pooling(64, 128), pooling(32, 64)
     for which, (held, at) in enumerate(((loc_ref, QUERY), (v_ref, COTANGENT))):
         fetches[2 * which].wait()
+        one = mm(half_mat, held[0:TOKENS, :]).astype(BF16)
+        held[TOKENS : TOKENS + 64, :] = one
+        held[TOKENS + 64 : LOCAL, :] = mm(quarter_mat, one).astype(BF16)
         fetches[2 * which + 1].wait()
         for h in range(HEADS):
             sl = slice(h * HEAD_DIM, (h + 1) * HEAD_DIM)
@@ -353,12 +347,12 @@
     q, k, v, c = queries[0], keys_in[0], values_in[0], cotangent[0]
     wide = WIDTH
     block = pltpu.VMEM((TOKENS, wide), BF16)
-    low, l3, l4, slots = call(
+    l3, l4, slots = call(
         pool_kernel,
-        [((STEP + 16, wide), BF16), ((32, wide), BF16), ((16, wide), BF16), ((PEERS, 8, wide), BF16)],
-        (k, v, level_slope),
-        [pl.ANY] * 3,
-        scratch=[block, block, pltpu.SMEM((HEADS,), F32), pltpu.SemaphoreType.DMA((3,))],
+        [((32, wide), BF16), ((16, wide), BF16), ((PEERS, 8, wide), BF16)],
+        (k, v),
+        [pl.ANY] * 2,
+        scratch=[block, block, pltpu.SemaphoreType.DMA((2,))],
         vmem=58,
     )
     far = exchange(slots)
@@ -368,9 +362,10 @@
     loc, near = call(
         local_kernel,
         [((STEPS + 16, wide), BF16), ((128, wide), F32)],
-        (q, c, k, v, low),
-        [pl.ANY] * 4 + [pltpu.VMEM],
-        scratch=[pltpu.VMEM((LOCAL, wide), BF16), pltpu.SemaphoreType.DMA((4,))],
+        (q, c, k, v, level_slope),
+        [pl.ANY] * 5,
+        scratch=[pltpu.VMEM((LOCAL, wide), BF16), pltpu.SMEM((HEADS,), F32),
+                 pltpu.SemaphoreType.DMA((5,))],
         cost=LONG,
     )
     groups = lax.axis_size("dp")

time: 74.4 us -> 74.5 us (level)
  Pallas kernels: 10.7 us -> 11.8 us
  waiting for transfers between devices: 11.4 us -> 10.5 us
    pallas_call x7, Pallas kernels: 10.7 us -> 11.8 us  [call(): pl.pallas_call(kernel, out_shape=[jax.ShapeDtypeStruct(s, t) for s, t in...]
    ppermute x7, waiting for transfers between devices: 6.69 us -> 5.92 us  [swap(): return lax.ppermute(block, 'seq', [(i, i ^ apart) for i in range(PEERS)])]
  transfers between devices with their start and end apart: 10 -> 10, of which waited for: 5 -> 5; matrix products, arithmetic and copies ran while one was open for 0% -> 0% of each run, Pallas kernels for 5% -> 7%
where the time goes in v7:
time: 74.5 us; the launch traced here: 73.9 us
  starting transfers between devices  50.1 us (67%)
  Pallas kernels  11.8 us (16%)
  waiting for transfers between devices  10.5 us (14%)
  between operations  0.82 us (1%)
    ppermute x7, starting transfers between devices, swap(): return lax.ppermute(block, 'seq', [(i, i ^ apart) for i in range(PEERS)])  21.9 us
    all_to_all x2, starting transfers between devices, exchange(): back = lax.all_to_all(slots.reshape(PEERS, 8, width), 'seq', 0, 0)  18.7 us
    pallas_call x7, Pallas kernels, call(): pl.pallas_call(kernel, out_shape=[jax.ShapeDtypeStruct(s, t) for s, t in...  11.8 us
    all_to_all x1, starting transfers between devices, per_device(): slopes = lax.all_to_all(slopes, 'dp', 0, 0)  9.52 us
    ppermute x7, waiting for transfers between devices, swap(): return lax.ppermute(block, 'seq', [(i, i ^ apart) for i in range(PEERS)])  5.92 us
    all_to_all x2, waiting for transfers between devices, exchange(): back = lax.all_to_all(slots.reshape(PEERS, 8, width), 'seq', 0, 0)  2.72 us
    all_to_all x1, waiting for transfers between devices, per_device(): slopes = lax.all_to_all(slopes, 'dp', 0, 0)  1.9 us
  transfers between devices with their start and end apart: 10, of which 5 were waited for; matrix products, arithmetic and copies ran while one was open for 0% of the time, Pallas kernels for 7%

profile of v7, /device:TPU:1, one launch (start us, length us, event | category | flops | bytes accessed | tf_op | source)
XLA Modules:
  0.0 73.9 jit_solution(4822971259091880875)
XLA Ops:
  0.6 3.0 %shard_map.85 = (bf16[32,1024]{1,0:T(8,128)(2,1)}, bf16[16,1024]{1,0:T(8,128)(2,1)}, bf16[32,8,1024]{2,1,0:T(8,128)(2,1)}) custom-call(bf16[128,1024]{1,0:T(8,128)(2,1)} %bitcast.13, bf16[128,1024]{1,0:T(8,128)(2,1)} %bitcast.15), custom_call_target="tpu_custom_call" | custom-call | bytes 1048576 | tf_op jit(solution)/shard_map/pallas_call | solution.py:324
  3.7 0.0 copy-start
  3.7 0.0 copy-start.1
  3.7 0.0 copy-start.2
  3.7 0.0 copy-start.3
  3.7 13.9 %all-to-all-start = ((bf16[32,8,1024]{2,1,0:T(8,128)(2,1)}), bf16[32,8,1024]{2,1,0:T(8,128)(2,1)S(1)}, u32[]{:S(2)}, u32[]{:S(2)}) async-start(bf16[32,8,1024]{2,1,0:T(8,128)(2,1)} %get-tuple-element.31), calls=%async_computation | async-start | bytes 1048576 | tf_op jit(solution)/shard_map/all_to_all | solution.py:342
  17.6 3.1 %collective-permute-start = (bf16[32,1024]{1,0:T(8,128)(2,1)}, bf16[32,1024]{1,0:T(8,128)(2,1)S(1)}, u32[]{:S(2)}, u32[]{:S(2)}) collective-permute-start(bf16[32,1024]{1,0:T(8,128)(2,1)} %get-tuple-element.29), channel_id=1, source_target_pairs={{0,1},{1,0},{2,3},{3,2},{4,5},{5,4},{6,7},{7,6},{8,9},{9,8},{10,11... | collective-permute-start | bytes 196616 | tf_op jit(solution)/shard_map/ppermute | solution.py:337
  20.7 3.7 %collective-permute-start.2 = (bf16[16,1024]{1,0:T(8,128)(2,1)}, bf16[16,1024]{1,0:T(8,128)(2,1)S(1)}, u32[]{:S(2)}, u32[]{:S(2)}) collective-permute-start(bf16[16,1024]{1,0:T(8,128)(2,1)} %get-tuple-element.30), channel_id=1, source_target_pairs={{0,3},{1,2},{2,1},{3,0},{4,7},{5,6},{6,5},{7,4},{8,11},{9,10},{10,... | collective-permute-start | bytes 98312 | tf_op jit(solution)/shard_map/ppermute | solution.py:337
  24.4 2.5 %collective-permute-start.1 = (bf16[16,1024]{1,0:T(8,128)(2,1)}, bf16[16,1024]{1,0:T(8,128)(2,1)S(1)}, u32[]{:S(2)}, u32[]{:S(2)}) collective-permute-start(bf16[16,1024]{1,0:T(8,128)(2,1)} %get-tuple-element.30), channel_id=1, source_target_pairs={{0,2},{1,3},{2,0},{3,1},{4,6},{5,7},{6,4},{7,5},{8,10},{9,11},{10,... | collective-permute-start | bytes 98312 | tf_op jit(solution)/shard_map/ppermute | solution.py:337
  27.0 0.0 copy-start.4
  27.0 0.6 copy-done.4
  27.6 1.9 %shard_map.84 = (bf16[496,1024]{1,0:T(8,128)(2,1)S(1)}, f32[128,1024]{1,0:T(8,128)S(1)}) custom-call(bf16[128,1024]{1,0:T(8,128)(2,1)S(1)} %bitcast.17, bf16[128,1024]{1,0:T(8,128)(2,1)S(1)} %bitcast.18, bf16[128,1024]{1,0:T(8,128)(2,1)S(1)} %bitcast.14, bf16[128,1024]{1,0:T(8,128)(2,1)S(1)} %bitcast.16, f32[8]{0:T(128)S(1)} %copy-done.4), custom_call_target="tpu_custom_call" | custom-call | bytes 268435456 | tf_op jit(solution)/shard_map/pallas_call | solution.py:324
  29.6 0.0 collective-permute-done.2.r4b_ref
  29.6 1.5 %collective-permute-done.1.r4a_ref = bf16[16,1024]{1,0:T(8,128)(2,1)S(1)} collective-permute-done((bf16[16,1024]{1,0:T(8,128)(2,1)}, bf16[16,1024]{1,0:T(8,128)(2,1)S(1)}, u32[]{:S(2)}, u32[]{:S(2)}) %collective-permute-start.1) | collective-permute-done | bytes 32800 | tf_op jit(solution)/shard_map/ppermute | solution.py:337
  31.1 0.0 collective-permute-done.r3_ref
  31.1 2.7 %all-to-all-done = bf16[32,8,1024]{2,1,0:T(8,128)(2,1)S(1)} async-done(((bf16[32,8,1024]{2,1,0:T(8,128)(2,1)}), bf16[32,8,1024]{2,1,0:T(8,128)(2,1)S(1)}, u32[]{:S(2)}, u32[]{:S(2)}) %all-to-all-start) | async-done | bytes 524320 | tf_op jit(solution)/shard_map/all_to_all | solution.py:342
  33.8 1.6 %shard_map.86 = (bf16[448,1024]{1,0:T(8,128)(2,1)S(1)}, f32[16,8,128]{2,1,0:T(8,128)}) custom-call(bf16[496,1024]{1,0:T(8,128)(2,1)S(1)} %get-tuple-element.27.loc_ref, f32[128,1024]{1,0:T(8,128)S(1)} %get-tuple-element.28.near_ref, bf16[32,1024]{1,0:T(8,128)(2,1)S(1)} %collective-permute-done.r3_ref, bf16[16,1024]{1,0:T(8,128)(2,1)S(1)} %collective-permute-done.1.r4a_ref, ...), custom_call_target="tpu_custom_call" | custom-call | bytes 1048576 | tf_op jit(solution)/shard_map/pallas_call | solution.py:324
  35.4 9.5 %all-to-all-start.1 = ((f32[16,8,128]{2,1,0:T(8,128)}), f32[16,8,128]{2,1,0:T(8,128)S(1)}, u32[]{:S(2)}, u32[]{:S(2)}) async-start(f32[16,8,128]{2,1,0:T(8,128)} %get-tuple-element.37), calls=%async_computation.1 | async-start | bytes 131072 | tf_op jit(solution)/shard_map/all_to_all | solution.py:377
  45.0 0.3 shard_map.87
  45.3 2.9 %collective-permute-start.3 = (bf16[32,1024]{1,0:T(8,128)(2,1)S(1)}, bf16[32,1024]{1,0:T(8,128)(2,1)S(1)}, u32[]{:S(2)}, u32[]{:S(2)}) collective-permute-start(bf16[32,1024]{1,0:T(8,128)(2,1)S(1)} %get-tuple-element.38), channel_id=1, source_target_pairs={{0,4},{1,5},{2,6},{3,7},{4,0},{5,1},{6,2},{7,3},{8,12},{9,13},{10,... | collective-permute-start | bytes 196616 | tf_op jit(solution)/shard_map/ppermute | solution.py:337
  48.2 2.6 %shard_map.88 = (bf16[128,1024]{1,0:T(8,128)(2,1)}, f32[128,1024]{1,0:T(8,128)S(1)}, f32[128,1024]{1,0:T(8,128)S(1)}, bf16[256,640]{1,0:T(8,128)(2,1)}) custom-call(bf16[496,1024]{1,0:T(8,128)(2,1)S(1)} %get-tuple-element.27.loc_ref, bf16[448,1024]{1,0:T(8,128)(2,1)S(1)} %get-tuple-element.32.w_ref, bf16[64,1024]{1,0:T(8,128)(2,1)S(1)} %get-tuple-element.33.gf_ref), custom_call_target="tpu_custom_call" | custom-call | bytes 268435456 | tf_op jit(solution)/shard_map/pallas_call | solution.py:324
  50.9 1.9 %all-to-all-done.1.s_ref = f32[16,8,128]{2,1,0:T(8,128)S(1)} async-done(((f32[16,8,128]{2,1,0:T(8,128)}), f32[16,8,128]{2,1,0:T(8,128)S(1)}, u32[]{:S(2)}, u32[]{:S(2)}) %all-to-all-start.1) | async-done | bytes 65568 | tf_op jit(solution)/shard_map/all_to_all | solution.py:377
  52.8 0.8 %shard_map.89 = (bf16[48,1024]{1,0:T(8,128)(2,1)S(1)}, bf16[32,1024]{1,0:T(8,128)(2,1)S(1)}, bf16[32,1024]{1,0:T(8,128)(2,1)S(1)}, bf16[256,640]{1,0:T(8,128)(2,1)}) custom-call(f32[16,8,128]{2,1,0:T(8,128)S(1)} %all-to-all-done.1.s_ref, bf16[32,1024]{1,0:T(8,128)(2,1)S(1)} %collective-permute-done.3.r5_ref, ...), custom_call_target="tpu_custom_call", output_to_operand_aliasing={{3}: (5, {})} | custom-call | bytes 1048576 | tf_op jit(solution)/shard_map/pallas_call | solution.py:324
  53.5 4.9 %all-to-all-start.2 = ((bf16[32,8,640]{2,1,0:T(8,128)(2,1)}), bf16[32,8,640]{2,1,0:T(8,128)(2,1)S(1)}, u32[]{:S(2)}, u32[]{:S(2)}) async-start(bf16[32,8,640]{2,1,0:T(8,128)(2,1)} %bitcast.6), calls=%async_computation.2 | async-start | bytes 655360 | tf_op jit(solution)/shard_map/all_to_all | solution.py:342
  58.4 3.1 %collective-permute-start.4 = (bf16[48,1024]{1,0:T(8,128)(2,1)S(1)}, bf16[48,1024]{1,0:T(8,128)(2,1)S(1)}, u32[]{:S(2)}, u32[]{:S(2)}) collective-permute-start(bf16[48,1024]{1,0:T(8,128)(2,1)S(1)} %get-tuple-element.43), channel_id=1, source_target_pairs={{0,1},{1,0},{2,3},{3,2},{4,5},{5,4},{6,7},{7,6},{8,9},{9,8},{10,11... | collective-permute-start | bytes 294920 | tf_op jit(solution)/shard_map/ppermute | solution.py:337
  61.6 4.3 %collective-permute-start.5 = (bf16[32,1024]{1,0:T(8,128)(2,1)S(1)}, bf16[32,1024]{1,0:T(8,128)(2,1)S(1)}, u32[]{:S(2)}, u32[]{:S(2)}) collective-permute-start(bf16[32,1024]{1,0:T(8,128)(2,1)S(1)} %get-tuple-element.44), channel_id=1, source_target_pairs={{0,2},{1,3},{2,0},{3,1},{4,6},{5,7},{6,4},{7,5},{8,10},{9,11},{10,... | collective-permute-start | bytes 196616 | tf_op jit(solution)/shard_map/ppermute | solution.py:337
  65.9 2.1 %collective-permute-start.6 = (bf16[32,1024]{1,0:T(8,128)(2,1)S(1)}, bf16[32,1024]{1,0:T(8,128)(2,1)S(1)}, u32[]{:S(2)}, u32[]{:S(2)}) collective-permute-start(bf16[32,1024]{1,0:T(8,128)(2,1)S(1)} %get-tuple-element.45), channel_id=1, source_target_pairs={{0,3},{1,2},{2,1},{3,0},{4,7},{5,6},{6,5},{7,4},{8,11},{9,10},{10,... | collective-permute-start | bytes 196616 | tf_op jit(solution)/shard_map/ppermute | solution.py:337
  68.0 2.5 %collective-permute-done.5.a_ref = bf16[32,1024]{1,0:T(8,128)(2,1)S(1)} collective-permute-done((bf16[32,1024]{1,0:T(8,128)(2,1)S(1)}, bf16[32,1024]{1,0:T(8,128)(2,1)S(1)}, u32[]{:S(2)}, u32[]{:S(2)}) %collective-permute-start.5) | collective-permute-done | bytes 65568 | tf_op jit(solution)/shard_map/ppermute | solution.py:337
  70.5 1.9 %collective-permute-done.6.b_ref = bf16[32,1024]{1,0:T(8,128)(2,1)S(1)} collective-permute-done((bf16[32,1024]{1,0:T(8,128)(2,1)S(1)}, bf16[32,1024]{1,0:T(8,128)(2,1)S(1)}, u32[]{:S(2)}, u32[]{:S(2)}) %collective-permute-start.6) | collective-permute-done | bytes 65568 | tf_op jit(solution)/shard_map/ppermute | solution.py:337
  72.4 0.0 collective-permute-done.4.pair_ref
  72.4 0.0 all-to-all-done.2
  72.4 1.5 %shard_map.90 = (bf16[128,1024]{1,0:T(8,128)(2,1)}, bf16[128,1024]{1,0:T(8,128)(2,1)}, f32[1,8]{1,0:T(1,128)}) custom-call(f32[128,1024]{1,0:T(8,128)S(1)} %get-tuple-element.35.gk_ref, f32[128,1024]{1,0:T(8,128)S(1)} %get-tuple-element.36.gv_ref, bf16[48,1024]{1,0:T(8,128)(2,1)S(1)} %collective-permute-done.4.pair_ref, ...), custom_call_target="tpu_custom_call" | custom-call | bytes 1048576 | tf_op jit(solution)/shard_map/pallas_call | solution.py:324
  (5 shorter events, 0.0 us)
Async XLA Ops:
  3.7 23.3 %copy-start = (bf16[1,128,1024]{2,1,0:T(8,128)(2,1)S(1)}, bf16[1,128,1024]{2,1,0:T(8,128)(2,1)}, u32[]{:S(2)}) copy-start(bf16[1,128,1024]{2,1,0:T(8,128)(2,1)} %param.6) | copy-start | bytes 786436
  3.7 23.3 %copy-start.1 = (bf16[1,128,1024]{2,1,0:T(8,128)(2,1)S(1)}, bf16[1,128,1024]{2,1,0:T(8,128)(2,1)}, u32[]{:S(2)}) copy-start(bf16[1,128,1024]{2,1,0:T(8,128)(2,1)} %param.7) | copy-start | bytes 786436
  3.7 23.3 %copy-start.2 = (bf16[1,128,1024]{2,1,0:T(8,128)(2,1)S(1)}, bf16[1,128,1024]{2,1,0:T(8,128)(2,1)}, u32[]{:S(2)}) copy-start(bf16[1,128,1024]{2,1,0:T(8,128)(2,1)} %param.5) | copy-start | bytes 786436
  3.7 23.3 %copy-start.3 = (bf16[1,128,1024]{2,1,0:T(8,128)(2,1)S(1)}, bf16[1,128,1024]{2,1,0:T(8,128)(2,1)}, u32[]{:S(2)}) copy-start(bf16[1,128,1024]{2,1,0:T(8,128)(2,1)} %param.8) | copy-start | bytes 786436
  3.7 30.1 %all-to-all-start = ((bf16[32,8,1024]{2,1,0:T(8,128)(2,1)}), bf16[32,8,1024]{2,1,0:T(8,128)(2,1)S(1)}, u32[]{:S(2)}, u32[]{:S(2)}) async-start(bf16[32,8,1024]{2,1,0:T(8,128)(2,1)} %get-tuple-element.31), calls=%async_computation | async-start | bytes 1048576 | tf_op jit(solution)/shard_map/all_to_all | solution.py:342
  17.6 13.5 %collective-permute-start = (bf16[32,1024]{1,0:T(8,128)(2,1)}, bf16[32,1024]{1,0:T(8,128)(2,1)S(1)}, u32[]{:S(2)}, u32[]{:S(2)}) collective-permute-start(bf16[32,1024]{1,0:T(8,128)(2,1)} %get-tuple-element.29), channel_id=1, source_target_pairs={{0,1},{1,0},{2,3},{3,2},{4,5},{5,4},{6,7},{7,6},{8,9},{9,8},{10,11... | collective-permute-start | bytes 196616 | tf_op jit(solution)/shard_map/ppermute | solution.py:337
  20.7 8.8 %collective-permute-start.2 = (bf16[16,1024]{1,0:T(8,128)(2,1)}, bf16[16,1024]{1,0:T(8,128)(2,1)S(1)}, u32[]{:S(2)}, u32[]{:S(2)}) collective-permute-start(bf16[16,1024]{1,0:T(8,128)(2,1)} %get-tuple-element.30), channel_id=1, source_target_pairs={{0,3},{1,2},{2,1},{3,0},{4,7},{5,6},{6,5},{7,4},{8,11},{9,10},{10,... | collective-permute-start | bytes 98312 | tf_op jit(solution)/shard_map/ppermute | solution.py:337
  24.4 6.7 %collective-permute-start.1 = (bf16[16,1024]{1,0:T(8,128)(2,1)}, bf16[16,1024]{1,0:T(8,128)(2,1)S(1)}, u32[]{:S(2)}, u32[]{:S(2)}) collective-permute-start(bf16[16,1024]{1,0:T(8,128)(2,1)} %get-tuple-element.30), channel_id=1, source_target_pairs={{0,2},{1,3},{2,0},{3,1},{4,6},{5,7},{6,4},{7,5},{8,10},{9,11},{10,... | collective-permute-start | bytes 98312 | tf_op jit(solution)/shard_map/ppermute | solution.py:337
  27.0 0.7 copy-start.4
  35.4 17.3 %all-to-all-start.1 = ((f32[16,8,128]{2,1,0:T(8,128)}), f32[16,8,128]{2,1,0:T(8,128)S(1)}, u32[]{:S(2)}, u32[]{:S(2)}) async-start(f32[16,8,128]{2,1,0:T(8,128)} %get-tuple-element.37), calls=%async_computation.1 | async-start | bytes 131072 | tf_op jit(solution)/shard_map/all_to_all | solution.py:377
  45.3 5.6 %collective-permute-start.3 = (bf16[32,1024]{1,0:T(8,128)(2,1)S(1)}, bf16[32,1024]{1,0:T(8,128)(2,1)S(1)}, u32[]{:S(2)}, u32[]{:S(2)}) collective-permute-start(bf16[32,1024]{1,0:T(8,128)(2,1)S(1)} %get-tuple-element.38), channel_id=1, source_target_pairs={{0,4},{1,5},{2,6},{3,7},{4,0},{5,1},{6,2},{7,3},{8,12},{9,13},{10,... | collective-permute-start | bytes 196616 | tf_op jit(solution)/shard_map/ppermute | solution.py:337
  53.5 18.9 %all-to-all-start.2 = ((bf16[32,8,640]{2,1,0:T(8,128)(2,1)}), bf16[32,8,640]{2,1,0:T(8,128)(2,1)S(1)}, u32[]{:S(2)}, u32[]{:S(2)}) async-start(bf16[32,8,640]{2,1,0:T(8,128)(2,1)} %bitcast.6), calls=%async_computation.2 | async-start | bytes 655360 | tf_op jit(solution)/shard_map/all_to_all | solution.py:342
  58.4 14.0 %collective-permute-start.4 = (bf16[48,1024]{1,0:T(8,128)(2,1)S(1)}, bf16[48,1024]{1,0:T(8,128)(2,1)S(1)}, u32[]{:S(2)}, u32[]{:S(2)}) collective-permute-start(bf16[48,1024]{1,0:T(8,128)(2,1)S(1)} %get-tuple-element.43), channel_id=1, source_target_pairs={{0,1},{1,0},{2,3},{3,2},{4,5},{5,4},{6,7},{7,6},{8,9},{9,8},{10,11... | collective-permute-start | bytes 294920 | tf_op jit(solution)/shard_map/ppermute | solution.py:337
  61.6 9.0 %collective-permute-start.5 = (bf16[32,1024]{1,0:T(8,128)(2,1)S(1)}, bf16[32,1024]{1,0:T(8,128)(2,1)S(1)}, u32[]{:S(2)}, u32[]{:S(2)}) collective-permute-start(bf16[32,1024]{1,0:T(8,128)(2,1)S(1)} %get-tuple-element.44), channel_id=1, source_target_pairs={{0,2},{1,3},{2,0},{3,1},{4,6},{5,7},{6,4},{7,5},{8,10},{9,11},{10,... | collective-permute-start | bytes 196616 | tf_op jit(solution)/shard_map/ppermute | solution.py:337
  65.9 6.5 %collective-permute-start.6 = (bf16[32,1024]{1,0:T(8,128)(2,1)S(1)}, bf16[32,1024]{1,0:T(8,128)(2,1)S(1)}, u32[]{:S(2)}, u32[]{:S(2)}) collective-permute-start(bf16[32,1024]{1,0:T(8,128)(2,1)S(1)} %get-tuple-element.45), channel_id=1, source_target_pairs={{0,3},{1,2},{2,1},{3,0},{4,7},{5,6},{6,5},{7,4},{8,11},{9,10},{10,... | collective-permute-start | bytes 196616 | tf_op jit(solution)/shard_map/ppermute | solution.py:337

commit v8 on v7

--- a/solution.py
+++ b/solution.py
@@ -58,17 +58,20 @@
 STEPS = LOCAL + 2 * TOKENS
 
 
-def pool_kernel(k_hbm, v_hbm, l3_ref, l4_ref, slot_ref, k_ref, v_ref, sems):
+def pool_kernel(k_hbm, v_hbm, l3_ref, l4_ref, slot_hbm, k_ref, v_ref, slot_ref, sems):
     me = lax.axis_index("seq")
-    fetch_k = pltpu.make_async_copy(k_hbm, k_ref, sems.at[0])
-    fetch_v = pltpu.make_async_copy(v_hbm, v_ref, sems.at[1])
-    fetch_k.start()
-    fetch_v.start()
+    fetches = []
+    for source, held in ((k_hbm, k_ref), (v_hbm, v_ref)):
+        for rows in (pl.ds(0, 64), pl.ds(64, 64)):
+            sem = sems.at[len(fetches)]
+            fetches.append(pltpu.make_async_copy(source.at[rows], held.at[rows], sem))
+            fetches[-1].start()
     half = pooling(64, 128)
     quarter = pooling(32, 64)
     l2 = []
-    for fetch, held in ((fetch_k, k_ref), (fetch_v, v_ref)):
-        fetch.wait()
+    for i, held in enumerate((k_ref, v_ref)):
+        fetches[2 * i].wait()
+        fetches[2 * i + 1].wait()
         one = mm(half, held[...]).astype(BF16)
         l2.append(mm(quarter, one).astype(BF16))
     l3 = mm(quarter, jnp.concatenate(l2, axis=0)).astype(BF16)
@@ -76,24 +79,37 @@
     l4 = mm(pooling(16, 32), l3).astype(BF16)
     l4_ref[...] = l4
     row, col = iota2(16, 16)
-    l5 = mm(pooling(16, 16), l4).astype(BF16)
-    m6 = mat((row < 8) & ((row & 3) < 2) & ((col >> 1) == ((row >> 2) * 2 + (row & 3))), 0.5)
-    l6 = mm(m6, l5).astype(BF16)
-    m7 = mat((row < 8) & ((row & 3) == 0) & ((col >> 1) == (row >> 1)), 0.5)
-    l7 = mm(m7, l6).astype(BF16)
-    b5, b6, b7 = l5[0:8], l6[0:8], l7[0:8]
+    puts = []
+
+    def put(at):
+        rows = pl.ds(at, 8)
+        puts.append(pltpu.make_async_copy(slot_ref.at[rows], slot_hbm.at[rows], sems.at[4 + len(puts)]))
+        puts[-1].start()
+
     base7 = ((me >> 4) ^ 1) << 4
     base6 = ((me >> 3) ^ 1) << 3
     base5 = ((me >> 2) ^ 1) << 2
     base4 = (me >> 2) << 2
-    for i in range(16):
-        slot_ref[base7 + i] = b7
+    l5 = mm(pooling(16, 16), l4).astype(BF16)
+    for i in range(4):
+        slot_ref[base5 + i] = l5[0:8]
+        slot_ref[base4 + i] = jnp.zeros((8, WIDTH), BF16)
+    put((me >> 3) << 3)
+    m6 = mat((row < 8) & ((row & 3) < 2) & ((col >> 1) == ((row >> 2) * 2 + (row & 3))), 0.5)
+    l6 = mm(m6, l5).astype(BF16)
     for i in range(8):
-        slot_ref[base6 + i] = b6
-    for i in range(4):
-        slot_ref[base5 + i] = b5
-    for i in range(4):
-        slot_ref[base4 + i] = jnp.zeros((8, WIDTH), BF16)
+        slot_ref[base6 + i] = l6[0:8]
+    put(base6)
+    m7 = mat((row < 8) & ((row & 3) == 0) & ((col >> 1) == (row >> 1)), 0.5)
+    l7 = mm(m7, l6).astype(BF16)
+    for i in range(8):
+        slot_ref[base7 + i] = l7[0:8]
+    put(base7)
+    for i in range(8, 16):
+        slot_ref[base7 + i] = l7[0:8]
+    put(base7 + 8)
+    for copy in puts:
+        copy.wait()
 
 
 def far_column(me, line):
@@ -285,7 +301,7 @@
 
 
 def final_kernel(
-    gk_ref, gv_ref, pair_ref, a_ref, b_ref, r5_ref, r_ref, ok_ref, ov_ref, os_ref
+    gk_ref, gv_ref, pair_ref, a_ref, b_ref, r5_ref, r_ref, ok_hbm, ov_hbm, os_ref, ok_ref, ov_ref, sems
 ):
     me = lax.axis_index("seq")
     row, col = iota2(TOKENS, PEERS * 8)
@@ -296,7 +312,8 @@
     covers = lax.shift_right_logical(row, shift)
     row3, col3 = iota2(TOKENS, 48)
     row4, col4 = iota2(TOKENS, 32)
-    for out_ref, own_ref, which in ((ok_ref, gk_ref, 0), (ov_ref, gv_ref, 1)):
+    puts = []
+    for out_hbm, out_ref, own_ref, which in ((ok_hbm, ok_ref, gk_ref, 0), (ov_hbm, ov_ref, gv_ref, 1)):
         near = own_ref[...]
         three = jnp.where((row3 >> 3) + 16 * which == col3, 2.0**-3, 0.0)
         five = jnp.where((row3 >> 5) + 32 + 4 * which == col3, 2.0**-5, 0.0)
@@ -311,11 +328,17 @@
             sl = slice(HALF * half, HALF * half + HALF)
             far = mat(covers + 2 * which + 4 * half == line, weight)
             out_ref[:, sl] = (near[:, sl] + mm(far, r_ref[:, 0:HALF])).astype(BF16)
+        for rows in (pl.ds(0, 64), pl.ds(64, 64)):
+            sem = sems.at[len(puts)]
+            puts.append(pltpu.make_async_copy(out_ref.at[rows], out_hbm.at[rows], sem))
+            puts[-1].start()
     slopes = r_ref[:, HALF:].astype(F32).reshape(PEERS, HEADS, 128)
     value = jnp.sum(jnp.sum(slopes, axis=0), axis=1, keepdims=True)
     srow, scol = iota2(HEADS, 128)
     line = jnp.sum(jnp.where(srow == scol, value, 0.0), axis=0, keepdims=True)
     os_ref[...] = line[:, 0:HEADS]
+    for copy in puts:
+        copy.wait()
 
 
 def call(kernel, outs, ins, places=None, out_places=None, scratch=(), cost=1 << 20, alias=None, vmem=12):
@@ -352,7 +375,8 @@
         [((32, wide), BF16), ((16, wide), BF16), ((PEERS, 8, wide), BF16)],
         (k, v),
         [pl.ANY] * 2,
-        scratch=[block, block, pltpu.SemaphoreType.DMA((2,))],
+        [pltpu.VMEM, pltpu.VMEM, pl.ANY],
+        [block, block, pltpu.VMEM((PEERS, 8, wide), BF16), pltpu.SemaphoreType.DMA((8,))],
         vmem=58,
     )
     far = exchange(slots)
@@ -405,6 +429,8 @@
         final_kernel,
         [((TOKENS, wide), BF16), ((TOKENS, wide), BF16), ((1, HEADS), F32)],
         (gk, gv, pair, four_a, four_b, near5, far),
+        out_places=[pl.ANY, pl.ANY, pltpu.VMEM],
+        scratch=[block, block, pltpu.SemaphoreType.DMA((4,))],
     )
     return dq[None], dk[None], dv[None], ds.reshape(HEADS)
 

time: 74.5 us -> 75.7 us (1.016)
  Pallas kernels: 11.8 us -> 12.9 us
    pallas_call x7, Pallas kernels: 11.8 us -> 12.9 us  [call(): pl.pallas_call(kernel, out_shape=[jax.ShapeDtypeStruct(s, t) for s, t in...]
where the time goes in v8:
time: 75.7 us; the launch traced here: 75.1 us
  starting transfers between devices  50.1 us (66%)
  Pallas kernels  12.9 us (17%)
  waiting for transfers between devices  10.5 us (14%)
  between operations  0.82 us (1%)
    ppermute x7, starting transfers between devices, swap(): return lax.ppermute(block, 'seq', [(i, i ^ apart) for i in range(PEERS)])  21.9 us
    all_to_all x2, starting transfers between devices, exchange(): back = lax.all_to_all(slots.reshape(PEERS, 8, width), 'seq', 0, 0)  18.8 us
    pallas_call x7, Pallas kernels, call(): pl.pallas_call(kernel, out_shape=[jax.ShapeDtypeStruct(s, t) for s, t in...  12.9 us
    all_to_all x1, starting transfers between devices, per_device(): slopes = lax.all_to_all(slopes, 'dp', 0, 0)  9.5 us
    ppermute x7, waiting for transfers between devices, swap(): return lax.ppermute(block, 'seq', [(i, i ^ apart) for i in range(PEERS)])  5.91 us
    all_to_all x2, waiting for transfers between devices, exchange(): back = lax.all_to_all(slots.reshape(PEERS, 8, width), 'seq', 0, 0)  2.73 us
    all_to_all x1, waiting for transfers between devices, per_device(): slopes = lax.all_to_all(slopes, 'dp', 0, 0)  1.9 us
  transfers between devices with their start and end apart: 10, of which 5 were waited for; matrix products, arithmetic and copies ran while one was open for 0% of the time, Pallas kernels for 7%

profile of v8, /device:TPU:1, one launch (start us, length us, event | category | flops | bytes accessed | tf_op | source)
XLA Modules:
  0.0 75.1 jit_solution(16226722552613452373)
XLA Ops:
  0.6 3.6 %shard_map.85 = (bf16[32,1024]{1,0:T(8,128)(2,1)}, bf16[16,1024]{1,0:T(8,128)(2,1)}, bf16[32,8,1024]{2,1,0:T(8,128)(2,1)}) custom-call(bf16[128,1024]{1,0:T(8,128)(2,1)} %bitcast.13, bf16[128,1024]{1,0:T(8,128)(2,1)} %bitcast.15), custom_call_target="tpu_custom_call" | custom-call | bytes 1048576 | tf_op jit(solution)/shard_map/pallas_call | solution.py:347
  4.2 0.0 copy-start
  4.3 0.0 copy-start.1
  4.3 0.0 copy-start.2
  4.3 0.0 copy-start.3
  4.3 13.9 %all-to-all-start = ((bf16[32,8,1024]{2,1,0:T(8,128)(2,1)}), bf16[32,8,1024]{2,1,0:T(8,128)(2,1)S(1)}, u32[]{:S(2)}, u32[]{:S(2)}) async-start(bf16[32,8,1024]{2,1,0:T(8,128)(2,1)} %get-tuple-element.31), calls=%async_computation | async-start | bytes 1048576 | tf_op jit(solution)/shard_map/all_to_all | solution.py:365
  18.2 3.1 %collective-permute-start = (bf16[32,1024]{1,0:T(8,128)(2,1)}, bf16[32,1024]{1,0:T(8,128)(2,1)S(1)}, u32[]{:S(2)}, u32[]{:S(2)}) collective-permute-start(bf16[32,1024]{1,0:T(8,128)(2,1)} %get-tuple-element.29), channel_id=1, source_target_pairs={{0,1},{1,0},{2,3},{3,2},{4,5},{5,4},{6,7},{7,6},{8,9},{9,8},{10,11... | collective-permute-start | bytes 196616 | tf_op jit(solution)/shard_map/ppermute | solution.py:360
  21.3 3.7 %collective-permute-start.2 = (bf16[16,1024]{1,0:T(8,128)(2,1)}, bf16[16,1024]{1,0:T(8,128)(2,1)S(1)}, u32[]{:S(2)}, u32[]{:S(2)}) collective-permute-start(bf16[16,1024]{1,0:T(8,128)(2,1)} %get-tuple-element.30), channel_id=1, source_target_pairs={{0,3},{1,2},{2,1},{3,0},{4,7},{5,6},{6,5},{7,4},{8,11},{9,10},{10,... | collective-permute-start | bytes 98312 | tf_op jit(solution)/shard_map/ppermute | solution.py:360
  25.0 2.5 %collective-permute-start.1 = (bf16[16,1024]{1,0:T(8,128)(2,1)}, bf16[16,1024]{1,0:T(8,128)(2,1)S(1)}, u32[]{:S(2)}, u32[]{:S(2)}) collective-permute-start(bf16[16,1024]{1,0:T(8,128)(2,1)} %get-tuple-element.30), channel_id=1, source_target_pairs={{0,2},{1,3},{2,0},{3,1},{4,6},{5,7},{6,4},{7,5},{8,10},{9,11},{10,... | collective-permute-start | bytes 98312 | tf_op jit(solution)/shard_map/ppermute | solution.py:360
  27.5 0.0 copy-start.4
  27.6 0.6 copy-done.4
  28.2 1.9 %shard_map.84 = (bf16[496,1024]{1,0:T(8,128)(2,1)S(1)}, f32[128,1024]{1,0:T(8,128)S(1)}) custom-call(bf16[128,1024]{1,0:T(8,128)(2,1)S(1)} %bitcast.17, bf16[128,1024]{1,0:T(8,128)(2,1)S(1)} %bitcast.18, bf16[128,1024]{1,0:T(8,128)(2,1)S(1)} %bitcast.14, bf16[128,1024]{1,0:T(8,128)(2,1)S(1)} %bitcast.16, f32[8]{0:T(128)S(1)} %copy-done.4), custom_call_target="tpu_custom_call" | custom-call | bytes 268435456 | tf_op jit(solution)/shard_map/pallas_call | solution.py:347
  30.2 1.5 %collective-permute-done.1.r4a_ref = bf16[16,1024]{1,0:T(8,128)(2,1)S(1)} collective-permute-done((bf16[16,1024]{1,0:T(8,128)(2,1)}, bf16[16,1024]{1,0:T(8,128)(2,1)S(1)}, u32[]{:S(2)}, u32[]{:S(2)}) %collective-permute-start.1) | collective-permute-done | bytes 32800 | tf_op jit(solution)/shard_map/ppermute | solution.py:360
  31.7 0.0 collective-permute-done.r3_ref
  31.7 2.7 %all-to-all-done = bf16[32,8,1024]{2,1,0:T(8,128)(2,1)S(1)} async-done(((bf16[32,8,1024]{2,1,0:T(8,128)(2,1)}), bf16[32,8,1024]{2,1,0:T(8,128)(2,1)S(1)}, u32[]{:S(2)}, u32[]{:S(2)}) %all-to-all-start) | async-done | bytes 524320 | tf_op jit(solution)/shard_map/all_to_all | solution.py:365
  34.4 1.6 %shard_map.86 = (bf16[448,1024]{1,0:T(8,128)(2,1)S(1)}, f32[16,8,128]{2,1,0:T(8,128)}) custom-call(bf16[496,1024]{1,0:T(8,128)(2,1)S(1)} %get-tuple-element.27.loc_ref, f32[128,1024]{1,0:T(8,128)S(1)} %get-tuple-element.28.near_ref, bf16[32,1024]{1,0:T(8,128)(2,1)S(1)} %collective-permute-done.r3_ref, bf16[16,1024]{1,0:T(8,128)(2,1)S(1)} %collective-permute-done.1.r4a_ref, ...), custom_call_target="tpu_custom_call" | custom-call | bytes 1048576 | tf_op jit(solution)/shard_map/pallas_call | solution.py:347
  36.0 9.5 %all-to-all-start.1 = ((f32[16,8,128]{2,1,0:T(8,128)}), f32[16,8,128]{2,1,0:T(8,128)S(1)}, u32[]{:S(2)}, u32[]{:S(2)}) async-start(f32[16,8,128]{2,1,0:T(8,128)} %get-tuple-element.37), calls=%async_computation.1 | async-start | bytes 131072 | tf_op jit(solution)/shard_map/all_to_all | solution.py:401
  45.5 0.3 shard_map.87
  45.9 2.9 %collective-permute-start.3 = (bf16[32,1024]{1,0:T(8,128)(2,1)S(1)}, bf16[32,1024]{1,0:T(8,128)(2,1)S(1)}, u32[]{:S(2)}, u32[]{:S(2)}) collective-permute-start(bf16[32,1024]{1,0:T(8,128)(2,1)S(1)} %get-tuple-element.38), channel_id=1, source_target_pairs={{0,4},{1,5},{2,6},{3,7},{4,0},{5,1},{6,2},{7,3},{8,12},{9,13},{10,... | collective-permute-start | bytes 196616 | tf_op jit(solution)/shard_map/ppermute | solution.py:360
  48.8 2.6 %shard_map.88 = (bf16[128,1024]{1,0:T(8,128)(2,1)}, f32[128,1024]{1,0:T(8,128)S(1)}, f32[128,1024]{1,0:T(8,128)S(1)}, bf16[256,640]{1,0:T(8,128)(2,1)}) custom-call(bf16[496,1024]{1,0:T(8,128)(2,1)S(1)} %get-tuple-element.27.loc_ref, bf16[448,1024]{1,0:T(8,128)(2,1)S(1)} %get-tuple-element.32.w_ref, bf16[64,1024]{1,0:T(8,128)(2,1)S(1)} %get-tuple-element.33.gf_ref), custom_call_target="tpu_custom_call" | custom-call | bytes 268435456 | tf_op jit(solution)/shard_map/pallas_call | solution.py:347
  51.5 0.0 collective-permute-done.3.r5_ref
  51.5 1.9 %all-to-all-done.1.s_ref = f32[16,8,128]{2,1,0:T(8,128)S(1)} async-done(((f32[16,8,128]{2,1,0:T(8,128)}), f32[16,8,128]{2,1,0:T(8,128)S(1)}, u32[]{:S(2)}, u32[]{:S(2)}) %all-to-all-start.1) | async-done | bytes 65568 | tf_op jit(solution)/shard_map/all_to_all | solution.py:401
  53.3 0.8 %shard_map.89 = (bf16[48,1024]{1,0:T(8,128)(2,1)S(1)}, bf16[32,1024]{1,0:T(8,128)(2,1)S(1)}, bf16[32,1024]{1,0:T(8,128)(2,1)S(1)}, bf16[256,640]{1,0:T(8,128)(2,1)}) custom-call(f32[16,8,128]{2,1,0:T(8,128)S(1)} %all-to-all-done.1.s_ref, bf16[32,1024]{1,0:T(8,128)(2,1)S(1)} %collective-permute-done.3.r5_ref, ...), custom_call_target="tpu_custom_call", output_to_operand_aliasing={{3}: (5, {})} | custom-call | bytes 1048576 | tf_op jit(solution)/shard_map/pallas_call | solution.py:347
  54.1 4.9 %all-to-all-start.2 = ((bf16[32,8,640]{2,1,0:T(8,128)(2,1)}), bf16[32,8,640]{2,1,0:T(8,128)(2,1)S(1)}, u32[]{:S(2)}, u32[]{:S(2)}) async-start(bf16[32,8,640]{2,1,0:T(8,128)(2,1)} %bitcast.6), calls=%async_computation.2 | async-start | bytes 655360 | tf_op jit(solution)/shard_map/all_to_all | solution.py:365
  59.0 3.1 %collective-permute-start.4 = (bf16[48,1024]{1,0:T(8,128)(2,1)S(1)}, bf16[48,1024]{1,0:T(8,128)(2,1)S(1)}, u32[]{:S(2)}, u32[]{:S(2)}) collective-permute-start(bf16[48,1024]{1,0:T(8,128)(2,1)S(1)} %get-tuple-element.43), channel_id=1, source_target_pairs={{0,1},{1,0},{2,3},{3,2},{4,5},{5,4},{6,7},{7,6},{8,9},{9,8},{10,11... | collective-permute-start | bytes 294920 | tf_op jit(solution)/shard_map/ppermute | solution.py:360
  62.2 4.3 %collective-permute-start.5 = (bf16[32,1024]{1,0:T(8,128)(2,1)S(1)}, bf16[32,1024]{1,0:T(8,128)(2,1)S(1)}, u32[]{:S(2)}, u32[]{:S(2)}) collective-permute-start(bf16[32,1024]{1,0:T(8,128)(2,1)S(1)} %get-tuple-element.44), channel_id=1, source_target_pairs={{0,2},{1,3},{2,0},{3,1},{4,6},{5,7},{6,4},{7,5},{8,10},{9,11},{10,... | collective-permute-start | bytes 196616 | tf_op jit(solution)/shard_map/ppermute | solution.py:360
  66.5 2.1 %collective-permute-start.6 = (bf16[32,1024]{1,0:T(8,128)(2,1)S(1)}, bf16[32,1024]{1,0:T(8,128)(2,1)S(1)}, u32[]{:S(2)}, u32[]{:S(2)}) collective-permute-start(bf16[32,1024]{1,0:T(8,128)(2,1)S(1)} %get-tuple-element.45), channel_id=1, source_target_pairs={{0,3},{1,2},{2,1},{3,0},{4,7},{5,6},{6,5},{7,4},{8,11},{9,10},{10,... | collective-permute-start | bytes 196616 | tf_op jit(solution)/shard_map/ppermute | solution.py:360
  68.6 2.5 %collective-permute-done.5.a_ref = bf16[32,1024]{1,0:T(8,128)(2,1)S(1)} collective-permute-done((bf16[32,1024]{1,0:T(8,128)(2,1)S(1)}, bf16[32,1024]{1,0:T(8,128)(2,1)S(1)}, u32[]{:S(2)}, u32[]{:S(2)}) %collective-permute-start.5) | collective-permute-done | bytes 65568 | tf_op jit(solution)/shard_map/ppermute | solution.py:360
  71.1 1.9 %collective-permute-done.6.b_ref = bf16[32,1024]{1,0:T(8,128)(2,1)S(1)} collective-permute-done((bf16[32,1024]{1,0:T(8,128)(2,1)S(1)}, bf16[32,1024]{1,0:T(8,128)(2,1)S(1)}, u32[]{:S(2)}, u32[]{:S(2)}) %collective-permute-start.6) | collective-permute-done | bytes 65568 | tf_op jit(solution)/shard_map/ppermute | solution.py:360
  73.0 0.0 collective-permute-done.4.pair_ref
  73.0 0.0 all-to-all-done.2
  73.0 2.1 %shard_map.90 = (bf16[128,1024]{1,0:T(8,128)(2,1)}, bf16[128,1024]{1,0:T(8,128)(2,1)}, f32[1,8]{1,0:T(1,128)}) custom-call(f32[128,1024]{1,0:T(8,128)S(1)} %get-tuple-element.35.gk_ref, f32[128,1024]{1,0:T(8,128)S(1)} %get-tuple-element.36.gv_ref, bf16[48,1024]{1,0:T(8,128)(2,1)S(1)} %collective-permute-done.4.pair_ref, ...), custom_call_target="tpu_custom_call" | custom-call | bytes 1048576 | tf_op jit(solution)/shard_map/pallas_call | solution.py:347
  (5 shorter events, 0.0 us)
Async XLA Ops:
  4.2 23.3 %copy-start = (bf16[1,128,1024]{2,1,0:T(8,128)(2,1)S(1)}, bf16[1,128,1024]{2,1,0:T(8,128)(2,1)}, u32[]{:S(2)}) copy-start(bf16[1,128,1024]{2,1,0:T(8,128)(2,1)} %param.6) | copy-start | bytes 786436
  4.3 23.3 %copy-start.1 = (bf16[1,128,1024]{2,1,0:T(8,128)(2,1)S(1)}, bf16[1,128,1024]{2,1,0:T(8,128)(2,1)}, u32[]{:S(2)}) copy-start(bf16[1,128,1024]{2,1,0:T(8,128)(2,1)} %param.7) | copy-start | bytes 786436
  4.3 23.3 %copy-start.2 = (bf16[1,128,1024]{2,1,0:T(8,128)(2,1)S(1)}, bf16[1,128,1024]{2,1,0:T(8,128)(2,1)}, u32[]{:S(2)}) copy-start(bf16[1,128,1024]{2,1,0:T(8,128)(2,1)} %param.5) | copy-start | bytes 786436
  4.3 23.3 %copy-start.3 = (bf16[1,128,1024]{2,1,0:T(8,128)(2,1)S(1)}, bf16[1,128,1024]{2,1,0:T(8,128)(2,1)}, u32[]{:S(2)}) copy-start(bf16[1,128,1024]{2,1,0:T(8,128)(2,1)} %param.8) | copy-start | bytes 786436
  4.3 30.1 %all-to-all-start = ((bf16[32,8,1024]{2,1,0:T(8,128)(2,1)}), bf16[32,8,1024]{2,1,0:T(8,128)(2,1)S(1)}, u32[]{:S(2)}, u32[]{:S(2)}) async-start(bf16[32,8,1024]{2,1,0:T(8,128)(2,1)} %get-tuple-element.31), calls=%async_computation | async-start | bytes 1048576 | tf_op jit(solution)/shard_map/all_to_all | solution.py:365
  18.2 13.5 %collective-permute-start = (bf16[32,1024]{1,0:T(8,128)(2,1)}, bf16[32,1024]{1,0:T(8,128)(2,1)S(1)}, u32[]{:S(2)}, u32[]{:S(2)}) collective-permute-start(bf16[32,1024]{1,0:T(8,128)(2,1)} %get-tuple-element.29), channel_id=1, source_target_pairs={{0,1},{1,0},{2,3},{3,2},{4,5},{5,4},{6,7},{7,6},{8,9},{9,8},{10,11... | collective-permute-start | bytes 196616 | tf_op jit(solution)/shard_map/ppermute | solution.py:360
  21.3 8.8 %collective-permute-start.2 = (bf16[16,1024]{1,0:T(8,128)(2,1)}, bf16[16,1024]{1,0:T(8,128)(2,1)S(1)}, u32[]{:S(2)}, u32[]{:S(2)}) collective-permute-start(bf16[16,1024]{1,0:T(8,128)(2,1)} %get-tuple-element.30), channel_id=1, source_target_pairs={{0,3},{1,2},{2,1},{3,0},{4,7},{5,6},{6,5},{7,4},{8,11},{9,10},{10,... | collective-permute-start | bytes 98312 | tf_op jit(solution)/shard_map/ppermute | solution.py:360
  25.0 6.7 %collective-permute-start.1 = (bf16[16,1024]{1,0:T(8,128)(2,1)}, bf16[16,1024]{1,0:T(8,128)(2,1)S(1)}, u32[]{:S(2)}, u32[]{:S(2)}) collective-permute-start(bf16[16,1024]{1,0:T(8,128)(2,1)} %get-tuple-element.30), channel_id=1, source_target_pairs={{0,2},{1,3},{2,0},{3,1},{4,6},{5,7},{6,4},{7,5},{8,10},{9,11},{10,... | collective-permute-start | bytes 98312 | tf_op jit(solution)/shard_map/ppermute | solution.py:360
  27.5 0.7 copy-start.4
  36.0 17.3 %all-to-all-start.1 = ((f32[16,8,128]{2,1,0:T(8,128)}), f32[16,8,128]{2,1,0:T(8,128)S(1)}, u32[]{:S(2)}, u32[]{:S(2)}) async-start(f32[16,8,128]{2,1,0:T(8,128)} %get-tuple-element.37), calls=%async_computation.1 | async-start | bytes 131072 | tf_op jit(solution)/shard_map/all_to_all | solution.py:401
  45.9 5.6 %collective-permute-start.3 = (bf16[32,1024]{1,0:T(8,128)(2,1)S(1)}, bf16[32,1024]{1,0:T(8,128)(2,1)S(1)}, u32[]{:S(2)}, u32[]{:S(2)}) collective-permute-start(bf16[32,1024]{1,0:T(8,128)(2,1)S(1)} %get-tuple-element.38), channel_id=1, source_target_pairs={{0,4},{1,5},{2,6},{3,7},{4,0},{5,1},{6,2},{7,3},{8,12},{9,13},{10,... | collective-permute-start | bytes 196616 | tf_op jit(solution)/shard_map/ppermute | solution.py:360
  54.1 18.9 %all-to-all-start.2 = ((bf16[32,8,640]{2,1,0:T(8,128)(2,1)}), bf16[32,8,640]{2,1,0:T(8,128)(2,1)S(1)}, u32[]{:S(2)}, u32[]{:S(2)}) async-start(bf16[32,8,640]{2,1,0:T(8,128)(2,1)} %bitcast.6), calls=%async_computation.2 | async-start | bytes 655360 | tf_op jit(solution)/shard_map/all_to_all | solution.py:365
  59.0 14.0 %collective-permute-start.4 = (bf16[48,1024]{1,0:T(8,128)(2,1)S(1)}, bf16[48,1024]{1,0:T(8,128)(2,1)S(1)}, u32[]{:S(2)}, u32[]{:S(2)}) collective-permute-start(bf16[48,1024]{1,0:T(8,128)(2,1)S(1)} %get-tuple-element.43), channel_id=1, source_target_pairs={{0,1},{1,0},{2,3},{3,2},{4,5},{5,4},{6,7},{7,6},{8,9},{9,8},{10,11... | collective-permute-start | bytes 294920 | tf_op jit(solution)/shard_map/ppermute | solution.py:360
  62.2 9.0 %collective-permute-start.5 = (bf16[32,1024]{1,0:T(8,128)(2,1)S(1)}, bf16[32,1024]{1,0:T(8,128)(2,1)S(1)}, u32[]{:S(2)}, u32[]{:S(2)}) collective-permute-start(bf16[32,1024]{1,0:T(8,128)(2,1)S(1)} %get-tuple-element.44), channel_id=1, source_target_pairs={{0,2},{1,3},{2,0},{3,1},{4,6},{5,7},{6,4},{7,5},{8,10},{9,11},{10,... | collective-permute-start | bytes 196616 | tf_op jit(solution)/shard_map/ppermute | solution.py:360
  66.5 6.5 %collective-permute-start.6 = (bf16[32,1024]{1,0:T(8,128)(2,1)S(1)}, bf16[32,1024]{1,0:T(8,128)(2,1)S(1)}, u32[]{:S(2)}, u32[]{:S(2)}) collective-permute-start(bf16[32,1024]{1,0:T(8,128)(2,1)S(1)} %get-tuple-element.45), channel_id=1, source_target_pairs={{0,3},{1,2},{2,1},{3,0},{4,7},{5,6},{6,5},{7,4},{8,11},{9,10},{10,... | collective-permute-start | bytes 196616 | tf_op jit(solution)/shard_map/ppermute | solution.py:360

commit v9 on v5

--- a/solution.py
+++ b/solution.py
@@ -224,8 +224,7 @@
         gf_ref[32:64, sl] = dv[48:80].astype(BF16)
 
 
-def grad_kernel(loc_ref, w_ref, gf_ref, dq_ref, gk_ref, gv_ref, slot_ref):
-    me = lax.axis_index("seq")
+def grad_kernel(loc_ref, w_ref, dq_ref, gk_ref, gv_ref):
     lane = lax.broadcasted_iota(jnp.int32, (1, TOKENS), 1)
     quarter = lane >> 5
     lower = lane < 64
@@ -257,6 +256,12 @@
         dv = mm(p_near, c)
         gk_ref[:, sl] = dk[0:128] + mm(spread, dk[128:224].astype(BF16))
         gv_ref[:, sl] = dv[0:128] + mm(spread, dv[128:224].astype(BF16))
+
+
+def slope_kernel(
+    s_ref, gf_ref, r5_ref, g3_ref, g4a_ref, g4b_ref, pair_ref, a_ref, b_ref, slot_ref
+):
+    me = lax.axis_index("seq")
     row, col = iota2(PEERS * 8, 64)
     is_key = col < 32
     line = jnp.where(is_key, col, col - 32) + 16
@@ -264,22 +269,13 @@
     first = mm(mat(row == place, 1.0), gf_ref[:, 0:HALF])
     second = mm(mat(row == place + 4, 1.0), gf_ref[:, HALF:WIDTH])
     slot_ref[:, 0:HALF] = (first + second).astype(BF16)
-    slot_ref[:, HALF:] = jnp.zeros((PEERS * 8, 128), BF16)
-
-
-def slope_kernel(
-    s_ref, r5_ref, g3_ref, g4a_ref, g4b_ref, slot_in, pair_ref, a_ref, b_ref, slot_out, tile_ref, sem
-):
-    me = lax.axis_index("seq")
     value = jnp.sum(jnp.sum(s_ref[...], axis=0), axis=1, keepdims=True)
     high, middle, low = three_parts(value)
     lane = lax.broadcasted_iota(jnp.int32, (HEADS, 128), 1)
     tile = jnp.where(
         lane == 0, high, jnp.where(lane == 1, middle, jnp.where(lane == 2, low, 0.0))
     )
-    tile_ref[...] = jnp.concatenate([tile] * PEERS, axis=0).astype(BF16)
-    put = pltpu.make_async_copy(tile_ref, slot_out.at[:, pl.ds(HALF, 128)], sem)
-    put.start()
+    slot_ref[:, HALF:] = jnp.concatenate([tile] * PEERS, axis=0).astype(BF16)
     row, col = iota2(16, 32)
     for apart, own_ref, out_ref in ((1, g3_ref, pair_ref), (2, g4a_ref, a_ref), (3, g4b_ref, b_ref)):
         size = own_ref.shape[0]
@@ -287,7 +283,6 @@
         at = ((me & 3) ^ apart) * 4
         pick = ((row < 4) & (col == at + row)) | ((row >= 4) & (row < 8) & (col == at + row + 12))
         out_ref[size : size + 16, :] = mm(mat(pick, 1.0), r5_ref[...]).astype(BF16)
-    put.wait()
 
 
 def final_kernel(
@@ -386,26 +381,21 @@
         (loc, work),
     )
     near5 = swap(g5, 4)
-    dq, gk, gv, slots = call(
-        grad_kernel,
-        [((TOKENS, wide), BF16), ((TOKENS, wide), F32), ((TOKENS, wide), F32),
-         ((PEERS * 8, HALF + 128), BF16)],
-        (loc, work, gf),
-        cost=LONG,
-    )
     pair, four_a, four_b, slots = call(
         slope_kernel,
         [((48, wide), BF16), ((32, wide), BF16), ((32, wide), BF16), ((PEERS * 8, HALF + 128), BF16)],
-        (slopes, near5, g3, g4a, g4b, slots),
-        [pltpu.VMEM] * 5 + [pl.ANY],
-        [pltpu.VMEM] * 3 + [pl.ANY],
-        [pltpu.VMEM((PEERS * 8, 128), BF16), pltpu.SemaphoreType.DMA(())],
-        alias={5: 3},
+        (slopes, gf, near5, g3, g4a, g4b),
     )
     far = exchange(slots)
     pair = swap(pair, 1)
     four_a = swap(four_a, 2)
     four_b = swap(four_b, 3)
+    dq, gk, gv = call(
+        grad_kernel,
+        [((TOKENS, wide), BF16), ((TOKENS, wide), F32), ((TOKENS, wide), F32)],
+        (loc, work),
+        cost=LONG,
+    )
     dk, dv, ds = call(
         final_kernel,
         [((TOKENS, wide), BF16), ((TOKENS, wide), BF16), ((1, HEADS), F32)],

time: 74.4 us -> 76.1 us (1.023)
  local copies, waits for them, and re-layouts: 0.98 us -> 2.45 us
    unnamed x14 -> x18, local copies, waits for them, and re-layouts: 0.98 us -> 2.45 us
  transfers between devices with their start and end apart: 10 -> 10, of which waited for: 5 -> 6; matrix products, arithmetic and copies ran while one was open for 0% -> 0% of each run, Pallas kernels for 5% -> 5%
where the time goes in v9:
time: 76.1 us; the launch traced here: 75.5 us
  starting transfers between devices  49.9 us (66%)
  waiting for transfers between devices  11.7 us (15%)
  Pallas kernels  10.7 us (14%)
  local copies, waits for them, and re-layouts  2.45 us (3%)
  between operations  0.85 us (1%)
    ppermute x7, starting transfers between devices, swap(): return lax.ppermute(block, 'seq', [(i, i ^ apart) for i in range(PEERS)])  22.1 us
    all_to_all x2, starting transfers between devices, exchange(): back = lax.all_to_all(slots.reshape(PEERS, 8, width), 'seq', 0, 0)  18.3 us
    pallas_call x7, Pallas kernels, call(): pl.pallas_call(kernel, out_shape=[jax.ShapeDtypeStruct(s, t) for s, t in...  10.7 us
    all_to_all x1, starting transfers between devices, per_device(): slopes = lax.all_to_all(slopes, 'dp', 0, 0)  9.51 us
    ppermute x7, waiting for transfers between devices, swap(): return lax.ppermute(block, 'seq', [(i, i ^ apart) for i in range(PEERS)])  7.11 us
    all_to_all x2, waiting for transfers between devices, exchange(): back = lax.all_to_all(slots.reshape(PEERS, 8, width), 'seq', 0, 0)  2.63 us
    unnamed x18, local copies, waits for them, and re-layouts  2.45 us
    all_to_all x1, waiting for transfers between devices, per_device(): slopes = lax.all_to_all(slopes, 'dp', 0, 0)  1.92 us
  transfers between devices with their start and end apart: 10, of which 6 were waited for; matrix products, arithmetic and copies ran while one was open for 0% of the time, Pallas kernels for 5%

profile of v9, /device:TPU:1, one launch (start us, length us, event | category | flops | bytes accessed | tf_op | source)
XLA Modules:
  0.0 75.5 jit_solution(14918793490258797037)
XLA Ops:
  0.6 3.1 %shard_map.84 = (bf16[208,1024]{1,0:T(8,128)(2,1)}, bf16[32,1024]{1,0:T(8,128)(2,1)}, bf16[16,1024]{1,0:T(8,128)(2,1)}, bf16[32,8,1024]{2,1,0:T(8,128)(2,1)}) custom-call(bf16[128,1024]{1,0:T(8,128)(2,1)} %bitcast.13, bf16[128,1024]{1,0:T(8,128)(2,1)} %bitcast.15, f32[8]{0:T(128)} %slope_hbm.1), custom_call_target="tpu_custom_call" | custom-call | bytes 1048576 | tf_op jit(solution)/shard_map/pallas_call | solution.py:325
  3.7 0.0 copy-start.7
  3.7 0.0 copy-start.8
  3.7 0.0 copy-start
  3.8 0.0 copy-start.1
  3.8 13.9 %all-to-all-start = ((bf16[32,8,1024]{2,1,0:T(8,128)(2,1)}), bf16[32,8,1024]{2,1,0:T(8,128)(2,1)S(1)}, u32[]{:S(2)}, u32[]{:S(2)}) async-start(bf16[32,8,1024]{2,1,0:T(8,128)(2,1)} %get-tuple-element.32), calls=%async_computation | async-start | bytes 1048576 | tf_op jit(solution)/shard_map/all_to_all | solution.py:343
  17.7 3.1 %collective-permute-start = (bf16[32,1024]{1,0:T(8,128)(2,1)S(1)}, bf16[32,1024]{1,0:T(8,128)(2,1)S(1)}, u32[]{:S(2)}, u32[]{:S(2)}) collective-permute-start(bf16[32,1024]{1,0:T(8,128)(2,1)S(1)} %copy-done.7), channel_id=1, source_target_pairs={{0,1},{1,0},{2,3},{3,2},{4,5},{5,4},{6,7},{7,6},{8,9},{9,8},{10,11... | collective-permute-start | bytes 196616 | tf_op jit(solution)/shard_map/ppermute | solution.py:338
  20.8 4.3 %collective-permute-start.1 = (bf16[16,1024]{1,0:T(8,128)(2,1)S(1)}, bf16[16,1024]{1,0:T(8,128)(2,1)S(1)}, u32[]{:S(2)}, u32[]{:S(2)}) collective-permute-start(bf16[16,1024]{1,0:T(8,128)(2,1)S(1)} %copy-done.8), channel_id=1, source_target_pairs={{0,2},{1,3},{2,0},{3,1},{4,6},{5,7},{6,4},{7,5},{8,10},{9,11},{10,... | collective-permute-start | bytes 98312 | tf_op jit(solution)/shard_map/ppermute | solution.py:338
  25.1 2.1 %collective-permute-start.2 = (bf16[16,1024]{1,0:T(8,128)(2,1)S(1)}, bf16[16,1024]{1,0:T(8,128)(2,1)S(1)}, u32[]{:S(2)}, u32[]{:S(2)}) collective-permute-start(bf16[16,1024]{1,0:T(8,128)(2,1)S(1)} %copy-done.8), channel_id=1, source_target_pairs={{0,3},{1,2},{2,1},{3,0},{4,7},{5,6},{6,5},{7,4},{8,11},{9,10},{10,... | collective-permute-start | bytes 98312 | tf_op jit(solution)/shard_map/ppermute | solution.py:338
  27.3 0.0 copy-start.4
  27.3 0.9 %copy-done.4 = bf16[1,128,1024]{2,1,0:T(8,128)(2,1)S(1)} copy-done((bf16[1,128,1024]{2,1,0:T(8,128)(2,1)S(1)}, bf16[1,128,1024]{2,1,0:T(8,128)(2,1)}, u32[]{:S(2)}) %copy-start.4) | copy-done | bytes 262168
  28.3 0.8 %shard_map.85 = (bf16[496,1024]{1,0:T(8,128)(2,1)S(1)}, f32[128,1024]{1,0:T(8,128)S(1)}) custom-call(bf16[128,1024]{1,0:T(8,128)(2,1)S(1)} %bitcast.17, bf16[128,1024]{1,0:T(8,128)(2,1)S(1)} %bitcast.18, bf16[128,1024]{1,0:T(8,128)(2,1)S(1)} %bitcast.14, bf16[128,1024]{1,0:T(8,128)(2,1)S(1)} %bitcast.16, bf16[208,1024]{1,0:T(8,128)(2,1)S(1)} %copy-done.2), custom_call_target="tpu_custom_call" | custom-call | bytes 268435456 | tf_op jit(solution)/shard_map/pallas_call | solution.py:325
  29.0 0.0 collective-permute-done.1.r4a_ref
  29.1 2.2 %collective-permute-done.2.r4b_ref = bf16[16,1024]{1,0:T(8,128)(2,1)S(1)} collective-permute-done((bf16[16,1024]{1,0:T(8,128)(2,1)S(1)}, bf16[16,1024]{1,0:T(8,128)(2,1)S(1)}, u32[]{:S(2)}, u32[]{:S(2)}) %collective-permute-start.2) | collective-permute-done | bytes 32800 | tf_op jit(solution)/shard_map/ppermute | solution.py:338
  31.3 2.6 %all-to-all-done = bf16[32,8,1024]{2,1,0:T(8,128)(2,1)S(1)} async-done(((bf16[32,8,1024]{2,1,0:T(8,128)(2,1)}), bf16[32,8,1024]{2,1,0:T(8,128)(2,1)S(1)}, u32[]{:S(2)}, u32[]{:S(2)}) %all-to-all-start) | async-done | bytes 524320 | tf_op jit(solution)/shard_map/all_to_all | solution.py:343
  33.9 1.6 %shard_map.86 = (bf16[448,1024]{1,0:T(8,128)(2,1)S(1)}, f32[16,8,128]{2,1,0:T(8,128)}) custom-call(bf16[496,1024]{1,0:T(8,128)(2,1)S(1)} %get-tuple-element.28.loc_ref, f32[128,1024]{1,0:T(8,128)S(1)} %get-tuple-element.29.near_ref, bf16[32,1024]{1,0:T(8,128)(2,1)S(1)} %collective-permute-done.r3_ref, bf16[16,1024]{1,0:T(8,128)(2,1)S(1)} %collective-permute-done.1.r4a_ref, ...), custom_call_target="tpu_custom_call" | custom-call | bytes 1048576 | tf_op jit(solution)/shard_map/pallas_call | solution.py:325
  35.5 9.5 %all-to-all-start.1 = ((f32[16,8,128]{2,1,0:T(8,128)}), f32[16,8,128]{2,1,0:T(8,128)S(1)}, u32[]{:S(2)}, u32[]{:S(2)}) async-start(f32[16,8,128]{2,1,0:T(8,128)} %get-tuple-element.37), calls=%async_computation.1 | async-start | bytes 131072 | tf_op jit(solution)/shard_map/all_to_all | solution.py:377
  45.0 0.3 shard_map.88
  45.4 2.9 %collective-permute-start.3 = (bf16[32,1024]{1,0:T(8,128)(2,1)S(1)}, bf16[32,1024]{1,0:T(8,128)(2,1)S(1)}, u32[]{:S(2)}, u32[]{:S(2)}) collective-permute-start(bf16[32,1024]{1,0:T(8,128)(2,1)S(1)} %get-tuple-element.39), channel_id=1, source_target_pairs={{0,4},{1,5},{2,6},{3,7},{4,0},{5,1},{6,2},{7,3},{8,12},{9,13},{10,... | collective-permute-start | bytes 196616 | tf_op jit(solution)/shard_map/ppermute | solution.py:338
  48.3 2.6 %collective-permute-done.3.r5_ref = bf16[32,1024]{1,0:T(8,128)(2,1)S(1)} collective-permute-done((bf16[32,1024]{1,0:T(8,128)(2,1)S(1)}, bf16[32,1024]{1,0:T(8,128)(2,1)S(1)}, u32[]{:S(2)}, u32[]{:S(2)}) %collective-permute-start.3) | collective-permute-done | bytes 65568 | tf_op jit(solution)/shard_map/ppermute | solution.py:338
  50.9 1.9 %all-to-all-done.1.s_ref = f32[16,8,128]{2,1,0:T(8,128)S(1)} async-done(((f32[16,8,128]{2,1,0:T(8,128)}), f32[16,8,128]{2,1,0:T(8,128)S(1)}, u32[]{:S(2)}, u32[]{:S(2)}) %all-to-all-start.1) | async-done | bytes 65568 | tf_op jit(solution)/shard_map/all_to_all | solution.py:377
  52.8 1.1 %shard_map.89 = (bf16[48,1024]{1,0:T(8,128)(2,1)}, bf16[32,1024]{1,0:T(8,128)(2,1)}, bf16[32,1024]{1,0:T(8,128)(2,1)}, bf16[256,640]{1,0:T(8,128)(2,1)}) custom-call(f32[16,8,128]{2,1,0:T(8,128)S(1)} %all-to-all-done.1.s_ref, bf16[64,1024]{1,0:T(8,128)(2,1)S(1)} %get-tuple-element.38.gf_ref, bf16[32,1024]{1,0:T(8,128)(2,1)S(1)} %collective-permute-done.3.r5_ref, ...), custom_call_target="tpu_custom_call" | custom-call | bytes 1048576 | tf_op jit(solution)/shard_map/pallas_call | solution.py:325
  53.9 4.4 %all-to-all-start.2 = ((bf16[32,8,640]{2,1,0:T(8,128)(2,1)}), bf16[32,8,640]{2,1,0:T(8,128)(2,1)S(1)}, u32[]{:S(2)}, u32[]{:S(2)}) async-start(bf16[32,8,640]{2,1,0:T(8,128)(2,1)} %bitcast.6), calls=%async_computation.2 | async-start | bytes 655360 | tf_op jit(solution)/shard_map/all_to_all | solution.py:343
  58.3 3.1 %collective-permute-start.4 = (bf16[48,1024]{1,0:T(8,128)(2,1)}, bf16[48,1024]{1,0:T(8,128)(2,1)S(1)}, u32[]{:S(2)}, u32[]{:S(2)}) collective-permute-start(bf16[48,1024]{1,0:T(8,128)(2,1)} %get-tuple-element.43), channel_id=1, source_target_pairs={{0,1},{1,0},{2,3},{3,2},{4,5},{5,4},{6,7},{7,6},{8,9},{9,8},{10,11... | collective-permute-start | bytes 294920 | tf_op jit(solution)/shard_map/ppermute | solution.py:338
  61.5 4.3 %collective-permute-start.5 = (bf16[32,1024]{1,0:T(8,128)(2,1)}, bf16[32,1024]{1,0:T(8,128)(2,1)S(1)}, u32[]{:S(2)}, u32[]{:S(2)}) collective-permute-start(bf16[32,1024]{1,0:T(8,128)(2,1)} %get-tuple-element.44), channel_id=1, source_target_pairs={{0,2},{1,3},{2,0},{3,1},{4,6},{5,7},{6,4},{7,5},{8,10},{9,11},{10,... | collective-permute-start | bytes 196616 | tf_op jit(solution)/shard_map/ppermute | solution.py:338
  65.8 2.1 %collective-permute-start.6 = (bf16[32,1024]{1,0:T(8,128)(2,1)}, bf16[32,1024]{1,0:T(8,128)(2,1)S(1)}, u32[]{:S(2)}, u32[]{:S(2)}) collective-permute-start(bf16[32,1024]{1,0:T(8,128)(2,1)} %get-tuple-element.45), channel_id=1, source_target_pairs={{0,3},{1,2},{2,1},{3,0},{4,7},{5,6},{6,5},{7,4},{8,11},{9,10},{10,... | collective-permute-start | bytes 196616 | tf_op jit(solution)/shard_map/ppermute | solution.py:338
  67.9 2.3 %shard_map.87 = (bf16[128,1024]{1,0:T(8,128)(2,1)}, f32[128,1024]{1,0:T(8,128)S(1)}, f32[128,1024]{1,0:T(8,128)S(1)}) custom-call(bf16[496,1024]{1,0:T(8,128)(2,1)S(1)} %get-tuple-element.28.loc_ref, bf16[448,1024]{1,0:T(8,128)(2,1)S(1)} %get-tuple-element.33.w_ref), custom_call_target="tpu_custom_call" | custom-call | bytes 268435456 | tf_op jit(solution)/shard_map/pallas_call | solution.py:325
  70.3 0.3 collective-permute-done.5.a_ref
  70.6 1.9 %collective-permute-done.6.b_ref = bf16[32,1024]{1,0:T(8,128)(2,1)S(1)} collective-permute-done((bf16[32,1024]{1,0:T(8,128)(2,1)}, bf16[32,1024]{1,0:T(8,128)(2,1)S(1)}, u32[]{:S(2)}, u32[]{:S(2)}) %collective-permute-start.6) | collective-permute-done | bytes 65568 | tf_op jit(solution)/shard_map/ppermute | solution.py:338
  72.5 0.6 copy-done.5
  73.2 0.8 %copy-done.6 = bf16[32,1024]{1,0:T(8,128)(2,1)S(1)} copy-done((bf16[32,1024]{1,0:T(8,128)(2,1)S(1)}, bf16[32,1024]{1,0:T(8,128)(2,1)}, u32[]{:S(2)}) %copy-start.6) | copy-done | bytes 65560
  74.0 1.5 %shard_map.90 = (bf16[128,1024]{1,0:T(8,128)(2,1)}, bf16[128,1024]{1,0:T(8,128)(2,1)}, f32[1,8]{1,0:T(1,128)}) custom-call(f32[128,1024]{1,0:T(8,128)S(1)} %get-tuple-element.35.gk_ref, f32[128,1024]{1,0:T(8,128)S(1)} %get-tuple-element.36.gv_ref, bf16[48,1024]{1,0:T(8,128)(2,1)S(1)} %collective-permute-done.4.pair_ref, ...), custom_call_target="tpu_custom_call" | custom-call | bytes 1048576 | tf_op jit(solution)/shard_map/pallas_call | solution.py:325
  (13 shorter events, 0.0 us)
Async XLA Ops:
  0.6 26.7 %copy-start.3 = (bf16[1,128,1024]{2,1,0:T(8,128)(2,1)S(1)}, bf16[1,128,1024]{2,1,0:T(8,128)(2,1)}, u32[]{:S(2)}) copy-start(bf16[1,128,1024]{2,1,0:T(8,128)(2,1)} %param.5) | copy-start | bytes 786436
  3.7 13.9 %copy-start.7 = (bf16[32,1024]{1,0:T(8,128)(2,1)S(1)}, bf16[32,1024]{1,0:T(8,128)(2,1)}, u32[]{:S(2)}) copy-start(bf16[32,1024]{1,0:T(8,128)(2,1)} %get-tuple-element.30) | copy-start | bytes 196612
  3.7 17.1 %copy-start.8 = (bf16[16,1024]{1,0:T(8,128)(2,1)S(1)}, bf16[16,1024]{1,0:T(8,128)(2,1)}, u32[]{:S(2)}) copy-start(bf16[16,1024]{1,0:T(8,128)(2,1)} %get-tuple-element.31) | copy-start | bytes 98308
  3.7 23.5 %copy-start = (bf16[1,128,1024]{2,1,0:T(8,128)(2,1)S(1)}, bf16[1,128,1024]{2,1,0:T(8,128)(2,1)}, u32[]{:S(2)}) copy-start(bf16[1,128,1024]{2,1,0:T(8,128)(2,1)} %param.6) | copy-start | bytes 786436
  3.8 23.5 %copy-start.1 = (bf16[1,128,1024]{2,1,0:T(8,128)(2,1)S(1)}, bf16[1,128,1024]{2,1,0:T(8,128)(2,1)}, u32[]{:S(2)}) copy-start(bf16[1,128,1024]{2,1,0:T(8,128)(2,1)} %param.7) | copy-start | bytes 786436
  3.8 23.5 %copy-start.2 = (bf16[208,1024]{1,0:T(8,128)(2,1)S(1)}, bf16[208,1024]{1,0:T(8,128)(2,1)}, u32[]{:S(2)}) copy-start(bf16[208,1024]{1,0:T(8,128)(2,1)} %get-tuple-element.27.low_ref) | copy-start | bytes 1277956
  3.8 30.1 %all-to-all-start = ((bf16[32,8,1024]{2,1,0:T(8,128)(2,1)}), bf16[32,8,1024]{2,1,0:T(8,128)(2,1)S(1)}, u32[]{:S(2)}, u32[]{:S(2)}) async-start(bf16[32,8,1024]{2,1,0:T(8,128)(2,1)} %get-tuple-element.32), calls=%async_computation | async-start | bytes 1048576 | tf_op jit(solution)/shard_map/all_to_all | solution.py:343
  17.7 13.6 %collective-permute-start = (bf16[32,1024]{1,0:T(8,128)(2,1)S(1)}, bf16[32,1024]{1,0:T(8,128)(2,1)S(1)}, u32[]{:S(2)}, u32[]{:S(2)}) collective-permute-start(bf16[32,1024]{1,0:T(8,128)(2,1)S(1)} %copy-done.7), channel_id=1, source_target_pairs={{0,1},{1,0},{2,3},{3,2},{4,5},{5,4},{6,7},{7,6},{8,9},{9,8},{10,11... | collective-permute-start | bytes 196616 | tf_op jit(solution)/shard_map/ppermute | solution.py:338
  20.8 8.2 %collective-permute-start.1 = (bf16[16,1024]{1,0:T(8,128)(2,1)S(1)}, bf16[16,1024]{1,0:T(8,128)(2,1)S(1)}, u32[]{:S(2)}, u32[]{:S(2)}) collective-permute-start(bf16[16,1024]{1,0:T(8,128)(2,1)S(1)} %copy-done.8), channel_id=1, source_target_pairs={{0,2},{1,3},{2,0},{3,1},{4,6},{5,7},{6,4},{7,5},{8,10},{9,11},{10,... | collective-permute-start | bytes 98312 | tf_op jit(solution)/shard_map/ppermute | solution.py:338
  25.1 6.2 %collective-permute-start.2 = (bf16[16,1024]{1,0:T(8,128)(2,1)S(1)}, bf16[16,1024]{1,0:T(8,128)(2,1)S(1)}, u32[]{:S(2)}, u32[]{:S(2)}) collective-permute-start(bf16[16,1024]{1,0:T(8,128)(2,1)S(1)} %copy-done.8), channel_id=1, source_target_pairs={{0,3},{1,2},{2,1},{3,0},{4,7},{5,6},{6,5},{7,4},{8,11},{9,10},{10,... | collective-permute-start | bytes 98312 | tf_op jit(solution)/shard_map/ppermute | solution.py:338
  27.3 1.0 %copy-start.4 = (bf16[1,128,1024]{2,1,0:T(8,128)(2,1)S(1)}, bf16[1,128,1024]{2,1,0:T(8,128)(2,1)}, u32[]{:S(2)}) copy-start(bf16[1,128,1024]{2,1,0:T(8,128)(2,1)} %param.8) | copy-start | bytes 786436
  35.5 17.3 %all-to-all-start.1 = ((f32[16,8,128]{2,1,0:T(8,128)}), f32[16,8,128]{2,1,0:T(8,128)S(1)}, u32[]{:S(2)}, u32[]{:S(2)}) async-start(f32[16,8,128]{2,1,0:T(8,128)} %get-tuple-element.37), calls=%async_computation.1 | async-start | bytes 131072 | tf_op jit(solution)/shard_map/all_to_all | solution.py:377
  45.4 5.6 %collective-permute-start.3 = (bf16[32,1024]{1,0:T(8,128)(2,1)S(1)}, bf16[32,1024]{1,0:T(8,128)(2,1)S(1)}, u32[]{:S(2)}, u32[]{:S(2)}) collective-permute-start(bf16[32,1024]{1,0:T(8,128)(2,1)S(1)} %get-tuple-element.39), channel_id=1, source_target_pairs={{0,4},{1,5},{2,6},{3,7},{4,0},{5,1},{6,2},{7,3},{8,12},{9,13},{10,... | collective-permute-start | bytes 196616 | tf_op jit(solution)/shard_map/ppermute | solution.py:338
  53.9 19.2 %all-to-all-start.2 = ((bf16[32,8,640]{2,1,0:T(8,128)(2,1)}), bf16[32,8,640]{2,1,0:T(8,128)(2,1)S(1)}, u32[]{:S(2)}, u32[]{:S(2)}) async-start(bf16[32,8,640]{2,1,0:T(8,128)(2,1)} %bitcast.6), calls=%async_computation.2 | async-start | bytes 655360 | tf_op jit(solution)/shard_map/all_to_all | solution.py:343
  58.3 14.8 %collective-permute-start.4 = (bf16[48,1024]{1,0:T(8,128)(2,1)}, bf16[48,1024]{1,0:T(8,128)(2,1)S(1)}, u32[]{:S(2)}, u32[]{:S(2)}) collective-permute-start(bf16[48,1024]{1,0:T(8,128)(2,1)} %get-tuple-element.43), channel_id=1, source_target_pairs={{0,1},{1,0},{2,3},{3,2},{4,5},{5,4},{6,7},{7,6},{8,9},{9,8},{10,11... | collective-permute-start | bytes 294920 | tf_op jit(solution)/shard_map/ppermute | solution.py:338
  61.5 9.1 %collective-permute-start.5 = (bf16[32,1024]{1,0:T(8,128)(2,1)}, bf16[32,1024]{1,0:T(8,128)(2,1)S(1)}, u32[]{:S(2)}, u32[]{:S(2)}) collective-permute-start(bf16[32,1024]{1,0:T(8,128)(2,1)} %get-tuple-element.44), channel_id=1, source_target_pairs={{0,2},{1,3},{2,0},{3,1},{4,6},{5,7},{6,4},{7,5},{8,10},{9,11},{10,... | collective-permute-start | bytes 196616 | tf_op jit(solution)/shard_map/ppermute | solution.py:338
  65.8 6.7 %collective-permute-start.6 = (bf16[32,1024]{1,0:T(8,128)(2,1)}, bf16[32,1024]{1,0:T(8,128)(2,1)S(1)}, u32[]{:S(2)}, u32[]{:S(2)}) collective-permute-start(bf16[32,1024]{1,0:T(8,128)(2,1)} %get-tuple-element.45), channel_id=1, source_target_pairs={{0,3},{1,2},{2,1},{3,0},{4,7},{5,6},{6,5},{7,4},{8,11},{9,10},{10,... | collective-permute-start | bytes 196616 | tf_op jit(solution)/shard_map/ppermute | solution.py:338
  72.5 0.6 copy-start.5
  73.1 0.8 %copy-start.6 = (bf16[32,1024]{1,0:T(8,128)(2,1)S(1)}, bf16[32,1024]{1,0:T(8,128)(2,1)}, u32[]{:S(2)}) copy-start(bf16[32,1024]{1,0:T(8,128)(2,1)} %copy-done.5) | copy-start | bytes 196612
